TPU v7x, 768 devices: a whole 4x8x12 slice. The times are simulated.
768 devices in a mesh: row: 48 (over z, x), col: 16 (over y, core).
Axes of the slice: x: 4, y: 8, z: 12, core: 2. Of those that a mesh axis runs over, the one named last changes fastest.
Arguments:
- object_field: float32 [4, 2, 6144, 2048], P(None, None, 'row', 'col'), may hold values from -5 to 5
- probe_wave: float32 [2, 128, 128], replicated, may hold values from -6 to 6
- positions: int32 [48, 16, 2, 2], P('row', 'col'), may hold values from 0 to 6143, as said below
- counts: int32 [48, 16], P('row', 'col'), may hold values from 0 to 2, as said below
- measured: float32 [48, 16, 2, 128, 128], P('row', 'col'), may hold values from 0 to 2
Outputs:
- object_grad: float32 [4, 2, 6144, 2048], P(None, None, 'row', 'col')
- probe_grad: float32 [2, 128, 128], replicated
Inputs may be any that keep to these rules, and one draw needn't show every extreme that they name: positions[r, c, s] lies inside tile (r, c): its row in r * 128 to (r + 1) * 128 - 1 and its column in c * 128 to (c + 1) * 128 - 1; dead slots hold such positions too. `counts`: some tile has 2 live slots.
All inputs are finite; a program needn't handle non-finite values.
Results may differ from a plain program's by a relative error of at most 0.0003.
Values sent between devices are 32-bit elements; how exact they have to be, the bound alone decides.
No kernel may reach another device: no remote copies, remote signals or barrier semaphores. Data moves between devices by JAX's collectives and lax.ppermute only.
A program may use at most 32 MiB of HBM per device.

v0:
```python
import math

import jax
import jax.numpy as jnp
from jax import lax
from jax.sharding import PartitionSpec as P

FRESNEL = 0.01


def with_halo(array, sides, width):
    for axis, dim in sides:
        peers, length = (lax.axis_size(axis), array.shape[dim])
        up = [(i, (i + 1) % peers) for i in range(peers - 1)]
        down = [(j, i) for i, j in up]
        last = lax.slice_in_dim(array, length - width, length, axis=dim)
        initial = lax.slice_in_dim(array, 0, width, axis=dim)
        before = lax.ppermute(last, axis, up)
        after = lax.ppermute(initial, axis, down)
        array = jnp.concatenate([before, array, after], axis=dim)
    return array


def matmul_exact(left, right):
    return jnp.dot(left, right, precision=lax.Precision.HIGHEST, preferred_element_type=jnp.float32)


def complex_matmul(left_real, left_imag, right_real, right_imag):
    real_out = matmul_exact(left_real, right_real) - matmul_exact(left_imag, right_imag)
    imag_out = matmul_exact(left_real, right_imag) + matmul_exact(left_imag, right_real)
    return (real_out, imag_out)


def transform(real_part, imag_part, table_real, table_imag):
    first_real, first_imag = complex_matmul(table_real, table_imag, real_part, imag_part)
    return complex_matmul(first_real, first_imag, table_real, table_imag)


def make_tables(points):
    indices = jnp.arange(points, dtype=jnp.int32)
    product = indices[:, None] * indices[None, :] % points
    phase_angle = 2.0 * math.pi / points * product.astype(jnp.float32)
    norm_scale = 1.0 / math.sqrt(points)
    table_real = jnp.cos(phase_angle) * norm_scale
    table_imag = -jnp.sin(phase_angle) * norm_scale
    frequency = jnp.where(indices < points // 2, indices, indices - points).astype(jnp.float32)
    prop_phase = -FRESNEL * (frequency[:, None] ** 2 + frequency[None, :] ** 2)
    return (table_real, table_imag, jnp.cos(prop_phase), jnp.sin(prop_phase))


def position_loss(patch_stack, probe_wave, measured_one, tables):
    table_real, table_imag, prop_real, prop_imag = tables
    wave_real = probe_wave[0]
    wave_imag = probe_wave[1]
    slice_count = patch_stack.shape[0]
    for depth_index in range(slice_count):
        trans_real = patch_stack[depth_index, 0]
        trans_imag = patch_stack[depth_index, 1]
        exit_real = wave_real * trans_real - wave_imag * trans_imag
        exit_imag = wave_real * trans_imag + wave_imag * trans_real
        far_real, far_imag = transform(exit_real, exit_imag, table_real, table_imag)
        if depth_index + 1 < slice_count:
            moved_real = far_real * prop_real - far_imag * prop_imag
            moved_imag = far_real * prop_imag + far_imag * prop_real
            wave_real, wave_imag = transform(moved_real, moved_imag, table_real, -table_imag)
    amplitude = jnp.sqrt(far_real * far_real + far_imag * far_imag + 1.0)
    return jnp.sum((amplitude - measured_one) ** 2)


def per_device(object_field, probe_wave, positions, counts, measured):
    slice_count = object_field.shape[0]
    probe_size = probe_wave.shape[-1]
    half_probe = probe_size // 2
    tile_rows = object_field.shape[2]
    tile_cols = object_field.shape[3]
    tables = make_tables(probe_size)
    padded = with_halo(object_field, (("row", 2), ("col", 3)), half_probe)
    corner = jnp.stack([lax.axis_index("row") * tile_rows, lax.axis_index("col") * tile_cols])
    local_starts = positions[0, 0] - corner[None, :]
    my_count = counts[0, 0]
    patterns = measured[0, 0]
    gradient = jax.grad(position_loss, argnums=(0, 1))
    anchor = jnp.zeros((), jnp.int32)

    def visit(slot_index, state_pair):
        object_sum, probe_sum = state_pair
        centre = lax.dynamic_index_in_dim(local_starts, slot_index, 0, keepdims=False)
        pattern = lax.dynamic_index_in_dim(patterns, slot_index, 0, keepdims=False)
        starts = (anchor, anchor, centre[0], centre[1])
        patch_stack = lax.dynamic_slice(padded, starts, (slice_count, 2, probe_size, probe_size))
        patch_grad, wave_grad = gradient(patch_stack, probe_wave, pattern, tables)
        weight = (slot_index < my_count).astype(jnp.float32)
        current = lax.dynamic_slice(object_sum, starts, (slice_count, 2, probe_size, probe_size))
        object_sum = lax.dynamic_update_slice(object_sum, current + weight * patch_grad, starts)
        return (object_sum, probe_sum + weight * wave_grad)

    initial = (jnp.zeros(padded.shape, jnp.float32), jnp.zeros(probe_wave.shape, jnp.float32))
    object_sum, probe_sum = lax.fori_loop(0, local_starts.shape[0], visit, initial)
    stacked = jnp.concatenate(
        [object_sum[:, :, :half_probe], object_sum[:, :, -half_probe:]], axis=2
    )
    arrived = with_halo(stacked, (("row", 2),), half_probe)
    middle = object_sum[:, :, half_probe : half_probe + tile_rows]
    middle = middle.at[:, :, :half_probe].add(arrived[:, :, :half_probe])
    middle = middle.at[:, :, tile_rows - half_probe :].add(arrived[:, :, 3 * half_probe :])
    beside = jnp.concatenate([middle[:, :, :, :half_probe], middle[:, :, :, -half_probe:]], axis=3)
    received = with_halo(beside, (("col", 3),), half_probe)
    result = middle[:, :, :, half_probe : half_probe + tile_cols]
    result = result.at[:, :, :, :half_probe].add(received[:, :, :, :half_probe])
    result = result.at[:, :, :, tile_cols - half_probe :].add(received[:, :, :, 3 * half_probe :])
    probe_grad_all = lax.psum(probe_sum, ("row", "col"))
    return (result, probe_grad_all)


def solution(mesh):
    in_specs = (
        P(None, None, "row", "col"),
        P(),
        P("row", "col", None, None),
        P("row", "col"),
        P("row", "col", None, None, None),
    )
    out_specs = (P(None, None, "row", "col"), P())
    return jax.shard_map(
        per_device, mesh=mesh, in_specs=in_specs, out_specs=out_specs, check_vma=False
    )
```

profile of v0, /device:TPU:1, one launch (start us, length us, event | category | flops | bytes accessed | tf_op | source)
XLA Modules:
  0.0 706.2 jit_solution(14282259591668715477)
XLA Ops:
  7.2 1.2 copy.63
  8.7 4.0 collective-permute-start
  12.7 1.3 collective-permute-start.1
  14.0 4.8 collective-permute-done
  18.7 3.9 collective-permute-done.1
  23.1 1.1 fusion.777
  24.1 9.4 %collective-permute-start.2 = (f32[4,2,256,64]{2,3,1,0:T(8,128)}, f32[4,2,256,64]{2,3,1,0:T(8,128)S(1)}, u32[]{:S(2)}, u32[]{:S(2)}) collective-permute-start(f32[4,2,256,64]{2,3,1,0:T(8,128)} %get-tuple-element.1039), channel_id=1, source_target_pairs={{0,1},{1,2},{2,3},{3,4},{4,5},{5,6},{6,7},{7,8},{8,9},{9,10},{10,1... | collective-permute-start | bytes 1572872 | tf_op jit(solution)/shard_map/ppermute | solution.py:18
  33.5 2.8 collective-permute-start.3
  36.5 3.4 collective-permute-done.2
  39.9 4.3 collective-permute-done.3
  44.2 1.8 pad_maximum_fusion
  47.0 160.9 %while.24 = (s32[]{:T(128)}, f32[4,2,256,256]{3,2,1,0:T(8,128)S(1)}, f32[2,128,128]{2,1,0:T(8,128)S(1)}, s32[2,2]{1,0:T(2,128)S(1)}, s32[]{:T(128)}, /*index=5*/...) while((s32[]{:T(128)}, ...), condition=%wide.region_1.2_spmd.clone.clone.clone.clone, body=%wide.region_0.1_spmd.clone.clone.clone.clone.sunk | while | flops 2853437440 | bytes 28979552 | solution.py:98
  51.9 1.5 constant_dynamic-slice_fusion.9
  59.1 0.8 convolution_add_fusion.71
  59.9 0.8 fusion.1200
  60.7 0.8 convolution_subtract_fusion.27
  68.1 1.0 convolution_add_fusion.75
  69.1 0.8 fusion.1209
  70.0 0.8 convolution_subtract_fusion.30
  77.4 0.8 convolution_add_fusion.79
  79.0 0.8 convolution_subtract_fusion.33
  98.4 0.9 fusion.1242
  114.2 0.9 convolution_add_fusion.95
  119.1 7.1 dynamic_update_slice.13
  131.3 1.5 constant_dynamic-slice_fusion.9
  138.4 0.8 convolution_add_fusion.71
  139.2 0.8 fusion.1200
  140.0 0.8 convolution_subtract_fusion.27
  147.5 1.2 convolution_add_fusion.75
  148.7 0.8 fusion.1209
  149.5 0.8 convolution_subtract_fusion.30
  156.9 0.8 convolution_add_fusion.79
  158.6 0.8 convolution_subtract_fusion.33
  193.5 1.2 convolution_add_fusion.95
  198.6 6.4 dynamic_update_slice.13
  208.1 3.2 collective-permute-start.4
  211.3 1.3 collective-permute-start.5
  212.7 4.7 collective-permute-done.4
  217.4 4.0 collective-permute-done.5
  221.6 0.9 fusion.776
  222.6 7.7 %collective-permute-start.6 = (f32[4,2,128,64]{3,2,1,0:T(8,128)S(1)}, f32[4,2,128,64]{3,2,1,0:T(8,128)S(1)}, u32[]{:S(2)}, u32[]{:S(2)}) collective-permute-start(f32[4,2,128,64]{3,2,1,0:T(8,128)S(1)} %get-tuple-element.1038), channel_id=1, source_target_pairs={{0,1},{1,2},{2,3},{3,4},{4,5},{5,6},{6,7},{7,8},{8,9},{9,10},{10,1... | collective-permute-start | bytes 786440 | tf_op jit(solution)/shard_map/ppermute | solution.py:18
  230.5 1.9 collective-permute-start.7
  232.5 4.0 collective-permute-done.6
  236.6 1.0 scatter-add.16
  237.7 3.6 collective-permute-done.7
  241.4 2.6 scatter-add.19
  244.0 453.6 %all-reduce.12.cloned.1.call-done = f32[2,128,128]{2,1,0:T(8,128)} async-done(((f32[2,128,128]{2,1,0:T(8,128)}), f32[2,128,128]{2,1,0:T(8,128)}) %all-reduce.12.cloned.1.call-update) | async-done | bytes 131088 | tf_op jit(solution)/shard_map/psum | solution.py:111
  697.6 1.6 copy.135
  (257 shorter events, 117.4 us)
Async XLA Ops:
  7.2 690.4 %all-reduce.12.cloned.1.call-start = ((), (), s32[]{:S(2)}) async-start(), calls=%async_computation | async-start | bytes 262144 | tf_op jit(solution)/shard_map/psum | solution.py:111
  8.7 10.1 %collective-permute-start = (f32[4,2,64,128]{2,3,1,0:T(8,128)S(1)}, f32[4,2,64,128]{2,3,1,0:T(8,128)S(1)}, u32[]{:S(2)}, u32[]{:S(2)}) collective-permute-start(f32[4,2,64,128]{2,3,1,0:T(8,128)S(1)} %get-tuple-element.1041), channel_id=1, source_target_pairs={{0,16},{16,32},{32,48},{48,64},{64,80},{80,96},{96,112},{112,128},... | collective-permute-start | bytes 786440 | tf_op jit(solution)/shard_map/ppermute | solution.py:18
  12.6 23.9 %copy-start.3 = (s32[1,1,2,2]{3,2,1,0:T(2,128)S(1)}, s32[1,1,2,2]{3,2,1,0:T(2,128)}, u32[]{:S(2)}) copy-start(s32[1,1,2,2]{3,2,1,0:T(2,128)} %param.17) | copy-start | bytes 52
  12.7 9.9 %collective-permute-start.1 = (f32[4,2,64,128]{2,3,1,0:T(8,128)S(1)}, f32[4,2,64,128]{2,3,1,0:T(8,128)S(1)}, u32[]{:S(2)}, u32[]{:S(2)}) collective-permute-start(f32[4,2,64,128]{2,3,1,0:T(8,128)S(1)} %get-tuple-element.1042), channel_id=1, source_target_pairs={{16,0},{32,16},{48,32},{64,48},{80,64},{96,80},{112,96},{128,112},... | collective-permute-start | bytes 786440 | tf_op jit(solution)/shard_map/ppermute | solution.py:19
  24.1 15.8 %collective-permute-start.2 = (f32[4,2,256,64]{2,3,1,0:T(8,128)}, f32[4,2,256,64]{2,3,1,0:T(8,128)S(1)}, u32[]{:S(2)}, u32[]{:S(2)}) collective-permute-start(f32[4,2,256,64]{2,3,1,0:T(8,128)} %get-tuple-element.1039), channel_id=1, source_target_pairs={{0,1},{1,2},{2,3},{3,4},{4,5},{5,6},{6,7},{7,8},{8,9},{9,10},{10,1... | collective-permute-start | bytes 1572872 | tf_op jit(solution)/shard_map/ppermute | solution.py:18
  33.5 10.7 %collective-permute-start.3 = (f32[4,2,256,64]{2,3,1,0:T(8,128)}, f32[4,2,256,64]{2,3,1,0:T(8,128)S(1)}, u32[]{:S(2)}, u32[]{:S(2)}) collective-permute-start(f32[4,2,256,64]{2,3,1,0:T(8,128)} %get-tuple-element.1040), channel_id=1, source_target_pairs={{1,0},{2,1},{3,2},{4,3},{5,4},{6,5},{7,6},{8,7},{9,8},{10,9},{11,1... | collective-permute-start | bytes 1572872 | tf_op jit(solution)/shard_map/ppermute | solution.py:19
  46.1 0.9 copy-start
  46.1 1.0 copy-start.4
  207.9 4.8 copy-start.1
  208.1 9.3 %collective-permute-start.4 = (f32[4,2,64,256]{3,2,1,0:T(8,128)S(1)}, f32[4,2,64,256]{3,2,1,0:T(8,128)S(1)}, u32[]{:S(2)}, u32[]{:S(2)}) collective-permute-start(f32[4,2,64,256]{3,2,1,0:T(8,128)S(1)} %get-tuple-element.1036), channel_id=1, source_target_pairs={{0,16},{16,32},{32,48},{48,64},{64,80},{80,96},{96,112},{112,128},... | collective-permute-start | bytes 1572872 | tf_op jit(solution)/shard_map/ppermute | solution.py:18
  211.3 10.2 %collective-permute-start.5 = (f32[4,2,64,256]{3,2,1,0:T(8,128)S(1)}, f32[4,2,64,256]{3,2,1,0:T(8,128)S(1)}, u32[]{:S(2)}, u32[]{:S(2)}) collective-permute-start(f32[4,2,64,256]{3,2,1,0:T(8,128)S(1)} %get-tuple-element.1035), channel_id=1, source_target_pairs={{16,0},{32,16},{48,32},{64,48},{80,64},{96,80},{112,96},{128,112},... | collective-permute-start | bytes 1572872 | tf_op jit(solution)/shard_map/ppermute | solution.py:19
  222.6 13.8 %collective-permute-start.6 = (f32[4,2,128,64]{3,2,1,0:T(8,128)S(1)}, f32[4,2,128,64]{3,2,1,0:T(8,128)S(1)}, u32[]{:S(2)}, u32[]{:S(2)}) collective-permute-start(f32[4,2,128,64]{3,2,1,0:T(8,128)S(1)} %get-tuple-element.1038), channel_id=1, source_target_pairs={{0,1},{1,2},{2,3},{3,4},{4,5},{5,6},{6,7},{7,8},{8,9},{9,10},{10,1... | collective-permute-start | bytes 786440 | tf_op jit(solution)/shard_map/ppermute | solution.py:18
  230.5 10.7 %collective-permute-start.7 = (f32[4,2,128,64]{3,2,1,0:T(8,128)}, f32[4,2,128,64]{3,2,1,0:T(8,128)S(1)}, u32[]{:S(2)}, u32[]{:S(2)}) collective-permute-start(f32[4,2,128,64]{3,2,1,0:T(8,128)} %get-tuple-element.1037), channel_id=1, source_target_pairs={{1,0},{2,1},{3,2},{4,3},{5,4},{6,5},{7,6},{8,7},{9,8},{10,9},{11,1... | collective-permute-start | bytes 786440 | tf_op jit(solution)/shard_map/ppermute | solution.py:19
  244.0 455.1 %copy-start.2 = (f32[4,2,128,128]{3,2,1,0:T(8,128)}, f32[4,2,128,128]{3,2,1,0:T(8,128)S(1)}, u32[]{:S(2)}) copy-start(f32[4,2,128,128]{3,2,1,0:T(8,128)S(1)} %scatter-add.19) | copy-start | bytes 1572868
Sparse Core Ops, SparseCore 0:
  230.5 467.1 all-reduce.11
where the time goes:
time: 710 us; the launch traced here: 706 us
  waiting for transfers between devices  486 us (68%)
  matrix products  128 us (18%)
  starting transfers between devices  31.7 us (4%)
  local copies, waits for them, and re-layouts  29.3 us (4%)
  between operations  14.5 us (2%)
  loops' own time  13 us (2%)
    psum x1, waiting for transfers between devices, per_device(): probe_grad_all = lax.psum(probe_sum, ('row', 'col'))  454 us
    dot_general x224, matrix products, matmul_exact(): jnp.dot(left, right, precision=lax.Precision.HIGHEST, preferred_element_t...  128 us
    ppermute x4, starting transfers between devices, with_halo(): before = lax.ppermute(last, axis, up)  24.3 us
    ppermute x4, waiting for transfers between devices, with_halo(): before = lax.ppermute(last, axis, up)  16.8 us
    ppermute x4, waiting for transfers between devices, with_halo(): after = lax.ppermute(initial, axis, down)  15.8 us
  transfers between devices with their start and end apart: 9, of which 9 were waited for; matrix products, arithmetic and copies ran while one was open for 1% of the time, Pallas kernels for 0%

commit v1 on v0

v1 whole, which is shorter than its diff:
```python
import jax
import jax.numpy as jnp
import ml_dtypes
import numpy as np
from jax import lax
from jax.experimental import pallas as pl
from jax.experimental.pallas import tpu as pltpu
from jax.sharding import Mesh, PartitionSpec as P

FRESNEL = 0.01
N = 128
H = N // 2
CHIPS_X = 4
CORES = 2
ROW = ("z", "x")
COL = ("y", "c")


def constant_operands():
    k = np.arange(N)
    dft = np.exp(-2j * np.pi / N * (np.outer(k, k) % N)) / np.sqrt(N)
    u = np.where(k < H, k, k - N).astype(np.float64)
    p = np.exp(-1j * FRESNEL * u * u)
    step = dft.conj() @ (p[:, None] * dft)
    out = []
    for a in (step, dft):
        right = np.block([[a.real, a.imag], [-a.imag, a.real]])
        for m in (right, right.T):
            high = m.astype(ml_dtypes.bfloat16)
            low = (m - high.astype(np.float64)).astype(ml_dtypes.bfloat16)
            out += [high, low]
    return np.stack(out)


def split(x):
    high = x.astype(jnp.bfloat16)
    return high, (x - high.astype(jnp.float32)).astype(jnp.bfloat16)


def dot(a, b):
    return jnp.dot(a, b, preferred_element_type=jnp.float32)


def two_sided(wave, right, left):
    x = jnp.concatenate([jnp.concatenate(w, axis=1) for w in wave], axis=0)
    xh, xl = split(x)
    rh, rl = right
    z = dot(jnp.concatenate([xh, xl, xh], axis=1), jnp.concatenate([rh, rh, rl], axis=0))
    z = jnp.concatenate(
        [
            jnp.concatenate([z[:N, :N], z[N:, :N]], axis=1),
            jnp.concatenate([z[:N, N:], z[N:, N:]], axis=1),
        ],
        axis=0,
    )
    zh, zl = split(z)
    lh, ll = left
    y = dot(jnp.concatenate([lh, ll, lh], axis=1), jnp.concatenate([zh, zh, zl], axis=0))
    return [(y[:N, :N], y[N:, :N]), (y[:N, N:], y[N:, N:])]


def lane_mask():
    return lax.broadcasted_iota(jnp.int32, (N, N), 1) < H


def pack_kernel(tile, above, below, to_left, to_right):
    low = lane_mask()
    for k in range(tile.shape[0]):
        for c in range(2):
            t = tile[k, c]
            v = jnp.concatenate([above[k, c], below[k, c]], axis=0)
            to_right[k, c] = jnp.where(low, pltpu.roll(t, H, 1), v)
            to_left[k, c] = jnp.where(low, t, pltpu.roll(v, H, 1))


def turned_rows(x):
    return jnp.concatenate([x[H:], x[:H]], axis=0)


def grad_kernel(
    pos, count, tile, above, below, from_left, from_right, probe, measured, consts,
    own_out, vert_out, left_out, right_out, probe_out, patches, waves,
):
    slices = tile.shape[0]
    low = lane_mask()
    rows = lax.broadcasted_iota(jnp.int32, (N, N), 0)
    cols = lax.broadcasted_iota(jnp.int32, (N, N), 1)
    pair = lambda i: (consts[2 * i], consts[2 * i + 1])
    step, step_t, dft, dft_t = (pair(i) for i in range(4))

    shifts, row_own, col_own = [], [], []
    for s in range(2):
        ry = jnp.bitwise_and(pos[s, 0], N - 1)
        rx = jnp.bitwise_and(pos[s, 1], N - 1)
        shifts.append((ry, rx))
        row_own.append((rows < H) == (rows < ry))
        col_own.append((cols < H) == (cols < rx))

    def candidates(k, c):
        own = pltpu.roll(turned_rows(tile[k, c]), H, 1)
        vert = pltpu.roll(jnp.concatenate([above[k, c], below[k, c]], axis=0), H, 1)
        fl, fr = from_left[k, c], from_right[k, c]
        horiz = turned_rows(jnp.where(low, fl, pltpu.roll(fr, H, 1)))
        corner = jnp.where(low, pltpu.roll(fl, H, 1), fr)
        return own, vert, horiz, corner

    wave = []
    for s in range(2):
        ry, rx = shifts[s]
        wave.append([pltpu.roll(pltpu.roll(probe[c], rx, 1), ry, 0) for c in range(2)])

    for k in range(slices):
        parts = [candidates(k, c) for c in range(2)]
        exit_wave = []
        for s in range(2):
            o = []
            for c in range(2):
                own, vert, horiz, corner = parts[c]
                picked = jnp.where(
                    row_own[s],
                    jnp.where(col_own[s], own, horiz),
                    jnp.where(col_own[s], vert, corner),
                )
                patches[k, s, c] = picked
                waves[k, s, c] = wave[s][c]
                o.append(picked)
            wr, wi = wave[s]
            exit_wave.append((wr * o[0] - wi * o[1], wr * o[1] + wi * o[0]))
        if k + 1 < slices:
            wave = two_sided(exit_wave, step, step_t)
        else:
            far = two_sided(exit_wave, dft, dft_t)

    grad = []
    for s in range(2):
        fr, fi = far[s]
        live = jnp.where(s < count[0, 0], 2.0, 0.0)
        scale = live * (1.0 - measured[s] * lax.rsqrt(fr * fr + fi * fi + 1.0))
        grad.append((scale * fr, scale * fi))
    for k in reversed(range(slices)):
        if k + 1 < slices:
            grad = two_sided(grad, step_t, step)
        else:
            grad = two_sided(grad, dft_t, dft)
        onto_object = [[], []]
        onto_wave = []
        for s in range(2):
            gr, gi = grad[s]
            wr, wi = waves[k, s, 0], waves[k, s, 1]
            pr, pi = patches[k, s, 0], patches[k, s, 1]
            onto_object[0].append(wr * gr + wi * gi)
            onto_object[1].append(wr * gi - wi * gr)
            onto_wave.append((pr * gr + pi * gi, pr * gi - pi * gr))
        grad = onto_wave
        for c in range(2):
            zero = jnp.zeros((N, N), jnp.float32)
            own, vert, horiz, corner = zero, zero, zero, zero
            for s in range(2):
                g = onto_object[c][s]
                inside = jnp.where(row_own[s], g, 0.0)
                outside = jnp.where(row_own[s], 0.0, g)
                own += jnp.where(col_own[s], inside, 0.0)
                horiz += jnp.where(col_own[s], 0.0, inside)
                vert += jnp.where(col_own[s], outside, 0.0)
                corner += jnp.where(col_own[s], 0.0, outside)
            own_out[k, c] = turned_rows(pltpu.roll(own, H, 1))
            vert_out[k, c] = pltpu.roll(vert, H, 1)
            horiz = turned_rows(horiz)
            left_out[k, c] = jnp.where(low, horiz, pltpu.roll(corner, H, 1))
            right_out[k, c] = jnp.where(low, pltpu.roll(horiz, H, 1), corner)

    for c in range(2):
        total = jnp.zeros((N, N), jnp.float32)
        for s in range(2):
            ry, rx = shifts[s]
            back_y = jnp.bitwise_and(N - ry, N - 1)
            back_x = jnp.bitwise_and(N - rx, N - 1)
            total += pltpu.roll(pltpu.roll(grad[s][c], back_x, 1), back_y, 0)
        probe_out[c] = total


def vertical_kernel(vert, from_left, from_right, up_out, down_out):
    low = lane_mask()
    for k in range(vert.shape[0]):
        for c in range(2):
            add = jnp.where(low, pltpu.roll(from_left[k, c], H, 1), from_right[k, c])
            v = vert[k, c] + add
            up_out[k, c] = v[:H]
            down_out[k, c] = v[H:]


def final_kernel(own, from_left, from_right, from_above, from_below, out):
    low = lane_mask()
    for k in range(own.shape[0]):
        for c in range(2):
            add = jnp.where(low, from_left[k, c], pltpu.roll(from_right[k, c], H, 1))
            v = jnp.concatenate([from_above[k, c], from_below[k, c]], axis=0)
            out[k, c] = own[k, c] + add + v


def call(kernel, outs, args, name, scalars=0, scratch=()):
    spec = pl.BlockSpec(memory_space=pltpu.VMEM)
    smem = pl.BlockSpec(memory_space=pltpu.SMEM)
    return pl.pallas_call(
        kernel,
        out_shape=[jax.ShapeDtypeStruct(s, jnp.float32) for s in outs],
        in_specs=[smem] * scalars + [spec] * (len(args) - scalars),
        out_specs=[spec] * len(outs),
        scratch_shapes=list(scratch),
        compiler_params=pltpu.CompilerParams(vmem_limit_bytes=40 * 1024 * 1024),
        name=name,
    )(*args)


def shift(x, axis, forward):
    size = lax.axis_size(axis)
    pairs = [(i, i + 1) if forward else (i + 1, i) for i in range(size - 1)]
    return lax.ppermute(x, axis, pairs)


def exchange(x, axis):
    return lax.all_to_all(x, axis, 0, 0, tiled=True)


def gathered_sum(x, axis):
    n = lax.axis_size(axis)
    rows = x.shape[0]
    parts = exchange(jnp.broadcast_to(x, (n, *x.shape)).reshape(n * rows, N), axis)
    return parts.reshape(n, rows, N).sum(axis=0)


def per_device(object_field, probe_wave, positions, counts, measured):
    slices = object_field.shape[0]
    full = (slices, 2, N, N)
    half = (slices, 2, H, N)
    consts = jnp.asarray(constant_operands())
    with jax.named_scope("object_halo"):
        above = shift(object_field[:, :, H:], ROW, True)
        below = shift(object_field[:, :, :H], ROW, False)
        to_left, to_right = call(
            pack_kernel, [full, full], (object_field, above, below), "pack_halo"
        )
        from_left = shift(to_right, COL, True)
        from_right = shift(to_left, COL, False)
    own, vert, left, right, probe_sum = call(
        grad_kernel,
        [full, full, full, full, (2, N, N)],
        (
            positions[0, 0], counts, object_field, above, below, from_left, from_right,
            probe_wave, measured[0, 0], consts,
        ),
        "slot_gradients",
        scalars=2,
        scratch=[pltpu.VMEM((slices, 2, 2, N, N), jnp.float32) for _ in range(2)],
    )
    with jax.named_scope("gradient_halo"):
        got_right = shift(left, COL, False)
        got_left = shift(right, COL, True)
        up, down = call(
            vertical_kernel, [half, half], (vert, got_left, got_right), "add_vertical"
        )
        got_below = shift(up, ROW, False)
        got_above = shift(down, ROW, True)
        (result,) = call(
            final_kernel, [full], (own, got_left, got_right, got_above, got_below), "add_own"
        )
    with jax.named_scope("probe_sum"):
        groups = lax.axis_size(("x", "c"))
        part = exchange(probe_sum.reshape(2 * N, N), ("x", "c"))
        part = part.reshape(groups, 2 * N // groups, N).sum(axis=0)
        part = gathered_sum(part, "y")
        part = gathered_sum(part, "z")
        spread = jnp.broadcast_to(part, (groups, *part.shape)).reshape(2 * N, N)
        probe_grad = exchange(spread, ("x", "c")).reshape(2, N, N)
    return (result, probe_grad)


def solution(mesh):
    rows, cols = mesh.devices.shape
    devices = mesh.devices.reshape(rows // CHIPS_X, CHIPS_X, cols // CORES, CORES)
    fine = Mesh(devices, ("z", "x", "y", "c"))
    in_specs = (
        P(None, None, ROW, COL),
        P(),
        P(ROW, COL, None, None),
        P(ROW, COL),
        P(ROW, COL, None, None, None),
    )
    out_specs = (P(None, None, ROW, COL), P())
    return jax.shard_map(
        per_device, mesh=fine, in_specs=in_specs, out_specs=out_specs, check_vma=False
    )
```

time: 710 us -> 107 us (0.15)
  waiting for transfers between devices: 486 us -> 18.2 us
  matrix products: 128 us -> 0 us
  starting transfers between devices: 31.7 us -> 62.8 us
  local copies, waits for them, and re-layouts: 29.3 us -> 4.56 us
  between operations: 14.5 us -> 1.45 us
  loops' own time: 13 us -> 0 us
  blocking collectives: 0 us -> 11.3 us
  Pallas kernels: 0 us -> 7.91 us
    psum x1 -> x0, waiting for transfers between devices: 454 us -> none  [per_device(): probe_grad_all = lax.psum(probe_sum, ('row', 'col'))]
    dot_general x224 -> x0, matrix products: 128 us -> none  [matmul_exact(): jnp.dot(left, right, precision=lax.Precision.HIGHEST, preferred_element_t...]
    all_to_all x0 -> x3, starting transfers between devices: none -> 32.4 us  [exchange(): return lax.all_to_all(x, axis, 0, 0, tiled=True)]
    ppermute x8, waiting for transfers between devices: 32.6 us -> 5.37 us  [shift(): return lax.ppermute(x, axis, pairs)]
    dynamic_update_slice x2 -> x0, local copies, waits for them, and re-layouts: 13.5 us -> none  [visit(): lax.dynamic_update_slice(object_sum, current + weight * patch_grad, starts)]
    another operation x1 -> x0, loops' own time: 13 us -> none  [per_device(): lax.fori_loop(0, local_starts.shape[0], visit, initial)]
    all_to_all x0 -> x3, waiting for transfers between devices: none -> 12.8 us  [exchange(): return lax.all_to_all(x, axis, 0, 0, tiled=True)]
    all_to_all x0 -> x1, blocking collectives: none -> 11.3 us  [exchange(): return lax.all_to_all(x, axis, 0, 0, tiled=True)]
  transfers between devices with their start and end apart: 9 -> 11, of which waited for: 9 -> 6; matrix products, arithmetic and copies ran while one was open for 1% -> 1% of each run, Pallas kernels for 0% -> 1%
where the time goes in v1:
time: 107 us; the launch traced here: 106 us
  starting transfers between devices  62.8 us (59%)
  waiting for transfers between devices  18.2 us (17%)
  blocking collectives  11.3 us (11%)
  Pallas kernels  7.91 us (7%)
  local copies, waits for them, and re-layouts  4.56 us (4%)
  between operations  1.45 us (1%)
    all_to_all x3, starting transfers between devices, exchange(): return lax.all_to_all(x, axis, 0, 0, tiled=True)  32.4 us
    ppermute x8, starting transfers between devices, shift(): return lax.ppermute(x, axis, pairs)  30.4 us
    all_to_all x3, waiting for transfers between devices, exchange(): return lax.all_to_all(x, axis, 0, 0, tiled=True)  12.8 us
    all_to_all x1, blocking collectives, exchange(): return lax.all_to_all(x, axis, 0, 0, tiled=True)  11.3 us
    pallas_call x4, Pallas kernels, call(): pl.pallas_call(kernel, out_shape=[jax.ShapeDtypeStruct(s, jnp.float32) fo...  7.91 us
    ppermute x8, waiting for transfers between devices, shift(): return lax.ppermute(x, axis, pairs)  5.37 us
  transfers between devices with their start and end apart: 11, of which 6 were waited for; matrix products, arithmetic and copies ran while one was open for 1% of the time, Pallas kernels for 1%

profile of v1, /device:TPU:1, one launch (start us, length us, event | category | flops | bytes accessed | tf_op | source)
XLA Modules:
  0.0 106.3 jit_solution(259146440458570541)
XLA Ops:
  0.6 0.0 copy-start
  0.6 0.0 copy-start.1
  0.7 1.2 %fusion = (f32[4,2,64,128]{3,2,1,0:T(8,128)S(1)}, f32[4,2,64,128]{3,2,1,0:T(8,128)S(1)}) fusion(f32[4,2,128,128]{3,2,1,0:T(8,128)} %tile.3), kind=kLoop, calls=%fused_computation | loop fusion | bytes 1048576 | tf_op jit(solution)/shard_map/object_halo/slice | solution.py:239
  1.9 1.3 %collective-permute-start.1 = (f32[4,2,64,128]{3,2,1,0:T(8,128)S(1)}, f32[4,2,64,128]{3,2,1,0:T(8,128)S(1)}, u32[]{:S(2)}, u32[]{:S(2)}) collective-permute-start(f32[4,2,64,128]{3,2,1,0:T(8,128)S(1)} %get-tuple-element.20), channel_id=1, source_target_pairs={{16,0},{32,16},{48,32},{64,48},{80,64},{96,80},{112,96},{128,112},... | collective-permute-start | bytes 786440 | tf_op jit(solution)/shard_map/object_halo/ppermute | solution.py:218
  3.2 0.0 copy-start.2
  3.2 0.0 copy-start.3
  3.2 4.7 %collective-permute-start = (f32[4,2,64,128]{3,2,1,0:T(8,128)S(1)}, f32[4,2,64,128]{3,2,1,0:T(8,128)S(1)}, u32[]{:S(2)}, u32[]{:S(2)}) collective-permute-start(f32[4,2,64,128]{3,2,1,0:T(8,128)S(1)} %get-tuple-element.21), channel_id=1, source_target_pairs={{0,16},{16,32},{32,48},{48,64},{64,80},{80,96},{96,112},{112,128},... | collective-permute-start | bytes 786440 | tf_op jit(solution)/shard_map/object_halo/ppermute | solution.py:218
  7.9 1.7 %collective-permute-done.1.below = f32[4,2,64,128]{3,2,1,0:T(8,128)S(1)} collective-permute-done((f32[4,2,64,128]{3,2,1,0:T(8,128)S(1)}, f32[4,2,64,128]{3,2,1,0:T(8,128)S(1)}, u32[]{:S(2)}, u32[]{:S(2)}) %collective-permute-start.1) | collective-permute-done | bytes 262176 | tf_op jit(solution)/shard_map/object_halo/ppermute | solution.py:218
  9.6 1.6 %collective-permute-done.above = f32[4,2,64,128]{3,2,1,0:T(8,128)S(1)} collective-permute-done((f32[4,2,64,128]{3,2,1,0:T(8,128)S(1)}, f32[4,2,64,128]{3,2,1,0:T(8,128)S(1)}, u32[]{:S(2)}, u32[]{:S(2)}) %collective-permute-start) | collective-permute-done | bytes 262176 | tf_op jit(solution)/shard_map/object_halo/ppermute | solution.py:218
  11.2 0.0 copy-done
  11.2 0.3 pack_halo.1
  11.5 6.5 %collective-permute-start.2 = (f32[4,2,128,128]{3,2,1,0:T(8,128)S(1)}, f32[4,2,128,128]{3,2,1,0:T(8,128)S(1)}, u32[]{:S(2)}, u32[]{:S(2)}) collective-permute-start(f32[4,2,128,128]{3,2,1,0:T(8,128)S(1)} %get-tuple-element.11), channel_id=1, source_target_pairs={{0,1},{1,2},{2,3},{3,4},{4,5},{5,6},{6,7},{7,8},{8,9},{9,10},{10,1... | collective-permute-start | bytes 1572872 | tf_op jit(solution)/shard_map/object_halo/ppermute | solution.py:218
  18.1 7.8 %collective-permute-start.3 = (f32[4,2,128,128]{3,2,1,0:T(8,128)S(1)}, f32[4,2,128,128]{3,2,1,0:T(8,128)S(1)}, u32[]{:S(2)}, u32[]{:S(2)}) collective-permute-start(f32[4,2,128,128]{3,2,1,0:T(8,128)S(1)} %get-tuple-element.12), channel_id=1, source_target_pairs={{1,0},{2,1},{3,2},{4,3},{5,4},{6,5},{7,6},{8,7},{9,8},{10,9},{11,1... | collective-permute-start | bytes 1572872 | tf_op jit(solution)/shard_map/object_halo/ppermute | solution.py:218
  26.5 0.0 collective-permute-done.2.from_left
  26.5 2.1 %collective-permute-done.3.from_right = f32[4,2,128,128]{3,2,1,0:T(8,128)S(1)} collective-permute-done((f32[4,2,128,128]{3,2,1,0:T(8,128)S(1)}, f32[4,2,128,128]{3,2,1,0:T(8,128)S(1)}, u32[]{:S(2)}, u32[]{:S(2)}) %collective-permute-start.3) | collective-permute-done | bytes 524320 | tf_op jit(solution)/shard_map/object_halo/ppermute | solution.py:218
  28.6 0.0 copy-start.4
  28.6 0.0 copy-done.1
  28.6 0.0 copy-done.2
  28.6 0.0 copy-done.3
  28.6 0.7 copy-done.4
  29.3 6.4 %slot_gradients.1 = (f32[4,2,128,128]{3,2,1,0:T(8,128)S(1)}, f32[4,2,128,128]{3,2,1,0:T(8,128)S(1)}, f32[4,2,128,128]{3,2,1,0:T(8,128)S(1)}, f32[4,2,128,128]{3,2,1,0:T(8,128)S(1)}, f32[2,128,128]{2,1,0:T(8,128)S(1)}) custom-call(s32[2,2]{1,0:T(2,128)S(1)} %bitcast.6, s32[1,1]{1,0:T(1,128)S(6)} %copy.9.count, f32[4,2,128,128]{3,2,1,0:T(8,128)S(1)} %copy-done, ...), custom_call_target="tpu_custom_call" | custom-call | tf_op jit(solution)/shard_map/slot_gradients/pallas_call | solution.py:204
  35.6 11.3 %all_to_all.27 = f32[8,32,128]{2,1,0:T(8,128)S(1)} all-to-all(f32[8,32,128]{2,1,0:T(8,128)S(1)} %bitcast.4), channel_id=1, replica_groups=mesh['z'=12,'x'=4,'y'=8,'c'=2] {'x','c'}, dimensions={0} | all-to-all | bytes 262144 | tf_op jit(solution)/shard_map/probe_sum/all_to_all | solution.py:222
  47.0 0.7 broadcast_in_dim.9
  47.7 7.0 %all-to-all-start.1 = ((f32[8,32,128]{2,1,0:T(8,128)}), f32[8,32,128]{2,1,0:T(8,128)S(1)}, u32[]{:S(2)}, u32[]{:S(2)}) async-start(f32[8,32,128]{2,1,0:T(8,128)} %broadcast_in_dim.9), calls=%async_computation.1 | async-start | bytes 262144 | tf_op jit(solution)/shard_map/probe_sum/all_to_all | solution.py:222
  54.7 4.7 %collective-permute-start.4 = (f32[4,2,128,128]{3,2,1,0:T(8,128)S(1)}, f32[4,2,128,128]{3,2,1,0:T(8,128)S(1)}, u32[]{:S(2)}, u32[]{:S(2)}) collective-permute-start(f32[4,2,128,128]{3,2,1,0:T(8,128)S(1)} %get-tuple-element.14), channel_id=1, source_target_pairs={{0,1},{1,2},{2,3},{3,4},{4,5},{5,6},{6,7},{7,8},{8,9},{9,10},{10,1... | collective-permute-start | bytes 1572872 | tf_op jit(solution)/shard_map/gradient_halo/ppermute | solution.py:218
  59.3 1.9 %collective-permute-start.5 = (f32[4,2,128,128]{3,2,1,0:T(8,128)S(1)}, f32[4,2,128,128]{3,2,1,0:T(8,128)S(1)}, u32[]{:S(2)}, u32[]{:S(2)}) collective-permute-start(f32[4,2,128,128]{3,2,1,0:T(8,128)S(1)} %get-tuple-element.15), channel_id=1, source_target_pairs={{1,0},{2,1},{3,2},{4,3},{5,4},{6,5},{7,6},{8,7},{9,8},{10,9},{11,1... | collective-permute-start | bytes 1572872 | tf_op jit(solution)/shard_map/gradient_halo/ppermute | solution.py:218
  61.3 1.2 %all-to-all-done.1 = f32[8,32,128]{2,1,0:T(8,128)S(1)} async-done(((f32[8,32,128]{2,1,0:T(8,128)}), f32[8,32,128]{2,1,0:T(8,128)S(1)}, u32[]{:S(2)}, u32[]{:S(2)}) %all-to-all-start.1) | async-done | bytes 131104 | tf_op jit(solution)/shard_map/probe_sum/all_to_all | solution.py:222
  62.5 0.7 broadcast_in_dim.10
  63.2 17.4 %all-to-all-start.2 = ((f32[12,32,128]{2,1,0:T(8,128)}), f32[12,32,128]{2,1,0:T(8,128)S(1)}, u32[]{:S(2)}, u32[]{:S(2)}) async-start(f32[12,32,128]{2,1,0:T(8,128)} %broadcast_in_dim.10), calls=%async_computation.2 | async-start | bytes 393216 | tf_op jit(solution)/shard_map/probe_sum/all_to_all | solution.py:222
  80.6 0.0 collective-permute-done.4.from_left
  80.7 0.0 collective-permute-done.5.from_right
  80.7 0.2 add_vertical.1
  80.9 2.2 %collective-permute-start.6 = (f32[4,2,64,128]{3,2,1,0:T(8,128)S(1)}, f32[4,2,64,128]{3,2,1,0:T(8,128)S(1)}, u32[]{:S(2)}, u32[]{:S(2)}) collective-permute-start(f32[4,2,64,128]{3,2,1,0:T(8,128)S(1)} %get-tuple-element.17), channel_id=1, source_target_pairs={{0,16},{16,32},{32,48},{48,64},{64,80},{80,96},{96,112},{112,128},... | collective-permute-start | bytes 786440 | tf_op jit(solution)/shard_map/gradient_halo/ppermute | solution.py:218
  83.1 1.3 %collective-permute-start.7 = (f32[4,2,64,128]{3,2,1,0:T(8,128)S(1)}, f32[4,2,64,128]{3,2,1,0:T(8,128)S(1)}, u32[]{:S(2)}, u32[]{:S(2)}) collective-permute-start(f32[4,2,64,128]{3,2,1,0:T(8,128)S(1)} %get-tuple-element.18), channel_id=1, source_target_pairs={{16,0},{32,16},{48,32},{64,48},{80,64},{96,80},{112,96},{128,112},... | collective-permute-start | bytes 786440 | tf_op jit(solution)/shard_map/gradient_halo/ppermute | solution.py:218
  84.4 7.3 %all-to-all-done.2 = f32[12,32,128]{2,1,0:T(8,128)S(1)} async-done(((f32[12,32,128]{2,1,0:T(8,128)}), f32[12,32,128]{2,1,0:T(8,128)S(1)}, u32[]{:S(2)}, u32[]{:S(2)}) %all-to-all-start.2) | async-done | bytes 196640 | tf_op jit(solution)/shard_map/probe_sum/all_to_all | solution.py:222
  91.7 0.7 broadcast_in_dim.11
  92.4 8.0 %all-to-all-start.3 = ((f32[8,32,128]{2,1,0:T(8,128)}), f32[8,32,128]{2,1,0:T(8,128)S(1)}, u32[]{:S(2)}, u32[]{:S(2)}) async-start(f32[8,32,128]{2,1,0:T(8,128)} %broadcast_in_dim.11), calls=%async_computation.3 | async-start | bytes 262144 | tf_op jit(solution)/shard_map/probe_sum/all_to_all | solution.py:222
  100.4 0.0 collective-permute-done.6.from_above
  100.4 0.0 collective-permute-done.7.from_below
  100.4 1.0 add_own.1
  101.4 4.3 %all-to-all-done.3 = f32[8,32,128]{2,1,0:T(8,128)S(1)} async-done(((f32[8,32,128]{2,1,0:T(8,128)}), f32[8,32,128]{2,1,0:T(8,128)S(1)}, u32[]{:S(2)}, u32[]{:S(2)}) %all-to-all-start.3) | async-done | bytes 131104 | tf_op jit(solution)/shard_map/probe_sum/all_to_all | solution.py:222
  105.6 0.7 copy.10
  (3 shorter events, 0.0 us)
Async XLA Ops:
  0.6 10.6 %copy-start = (f32[4,2,128,128]{3,2,1,0:T(8,128)S(1)}, f32[4,2,128,128]{3,2,1,0:T(8,128)}, u32[]{:S(2)}) copy-start(f32[4,2,128,128]{3,2,1,0:T(8,128)} %tile.3) | copy-start | bytes 1572868
  0.6 27.9 %copy-start.1 = (bf16[8,256,256]{2,1,0:T(8,128)(2,1)S(1)}, bf16[8,256,256]{2,1,0:T(8,128)(2,1)}, u32[]{:S(2)}) copy-start(bf16[8,256,256]{2,1,0:T(8,128)(2,1)} %constant.4.clone.consts) | copy-start | bytes 3145732
  1.9 7.7 %collective-permute-start.1 = (f32[4,2,64,128]{3,2,1,0:T(8,128)S(1)}, f32[4,2,64,128]{3,2,1,0:T(8,128)S(1)}, u32[]{:S(2)}, u32[]{:S(2)}) collective-permute-start(f32[4,2,64,128]{3,2,1,0:T(8,128)S(1)} %get-tuple-element.20), channel_id=1, source_target_pairs={{16,0},{32,16},{48,32},{64,48},{80,64},{96,80},{112,96},{128,112},... | collective-permute-start | bytes 786440 | tf_op jit(solution)/shard_map/object_halo/ppermute | solution.py:218
  3.2 25.4 %copy-start.2 = (f32[2,128,128]{2,1,0:T(8,128)S(1)}, f32[2,128,128]{2,1,0:T(8,128)}, u32[]{:S(2)}) copy-start(f32[2,128,128]{2,1,0:T(8,128)} %probe.1) | copy-start | bytes 393220
  3.2 25.4 %copy-start.3 = (f32[1,1,2,128,128]{4,3,2,1,0:T(8,128)S(1)}, f32[1,1,2,128,128]{4,3,2,1,0:T(8,128)}, u32[]{:S(2)}) copy-start(f32[1,1,2,128,128]{4,3,2,1,0:T(8,128)} %param.10) | copy-start | bytes 393220
  3.2 8.0 %collective-permute-start = (f32[4,2,64,128]{3,2,1,0:T(8,128)S(1)}, f32[4,2,64,128]{3,2,1,0:T(8,128)S(1)}, u32[]{:S(2)}, u32[]{:S(2)}) collective-permute-start(f32[4,2,64,128]{3,2,1,0:T(8,128)S(1)} %get-tuple-element.21), channel_id=1, source_target_pairs={{0,16},{16,32},{32,48},{48,64},{64,80},{80,96},{96,112},{112,128},... | collective-permute-start | bytes 786440 | tf_op jit(solution)/shard_map/object_halo/ppermute | solution.py:218
  11.5 15.0 %collective-permute-start.2 = (f32[4,2,128,128]{3,2,1,0:T(8,128)S(1)}, f32[4,2,128,128]{3,2,1,0:T(8,128)S(1)}, u32[]{:S(2)}, u32[]{:S(2)}) collective-permute-start(f32[4,2,128,128]{3,2,1,0:T(8,128)S(1)} %get-tuple-element.11), channel_id=1, source_target_pairs={{0,1},{1,2},{2,3},{3,4},{4,5},{5,6},{6,7},{7,8},{8,9},{9,10},{10,1... | collective-permute-start | bytes 1572872 | tf_op jit(solution)/shard_map/object_halo/ppermute | solution.py:218
  18.1 10.5 %collective-permute-start.3 = (f32[4,2,128,128]{3,2,1,0:T(8,128)S(1)}, f32[4,2,128,128]{3,2,1,0:T(8,128)S(1)}, u32[]{:S(2)}, u32[]{:S(2)}) collective-permute-start(f32[4,2,128,128]{3,2,1,0:T(8,128)S(1)} %get-tuple-element.12), channel_id=1, source_target_pairs={{1,0},{2,1},{3,2},{4,3},{5,4},{6,5},{7,6},{8,7},{9,8},{10,9},{11,1... | collective-permute-start | bytes 1572872 | tf_op jit(solution)/shard_map/object_halo/ppermute | solution.py:218
  28.6 0.7 copy-start.4
  47.7 14.9 %all-to-all-start.1 = ((f32[8,32,128]{2,1,0:T(8,128)}), f32[8,32,128]{2,1,0:T(8,128)S(1)}, u32[]{:S(2)}, u32[]{:S(2)}) async-start(f32[8,32,128]{2,1,0:T(8,128)} %broadcast_in_dim.9), calls=%async_computation.1 | async-start | bytes 262144 | tf_op jit(solution)/shard_map/probe_sum/all_to_all | solution.py:222
  54.7 26.0 %collective-permute-start.4 = (f32[4,2,128,128]{3,2,1,0:T(8,128)S(1)}, f32[4,2,128,128]{3,2,1,0:T(8,128)S(1)}, u32[]{:S(2)}, u32[]{:S(2)}) collective-permute-start(f32[4,2,128,128]{3,2,1,0:T(8,128)S(1)} %get-tuple-element.14), channel_id=1, source_target_pairs={{0,1},{1,2},{2,3},{3,4},{4,5},{5,6},{6,7},{7,8},{8,9},{9,10},{10,1... | collective-permute-start | bytes 1572872 | tf_op jit(solution)/shard_map/gradient_halo/ppermute | solution.py:218
  59.3 21.3 %collective-permute-start.5 = (f32[4,2,128,128]{3,2,1,0:T(8,128)S(1)}, f32[4,2,128,128]{3,2,1,0:T(8,128)S(1)}, u32[]{:S(2)}, u32[]{:S(2)}) collective-permute-start(f32[4,2,128,128]{3,2,1,0:T(8,128)S(1)} %get-tuple-element.15), channel_id=1, source_target_pairs={{1,0},{2,1},{3,2},{4,3},{5,4},{6,5},{7,6},{8,7},{9,8},{10,9},{11,1... | collective-permute-start | bytes 1572872 | tf_op jit(solution)/shard_map/gradient_halo/ppermute | solution.py:218
  63.2 28.5 %all-to-all-start.2 = ((f32[12,32,128]{2,1,0:T(8,128)}), f32[12,32,128]{2,1,0:T(8,128)S(1)}, u32[]{:S(2)}, u32[]{:S(2)}) async-start(f32[12,32,128]{2,1,0:T(8,128)} %broadcast_in_dim.10), calls=%async_computation.2 | async-start | bytes 393216 | tf_op jit(solution)/shard_map/probe_sum/all_to_all | solution.py:222
  80.9 19.5 %collective-permute-start.6 = (f32[4,2,64,128]{3,2,1,0:T(8,128)S(1)}, f32[4,2,64,128]{3,2,1,0:T(8,128)S(1)}, u32[]{:S(2)}, u32[]{:S(2)}) collective-permute-start(f32[4,2,64,128]{3,2,1,0:T(8,128)S(1)} %get-tuple-element.17), channel_id=1, source_target_pairs={{0,16},{16,32},{32,48},{48,64},{64,80},{80,96},{96,112},{112,128},... | collective-permute-start | bytes 786440 | tf_op jit(solution)/shard_map/gradient_halo/ppermute | solution.py:218
  83.1 17.3 %collective-permute-start.7 = (f32[4,2,64,128]{3,2,1,0:T(8,128)S(1)}, f32[4,2,64,128]{3,2,1,0:T(8,128)S(1)}, u32[]{:S(2)}, u32[]{:S(2)}) collective-permute-start(f32[4,2,64,128]{3,2,1,0:T(8,128)S(1)} %get-tuple-element.18), channel_id=1, source_target_pairs={{16,0},{32,16},{48,32},{64,48},{80,64},{96,80},{112,96},{128,112},... | collective-permute-start | bytes 786440 | tf_op jit(solution)/shard_map/gradient_halo/ppermute | solution.py:218
  92.4 13.2 %all-to-all-start.3 = ((f32[8,32,128]{2,1,0:T(8,128)}), f32[8,32,128]{2,1,0:T(8,128)S(1)}, u32[]{:S(2)}, u32[]{:S(2)}) async-start(f32[8,32,128]{2,1,0:T(8,128)} %broadcast_in_dim.11), calls=%async_computation.3 | async-start | bytes 262144 | tf_op jit(solution)/shard_map/probe_sum/all_to_all | solution.py:222

commit v2 on v1

--- a/solution.py
+++ b/solution.py
@@ -23,12 +23,9 @@
     p = np.exp(-1j * FRESNEL * u * u)
     step = dft.conj() @ (p[:, None] * dft)
     out = []
-    for a in (step, dft):
-        right = np.block([[a.real, a.imag], [-a.imag, a.real]])
-        for m in (right, right.T):
-            high = m.astype(ml_dtypes.bfloat16)
-            low = (m - high.astype(np.float64)).astype(ml_dtypes.bfloat16)
-            out += [high, low]
+    for m in (step.real, step.imag, dft.real, dft.imag):
+        high = m.astype(ml_dtypes.bfloat16)
+        out += [high, (m - high.astype(np.float64)).astype(ml_dtypes.bfloat16)]
     return np.stack(out)
 
 
@@ -63,14 +60,34 @@
     return lax.broadcasted_iota(jnp.int32, (N, N), 1) < H
 
 
-def pack_kernel(tile, above, below, to_left, to_right):
-    low = lane_mask()
+def pack_columns(x, to_left, to_right, k, c):
+    low = lax.broadcasted_iota(jnp.int32, (H, N), 1) < H
+    upper, lower = x[:H], x[H:]
+    to_right[k, c] = jnp.where(low, pltpu.roll(upper, H, 1), lower)
+    to_left[k, c] = jnp.where(low, upper, pltpu.roll(lower, H, 1))
+
+
+def unpack_columns(from_left, from_right):
+    low = lax.broadcasted_iota(jnp.int32, (H, N), 1) < H
+    upper = jnp.where(low, from_left, pltpu.roll(from_right, H, 1))
+    lower = jnp.where(low, pltpu.roll(from_left, H, 1), from_right)
+    return jnp.concatenate([upper, lower], axis=0)
+
+
+def edges_kernel(tile, to_up, to_down, to_left, to_right):
     for k in range(tile.shape[0]):
         for c in range(2):
             t = tile[k, c]
+            to_up[k, c] = t[:H]
+            to_down[k, c] = t[H:]
+            pack_columns(t, to_left, to_right, k, c)
+
+
+def corners_kernel(above, below, to_left, to_right):
+    for k in range(above.shape[0]):
+        for c in range(2):
             v = jnp.concatenate([above[k, c], below[k, c]], axis=0)
-            to_right[k, c] = jnp.where(low, pltpu.roll(t, H, 1), v)
-            to_left[k, c] = jnp.where(low, t, pltpu.roll(v, H, 1))
+            pack_columns(v, to_left, to_right, k, c)
 
 
 def turned_rows(x):
@@ -78,20 +95,30 @@
 
 
 def grad_kernel(
-    pos, count, tile, above, below, from_left, from_right, probe, measured, consts,
-    own_out, vert_out, left_out, right_out, probe_out, patches, waves,
+    pos, count, tile, above, below, from_left, from_right, corner_left, corner_right,
+    probe, measured, consts,
+    own_out, vert_out, horiz_out, corner_out, probe_out, patches, waves,
 ):
     slices = tile.shape[0]
     low = lane_mask()
     rows = lax.broadcasted_iota(jnp.int32, (N, N), 0)
     cols = lax.broadcasted_iota(jnp.int32, (N, N), 1)
-    pair = lambda i: (consts[2 * i], consts[2 * i + 1])
-    step, step_t, dft, dft_t = (pair(i) for i in range(4))
+    def operator(i):
+        right, left = [], []
+        for term in range(2):
+            real, imag = consts[4 * i + term], consts[4 * i + 2 + term]
+            row = jnp.concatenate([real, imag], axis=1)
+            col = jnp.concatenate([real, -imag], axis=1)
+            right.append(jnp.concatenate([row, jnp.concatenate([-imag, real], axis=1)], axis=0))
+            left.append(jnp.concatenate([col, jnp.concatenate([imag, real], axis=1)], axis=0))
+        return right, left
+
+    (step, step_t), (dft, dft_t) = operator(0), operator(1)
 
     shifts, row_own, col_own = [], [], []
     for s in range(2):
-        ry = jnp.bitwise_and(pos[s, 0], N - 1)
-        rx = jnp.bitwise_and(pos[s, 1], N - 1)
+        ry = jnp.bitwise_and(pos[0, 0, s, 0], N - 1)
+        rx = jnp.bitwise_and(pos[0, 0, s, 1], N - 1)
         shifts.append((ry, rx))
         row_own.append((rows < H) == (rows < ry))
         col_own.append((cols < H) == (cols < rx))
@@ -99,9 +126,8 @@
     def candidates(k, c):
         own = pltpu.roll(turned_rows(tile[k, c]), H, 1)
         vert = pltpu.roll(jnp.concatenate([above[k, c], below[k, c]], axis=0), H, 1)
-        fl, fr = from_left[k, c], from_right[k, c]
-        horiz = turned_rows(jnp.where(low, fl, pltpu.roll(fr, H, 1)))
-        corner = jnp.where(low, pltpu.roll(fl, H, 1), fr)
+        horiz = turned_rows(unpack_columns(from_left[k, c], from_right[k, c]))
+        corner = unpack_columns(corner_left[k, c], corner_right[k, c])
         return own, vert, horiz, corner
 
     wave = []
@@ -163,11 +189,10 @@
                 horiz += jnp.where(col_own[s], 0.0, inside)
                 vert += jnp.where(col_own[s], outside, 0.0)
                 corner += jnp.where(col_own[s], 0.0, outside)
-            own_out[k, c] = turned_rows(pltpu.roll(own, H, 1))
-            vert_out[k, c] = pltpu.roll(vert, H, 1)
-            horiz = turned_rows(horiz)
-            left_out[k, c] = jnp.where(low, horiz, pltpu.roll(corner, H, 1))
-            right_out[k, c] = jnp.where(low, pltpu.roll(horiz, H, 1), corner)
+            own_out[k, c] = own
+            vert_out[k, c] = vert
+            horiz_out[k, c] = horiz
+            corner_out[k, c] = corner
 
     for c in range(2):
         total = jnp.zeros((N, N), jnp.float32)
@@ -179,12 +204,21 @@
         probe_out[c] = total
 
 
+def sides_kernel(horiz_in, corner_in, left_out, right_out):
+    low = lane_mask()
+    for k in range(horiz_in.shape[0]):
+        for c in range(2):
+            horiz, corner = turned_rows(horiz_in[k, c]), corner_in[k, c]
+            left_out[k, c] = jnp.where(low, horiz, pltpu.roll(corner, H, 1))
+            right_out[k, c] = jnp.where(low, pltpu.roll(horiz, H, 1), corner)
+
+
 def vertical_kernel(vert, from_left, from_right, up_out, down_out):
     low = lane_mask()
     for k in range(vert.shape[0]):
         for c in range(2):
             add = jnp.where(low, pltpu.roll(from_left[k, c], H, 1), from_right[k, c])
-            v = vert[k, c] + add
+            v = pltpu.roll(vert[k, c], H, 1) + add
             up_out[k, c] = v[:H]
             down_out[k, c] = v[H:]
 
@@ -195,10 +229,10 @@
         for c in range(2):
             add = jnp.where(low, from_left[k, c], pltpu.roll(from_right[k, c], H, 1))
             v = jnp.concatenate([from_above[k, c], from_below[k, c]], axis=0)
-            out[k, c] = own[k, c] + add + v
-
-
-def call(kernel, outs, args, name, scalars=0, scratch=()):
+            out[k, c] = turned_rows(pltpu.roll(own[k, c], H, 1)) + add + v
+
+
+def call(kernel, outs, args, name, scalars=0, scratch=(), vmem=4, flops=0):
     spec = pl.BlockSpec(memory_space=pltpu.VMEM)
     smem = pl.BlockSpec(memory_space=pltpu.SMEM)
     return pl.pallas_call(
@@ -207,7 +241,12 @@
         in_specs=[smem] * scalars + [spec] * (len(args) - scalars),
         out_specs=[spec] * len(outs),
         scratch_shapes=list(scratch),
-        compiler_params=pltpu.CompilerParams(vmem_limit_bytes=40 * 1024 * 1024),
+        compiler_params=pltpu.CompilerParams(vmem_limit_bytes=vmem * 1024 * 1024),
+        cost_estimate=pl.CostEstimate(
+            flops=flops,
+            bytes_accessed=sum(4 * int(np.prod(s)) for s in outs) + sum(x.nbytes for x in args),
+            transcendentals=0,
+        ),
         name=name,
     )(*args)
 
@@ -235,25 +274,31 @@
     half = (slices, 2, H, N)
     consts = jnp.asarray(constant_operands())
     with jax.named_scope("object_halo"):
-        above = shift(object_field[:, :, H:], ROW, True)
-        below = shift(object_field[:, :, :H], ROW, False)
-        to_left, to_right = call(
-            pack_kernel, [full, full], (object_field, above, below), "pack_halo"
+        to_up, to_down, to_left, to_right = call(
+            edges_kernel, [half] * 4, (object_field,), "pack_edges"
         )
+        above = shift(to_down, ROW, True)
+        below = shift(to_up, ROW, False)
         from_left = shift(to_right, COL, True)
         from_right = shift(to_left, COL, False)
-    own, vert, left, right, probe_sum = call(
+        to_left, to_right = call(corners_kernel, [half] * 2, (above, below), "pack_corners")
+        corner_left = shift(to_right, COL, True)
+        corner_right = shift(to_left, COL, False)
+    own, vert, horiz, corner, probe_sum = call(
         grad_kernel,
         [full, full, full, full, (2, N, N)],
         (
-            positions[0, 0], counts, object_field, above, below, from_left, from_right,
-            probe_wave, measured[0, 0], consts,
+            positions, counts, object_field, above, below, from_left, from_right,
+            corner_left, corner_right, probe_wave, measured[0, 0], consts,
         ),
         "slot_gradients",
         scalars=2,
+        vmem=16,
+        flops=16 * 6 * (2 * N) ** 3,
         scratch=[pltpu.VMEM((slices, 2, 2, N, N), jnp.float32) for _ in range(2)],
     )
     with jax.named_scope("gradient_halo"):
+        left, right = call(sides_kernel, [full] * 2, (horiz, corner), "pack_sides")
         got_right = shift(left, COL, False)
         got_left = shift(right, COL, True)
         up, down = call(
@@ -265,13 +310,13 @@
             final_kernel, [full], (own, got_left, got_right, got_above, got_below), "add_own"
         )
     with jax.named_scope("probe_sum"):
-        groups = lax.axis_size(("x", "c"))
-        part = exchange(probe_sum.reshape(2 * N, N), ("x", "c"))
+        plane = ("x", "y", "c")
+        groups = lax.axis_size(plane)
+        part = exchange(probe_sum.reshape(2 * N, N), plane)
         part = part.reshape(groups, 2 * N // groups, N).sum(axis=0)
-        part = gathered_sum(part, "y")
         part = gathered_sum(part, "z")
         spread = jnp.broadcast_to(part, (groups, *part.shape)).reshape(2 * N, N)
-        probe_grad = exchange(spread, ("x", "c")).reshape(2, N, N)
+        probe_grad = exchange(spread, plane).reshape(2, N, N)
     return (result, probe_grad)
 
 

time: 107 us -> 108 us (level)
  blocking collectives: 11.3 us -> 41 us
  starting transfers between devices: 62.8 us -> 46.4 us
  waiting for transfers between devices: 18.2 us -> 7.49 us
  local copies, waits for them, and re-layouts: 4.56 us -> 2.36 us
    all_to_all x1 -> x2, blocking collectives: 11.3 us -> 41 us  [exchange(): return lax.all_to_all(x, axis, 0, 0, tiled=True)]
    all_to_all x3 -> x1, starting transfers between devices: 32.4 us -> 15.2 us  [exchange(): return lax.all_to_all(x, axis, 0, 0, tiled=True)]
    all_to_all x3 -> x1, waiting for transfers between devices: 12.8 us -> 5.31 us  [exchange(): return lax.all_to_all(x, axis, 0, 0, tiled=True)]
    ppermute x8 -> x10, waiting for transfers between devices: 5.37 us -> 2.18 us  [shift(): return lax.ppermute(x, axis, pairs)]
    slice x1 -> x0, local copies, waits for them, and re-layouts: 1.19 us -> none  [per_device(): below = shift(object_field[:, :, :H], ROW, False)]
    ppermute x8 -> x10, starting transfers between devices: 30.4 us -> 31.2 us  [shift(): return lax.ppermute(x, axis, pairs)]
    pallas_call x4 -> x6, Pallas kernels: 7.91 us -> 8.64 us  [call(): pl.pallas_call(kernel, out_shape=[jax.ShapeDtypeStruct(s, jnp.float32) fo...]
  transfers between devices with their start and end apart: 11 -> 11, of which waited for: 6 -> 2; matrix products, arithmetic and copies ran while one was open for 1% -> 1% of each run, Pallas kernels for 1% -> 0%
where the time goes in v2:
time: 108 us
  starting transfers between devices  46.4 us (43%)
  blocking collectives  41 us (38%)
  Pallas kernels  8.64 us (8%)
  waiting for transfers between devices  7.49 us (7%)
  local copies, waits for them, and re-layouts  2.36 us (2%)
  between operations  1.52 us (1%)
    all_to_all x2, blocking collectives, exchange(): return lax.all_to_all(x, axis, 0, 0, tiled=True)  41 us
    ppermute x10, starting transfers between devices, shift(): return lax.ppermute(x, axis, pairs)  31.2 us
    all_to_all x1, starting transfers between devices, exchange(): return lax.all_to_all(x, axis, 0, 0, tiled=True)  15.2 us
    pallas_call x6, Pallas kernels, call(): pl.pallas_call(kernel, out_shape=[jax.ShapeDtypeStruct(s, jnp.float32) fo...  8.64 us
    all_to_all x1, waiting for transfers between devices, exchange(): return lax.all_to_all(x, axis, 0, 0, tiled=True)  5.31 us
    ppermute x10, waiting for transfers between devices, shift(): return lax.ppermute(x, axis, pairs)  2.18 us
  transfers between devices with their start and end apart: 11, of which 2 were waited for; matrix products, arithmetic and copies ran while one was open for 1% of the time, Pallas kernels for 0%

profile of v2, /device:TPU:1, one launch (start us, length us, event | category | flops | bytes accessed | tf_op | source)
XLA Modules:
  0.0 107.5 jit_solution(17350917878886450608)
XLA Ops:
  0.6 0.0 copy-start
  0.6 1.0 copy-done
  1.7 0.0 copy-start.1
  1.7 0.2 pack_edges.1
  1.9 4.0 %collective-permute-start = (f32[4,2,64,128]{3,2,1,0:T(8,128)S(1)}, f32[4,2,64,128]{3,2,1,0:T(8,128)S(1)}, u32[]{:S(2)}, u32[]{:S(2)}) collective-permute-start(f32[4,2,64,128]{3,2,1,0:T(8,128)S(1)} %get-tuple-element.17), channel_id=1, source_target_pairs={{0,16},{16,32},{32,48},{48,64},{64,80},{80,96},{96,112},{112,128},... | collective-permute-start | bytes 786440 | tf_op jit(solution)/shard_map/object_halo/ppermute | solution.py:257
  5.9 1.3 %collective-permute-start.1 = (f32[4,2,64,128]{3,2,1,0:T(8,128)S(1)}, f32[4,2,64,128]{3,2,1,0:T(8,128)S(1)}, u32[]{:S(2)}, u32[]{:S(2)}) collective-permute-start(f32[4,2,64,128]{3,2,1,0:T(8,128)S(1)} %get-tuple-element.18), channel_id=1, source_target_pairs={{16,0},{32,16},{48,32},{64,48},{80,64},{96,80},{112,96},{128,112},... | collective-permute-start | bytes 786440 | tf_op jit(solution)/shard_map/object_halo/ppermute | solution.py:257
  7.2 4.0 %collective-permute-start.2 = (f32[4,2,64,128]{3,2,1,0:T(8,128)S(1)}, f32[4,2,64,128]{3,2,1,0:T(8,128)S(1)}, u32[]{:S(2)}, u32[]{:S(2)}) collective-permute-start(f32[4,2,64,128]{3,2,1,0:T(8,128)S(1)} %get-tuple-element.19), channel_id=1, source_target_pairs={{0,1},{1,2},{2,3},{3,4},{4,5},{5,6},{6,7},{7,8},{8,9},{9,10},{10,1... | collective-permute-start | bytes 786440 | tf_op jit(solution)/shard_map/object_halo/ppermute | solution.py:257
  11.2 0.0 copy-start.2
  11.2 0.0 copy-start.3
  11.2 0.0 copy-start.5
  11.2 7.2 %collective-permute-start.3 = (f32[4,2,64,128]{3,2,1,0:T(8,128)S(1)}, f32[4,2,64,128]{3,2,1,0:T(8,128)S(1)}, u32[]{:S(2)}, u32[]{:S(2)}) collective-permute-start(f32[4,2,64,128]{3,2,1,0:T(8,128)S(1)} %get-tuple-element.20), channel_id=1, source_target_pairs={{1,0},{2,1},{3,2},{4,3},{5,4},{6,5},{7,6},{8,7},{9,8},{10,9},{11,1... | collective-permute-start | bytes 786440 | tf_op jit(solution)/shard_map/object_halo/ppermute | solution.py:257
  18.4 0.0 collective-permute-done.above
  18.4 0.0 collective-permute-done.1.below
  18.4 0.2 pack_corners.1
  18.6 1.9 %collective-permute-start.4 = (f32[4,2,64,128]{3,2,1,0:T(8,128)S(1)}, f32[4,2,64,128]{3,2,1,0:T(8,128)S(1)}, u32[]{:S(2)}, u32[]{:S(2)}) collective-permute-start(f32[4,2,64,128]{3,2,1,0:T(8,128)S(1)} %get-tuple-element.21), channel_id=1, source_target_pairs={{0,1},{1,2},{2,3},{3,4},{4,5},{5,6},{6,7},{7,8},{8,9},{9,10},{10,1... | collective-permute-start | bytes 786440 | tf_op jit(solution)/shard_map/object_halo/ppermute | solution.py:257
  20.6 4.8 %collective-permute-start.5 = (f32[4,2,64,128]{3,2,1,0:T(8,128)S(1)}, f32[4,2,64,128]{3,2,1,0:T(8,128)S(1)}, u32[]{:S(2)}, u32[]{:S(2)}) collective-permute-start(f32[4,2,64,128]{3,2,1,0:T(8,128)S(1)} %get-tuple-element.22), channel_id=1, source_target_pairs={{1,0},{2,1},{3,2},{4,3},{5,4},{6,5},{7,6},{8,7},{9,8},{10,9},{11,1... | collective-permute-start | bytes 786440 | tf_op jit(solution)/shard_map/object_halo/ppermute | solution.py:257
  26.1 0.0 copy-start.4
  26.1 0.0 collective-permute-done.2.from_left
  26.1 0.0 collective-permute-done.3.from_right
  26.1 0.0 collective-permute-done.4.corner_left
  26.1 2.2 %collective-permute-done.5.corner_right = f32[4,2,64,128]{3,2,1,0:T(8,128)S(1)} collective-permute-done((f32[4,2,64,128]{3,2,1,0:T(8,128)S(1)}, f32[4,2,64,128]{3,2,1,0:T(8,128)S(1)}, u32[]{:S(2)}, u32[]{:S(2)}) %collective-permute-start.5) | collective-permute-done | bytes 262176 | tf_op jit(solution)/shard_map/object_halo/ppermute | solution.py:257
  28.3 0.0 copy-done.1
  28.3 0.0 copy-done.2
  28.3 0.0 copy-done.3
  28.3 0.0 copy-done.5
  28.3 0.0 copy-done.4
  28.3 6.4 %slot_gradients.1 = (f32[4,2,128,128]{3,2,1,0:T(8,128)S(1)}, f32[4,2,128,128]{3,2,1,0:T(8,128)S(1)}, f32[4,2,128,128]{3,2,1,0:T(8,128)S(1)}, f32[4,2,128,128]{3,2,1,0:T(8,128)S(1)}, f32[2,128,128]{2,1,0:T(8,128)S(1)}) custom-call(s32[1,1,2,2]{3,2,1,0:T(2,128)S(1)} %copy-done.4, s32[1,1]{1,0:T(1,128)S(6)} %copy.9.count, f32[4,2,128,128]{3,2,1,0:T(8,128)S(1)} %copy-done.1, ...), custom_call_target="tpu_custom_call" | custom-call | flops 1610612736 | bytes 4849684 | tf_op jit(solution)/shard_map/slot_gradients/pallas_call | solution.py:238
  34.7 0.3 pack_sides.1
  35.1 1.9 %collective-permute-start.6 = (f32[4,2,128,128]{3,2,1,0:T(8,128)S(1)}, f32[4,2,128,128]{3,2,1,0:T(8,128)S(1)}, u32[]{:S(2)}, u32[]{:S(2)}) collective-permute-start(f32[4,2,128,128]{3,2,1,0:T(8,128)S(1)} %get-tuple-element.26), channel_id=1, source_target_pairs={{0,1},{1,2},{2,3},{3,4},{4,5},{5,6},{6,7},{7,8},{8,9},{9,10},{10,1... | collective-permute-start | bytes 1572872 | tf_op jit(solution)/shard_map/gradient_halo/ppermute | solution.py:257
  37.0 2.4 %collective-permute-start.7 = (f32[4,2,128,128]{3,2,1,0:T(8,128)S(1)}, f32[4,2,128,128]{3,2,1,0:T(8,128)S(1)}, u32[]{:S(2)}, u32[]{:S(2)}) collective-permute-start(f32[4,2,128,128]{3,2,1,0:T(8,128)S(1)} %get-tuple-element.27), channel_id=1, source_target_pairs={{1,0},{2,1},{3,2},{4,3},{5,4},{6,5},{7,6},{8,7},{9,8},{10,9},{11,1... | collective-permute-start | bytes 1572872 | tf_op jit(solution)/shard_map/gradient_halo/ppermute | solution.py:257
  39.4 24.6 %all_to_all.21 = f32[64,4,128]{2,1,0:T(4,128)S(1)} all-to-all(f32[64,4,128]{2,1,0:T(4,128)S(1)} %bitcast.3), channel_id=1, replica_groups=mesh['z'=12,'x'=4,'y'=8,'c'=2] {'x','y','c'}, dimensions={0} | all-to-all | bytes 262144 | tf_op jit(solution)/shard_map/probe_sum/all_to_all | solution.py:261
  64.0 0.1 reduce_sum.18
  64.1 0.6 broadcast_in_dim.6
  64.7 15.2 %all-to-all-start.1 = ((f32[12,4,128]{2,1,0:T(4,128)}), f32[12,4,128]{2,1,0:T(4,128)S(1)}, u32[]{:S(2)}, u32[]{:S(2)}) async-start(f32[12,4,128]{2,1,0:T(4,128)} %broadcast_in_dim.6), calls=%async_computation.1 | async-start | bytes 49152 | tf_op jit(solution)/shard_map/probe_sum/all_to_all | solution.py:261
  79.9 0.0 collective-permute-done.6.from_left
  79.9 0.0 collective-permute-done.7.from_right
  79.9 0.3 add_vertical.1
  80.3 2.3 %collective-permute-start.8 = (f32[4,2,64,128]{3,2,1,0:T(8,128)S(1)}, f32[4,2,64,128]{3,2,1,0:T(8,128)S(1)}, u32[]{:S(2)}, u32[]{:S(2)}) collective-permute-start(f32[4,2,64,128]{3,2,1,0:T(8,128)S(1)} %get-tuple-element.29), channel_id=1, source_target_pairs={{0,16},{16,32},{32,48},{48,64},{64,80},{80,96},{96,112},{112,128},... | collective-permute-start | bytes 786440 | tf_op jit(solution)/shard_map/gradient_halo/ppermute | solution.py:257
  82.6 1.3 %collective-permute-start.9 = (f32[4,2,64,128]{3,2,1,0:T(8,128)S(1)}, f32[4,2,64,128]{3,2,1,0:T(8,128)S(1)}, u32[]{:S(2)}, u32[]{:S(2)}) collective-permute-start(f32[4,2,64,128]{3,2,1,0:T(8,128)S(1)} %get-tuple-element.30), channel_id=1, source_target_pairs={{16,0},{32,16},{48,32},{64,48},{80,64},{96,80},{112,96},{128,112},... | collective-permute-start | bytes 786440 | tf_op jit(solution)/shard_map/gradient_halo/ppermute | solution.py:257
  83.9 5.3 %all-to-all-done.1 = f32[12,4,128]{2,1,0:T(4,128)S(1)} async-done(((f32[12,4,128]{2,1,0:T(4,128)}), f32[12,4,128]{2,1,0:T(4,128)S(1)}, u32[]{:S(2)}, u32[]{:S(2)}) %all-to-all-start.1) | async-done | bytes 24608 | tf_op jit(solution)/shard_map/probe_sum/all_to_all | solution.py:261
  89.2 16.5 %all_to_all.22 = f32[64,4,128]{2,1,0:T(4,128)S(1)} all-to-all(f32[64,4,128]{2,1,0:T(4,128)S(1)} %broadcast_in_dim.7), channel_id=1, replica_groups=mesh['z'=12,'x'=4,'y'=8,'c'=2] {'x','y','c'}, dimensions={0} | all-to-all | bytes 262144 | tf_op jit(solution)/shard_map/probe_sum/all_to_all | solution.py:261
  105.7 0.0 collective-permute-done.8.from_above
  105.7 0.0 collective-permute-done.9.from_below
  105.7 1.1 %add_own.1 = f32[4,2,128,128]{3,2,1,0:T(8,128)} custom-call(f32[4,2,128,128]{3,2,1,0:T(8,128)S(1)} %get-tuple-element.23.own, f32[4,2,128,128]{3,2,1,0:T(8,128)S(1)} %collective-permute-done.6.from_left, f32[4,2,128,128]{3,2,1,0:T(8,128)S(1)} %collective-permute-done.7.from_right, f32[4,2,64,128]{3,2,1,0:T(8,128)S(1)} %collective-permute-done.8.from_above, ...), custom_call_target="tpu_custom_call" | custom-call | bytes 2621440 | tf_op jit(solution)/shard_map/gradient_halo/add_own/pallas_call | solution.py:238
  106.9 0.7 copy.10
  (2 shorter events, 0.0 us)
Async XLA Ops:
  0.6 1.0 copy-start
  1.7 26.6 %copy-start.1 = (f32[4,2,128,128]{3,2,1,0:T(8,128)S(1)}, f32[4,2,128,128]{3,2,1,0:T(8,128)}, u32[]{:S(2)}) copy-start(f32[4,2,128,128]{3,2,1,0:T(8,128)} %tile.3) | copy-start | bytes 1572868
  1.9 16.5 %collective-permute-start = (f32[4,2,64,128]{3,2,1,0:T(8,128)S(1)}, f32[4,2,64,128]{3,2,1,0:T(8,128)S(1)}, u32[]{:S(2)}, u32[]{:S(2)}) collective-permute-start(f32[4,2,64,128]{3,2,1,0:T(8,128)S(1)} %get-tuple-element.17), channel_id=1, source_target_pairs={{0,16},{16,32},{32,48},{48,64},{64,80},{80,96},{96,112},{112,128},... | collective-permute-start | bytes 786440 | tf_op jit(solution)/shard_map/object_halo/ppermute | solution.py:257
  5.9 12.6 %collective-permute-start.1 = (f32[4,2,64,128]{3,2,1,0:T(8,128)S(1)}, f32[4,2,64,128]{3,2,1,0:T(8,128)S(1)}, u32[]{:S(2)}, u32[]{:S(2)}) collective-permute-start(f32[4,2,64,128]{3,2,1,0:T(8,128)S(1)} %get-tuple-element.18), channel_id=1, source_target_pairs={{16,0},{32,16},{48,32},{64,48},{80,64},{96,80},{112,96},{128,112},... | collective-permute-start | bytes 786440 | tf_op jit(solution)/shard_map/object_halo/ppermute | solution.py:257
  7.2 18.9 %collective-permute-start.2 = (f32[4,2,64,128]{3,2,1,0:T(8,128)S(1)}, f32[4,2,64,128]{3,2,1,0:T(8,128)S(1)}, u32[]{:S(2)}, u32[]{:S(2)}) collective-permute-start(f32[4,2,64,128]{3,2,1,0:T(8,128)S(1)} %get-tuple-element.19), channel_id=1, source_target_pairs={{0,1},{1,2},{2,3},{3,4},{4,5},{5,6},{6,7},{7,8},{8,9},{9,10},{10,1... | collective-permute-start | bytes 786440 | tf_op jit(solution)/shard_map/object_halo/ppermute | solution.py:257
  11.2 17.1 %copy-start.2 = (f32[2,128,128]{2,1,0:T(8,128)S(1)}, f32[2,128,128]{2,1,0:T(8,128)}, u32[]{:S(2)}) copy-start(f32[2,128,128]{2,1,0:T(8,128)} %probe.1) | copy-start | bytes 393220
  11.2 17.0 %copy-start.3 = (f32[1,1,2,128,128]{4,3,2,1,0:T(8,128)S(1)}, f32[1,1,2,128,128]{4,3,2,1,0:T(8,128)}, u32[]{:S(2)}) copy-start(f32[1,1,2,128,128]{4,3,2,1,0:T(8,128)} %param.10) | copy-start | bytes 393220
  11.2 17.0 %copy-start.5 = (bf16[8,128,128]{2,1,0:T(8,128)(2,1)S(1)}, bf16[8,128,128]{2,1,0:T(8,128)(2,1)}, u32[]{:S(2)}) copy-start(bf16[8,128,128]{2,1,0:T(8,128)(2,1)} %constant.4.clone.consts) | copy-start | bytes 786436
  11.2 14.8 %collective-permute-start.3 = (f32[4,2,64,128]{3,2,1,0:T(8,128)S(1)}, f32[4,2,64,128]{3,2,1,0:T(8,128)S(1)}, u32[]{:S(2)}, u32[]{:S(2)}) collective-permute-start(f32[4,2,64,128]{3,2,1,0:T(8,128)S(1)} %get-tuple-element.20), channel_id=1, source_target_pairs={{1,0},{2,1},{3,2},{4,3},{5,4},{6,5},{7,6},{8,7},{9,8},{10,9},{11,1... | collective-permute-start | bytes 786440 | tf_op jit(solution)/shard_map/object_halo/ppermute | solution.py:257
  18.6 7.5 %collective-permute-start.4 = (f32[4,2,64,128]{3,2,1,0:T(8,128)S(1)}, f32[4,2,64,128]{3,2,1,0:T(8,128)S(1)}, u32[]{:S(2)}, u32[]{:S(2)}) collective-permute-start(f32[4,2,64,128]{3,2,1,0:T(8,128)S(1)} %get-tuple-element.21), channel_id=1, source_target_pairs={{0,1},{1,2},{2,3},{3,4},{4,5},{5,6},{6,7},{7,8},{8,9},{9,10},{10,1... | collective-permute-start | bytes 786440 | tf_op jit(solution)/shard_map/object_halo/ppermute | solution.py:257
  20.6 7.7 %collective-permute-start.5 = (f32[4,2,64,128]{3,2,1,0:T(8,128)S(1)}, f32[4,2,64,128]{3,2,1,0:T(8,128)S(1)}, u32[]{:S(2)}, u32[]{:S(2)}) collective-permute-start(f32[4,2,64,128]{3,2,1,0:T(8,128)S(1)} %get-tuple-element.22), channel_id=1, source_target_pairs={{1,0},{2,1},{3,2},{4,3},{5,4},{6,5},{7,6},{8,7},{9,8},{10,9},{11,1... | collective-permute-start | bytes 786440 | tf_op jit(solution)/shard_map/object_halo/ppermute | solution.py:257
  26.1 2.2 %copy-start.4 = (s32[1,1,2,2]{3,2,1,0:T(2,128)S(1)}, s32[1,1,2,2]{3,2,1,0:T(2,128)}, u32[]{:S(2)}) copy-start(s32[1,1,2,2]{3,2,1,0:T(2,128)} %pos.1) | copy-start | bytes 52
  35.1 44.8 %collective-permute-start.6 = (f32[4,2,128,128]{3,2,1,0:T(8,128)S(1)}, f32[4,2,128,128]{3,2,1,0:T(8,128)S(1)}, u32[]{:S(2)}, u32[]{:S(2)}) collective-permute-start(f32[4,2,128,128]{3,2,1,0:T(8,128)S(1)} %get-tuple-element.26), channel_id=1, source_target_pairs={{0,1},{1,2},{2,3},{3,4},{4,5},{5,6},{6,7},{7,8},{8,9},{9,10},{10,1... | collective-permute-start | bytes 1572872 | tf_op jit(solution)/shard_map/gradient_halo/ppermute | solution.py:257
  37.0 42.9 %collective-permute-start.7 = (f32[4,2,128,128]{3,2,1,0:T(8,128)S(1)}, f32[4,2,128,128]{3,2,1,0:T(8,128)S(1)}, u32[]{:S(2)}, u32[]{:S(2)}) collective-permute-start(f32[4,2,128,128]{3,2,1,0:T(8,128)S(1)} %get-tuple-element.27), channel_id=1, source_target_pairs={{1,0},{2,1},{3,2},{4,3},{5,4},{6,5},{7,6},{8,7},{9,8},{10,9},{11,1... | collective-permute-start | bytes 1572872 | tf_op jit(solution)/shard_map/gradient_halo/ppermute | solution.py:257
  64.7 24.5 %all-to-all-start.1 = ((f32[12,4,128]{2,1,0:T(4,128)}), f32[12,4,128]{2,1,0:T(4,128)S(1)}, u32[]{:S(2)}, u32[]{:S(2)}) async-start(f32[12,4,128]{2,1,0:T(4,128)} %broadcast_in_dim.6), calls=%async_computation.1 | async-start | bytes 49152 | tf_op jit(solution)/shard_map/probe_sum/all_to_all | solution.py:261
  80.3 25.5 %collective-permute-start.8 = (f32[4,2,64,128]{3,2,1,0:T(8,128)S(1)}, f32[4,2,64,128]{3,2,1,0:T(8,128)S(1)}, u32[]{:S(2)}, u32[]{:S(2)}) collective-permute-start(f32[4,2,64,128]{3,2,1,0:T(8,128)S(1)} %get-tuple-element.29), channel_id=1, source_target_pairs={{0,16},{16,32},{32,48},{48,64},{64,80},{80,96},{96,112},{112,128},... | collective-permute-start | bytes 786440 | tf_op jit(solution)/shard_map/gradient_halo/ppermute | solution.py:257
  82.6 23.1 %collective-permute-start.9 = (f32[4,2,64,128]{3,2,1,0:T(8,128)S(1)}, f32[4,2,64,128]{3,2,1,0:T(8,128)S(1)}, u32[]{:S(2)}, u32[]{:S(2)}) collective-permute-start(f32[4,2,64,128]{3,2,1,0:T(8,128)S(1)} %get-tuple-element.30), channel_id=1, source_target_pairs={{16,0},{32,16},{48,32},{64,48},{80,64},{96,80},{112,96},{128,112},... | collective-permute-start | bytes 786440 | tf_op jit(solution)/shard_map/gradient_halo/ppermute | solution.py:257

commit v3 on v2

--- a/solution.py
+++ b/solution.py
@@ -310,13 +310,14 @@
             final_kernel, [full], (own, got_left, got_right, got_above, got_below), "add_own"
         )
     with jax.named_scope("probe_sum"):
-        plane = ("x", "y", "c")
-        groups = lax.axis_size(plane)
-        part = exchange(probe_sum.reshape(2 * N, N), plane)
+        near = ("x", "c")
+        groups = lax.axis_size(near)
+        part = exchange(probe_sum.reshape(2 * N, N), near)
         part = part.reshape(groups, 2 * N // groups, N).sum(axis=0)
+        part = gathered_sum(part, "y")
         part = gathered_sum(part, "z")
         spread = jnp.broadcast_to(part, (groups, *part.shape)).reshape(2 * N, N)
-        probe_grad = exchange(spread, plane).reshape(2, N, N)
+        probe_grad = exchange(spread, near).reshape(2, N, N)
     return (result, probe_grad)
 
 

time: 108 us -> 104 us (0.963)
  blocking collectives: 41 us -> 11.3 us
  starting transfers between devices: 46.4 us -> 63.5 us
  waiting for transfers between devices: 7.49 us -> 14.4 us
  local copies, waits for them, and re-layouts: 2.36 us -> 3.75 us
    all_to_all x2 -> x1, blocking collectives: 41 us -> 11.3 us  [exchange(): return lax.all_to_all(x, axis, 0, 0, tiled=True)]
    all_to_all x1 -> x3, starting transfers between devices: 15.2 us -> 30.2 us  [exchange(): return lax.all_to_all(x, axis, 0, 0, tiled=True)]
    all_to_all x1 -> x3, waiting for transfers between devices: 5.31 us -> 12.2 us  [exchange(): return lax.all_to_all(x, axis, 0, 0, tiled=True)]
    ppermute x10, starting transfers between devices: 31.2 us -> 33.3 us  [shift(): return lax.ppermute(x, axis, pairs)]
  transfers between devices with their start and end apart: 11 -> 13, of which waited for: 2 -> 4; matrix products, arithmetic and copies ran while one was open for 1% -> 1% of each run, Pallas kernels for 0% -> 2%
where the time goes in v3:
time: 104 us; the launch traced here: 103 us
  starting transfers between devices  63.5 us (61%)
  waiting for transfers between devices  14.4 us (14%)
  blocking collectives  11.3 us (11%)
  Pallas kernels  8.65 us (8%)
  local copies, waits for them, and re-layouts  3.75 us (4%)
  between operations  1.53 us (1%)
    ppermute x10, starting transfers between devices, shift(): return lax.ppermute(x, axis, pairs)  33.3 us
    all_to_all x3, starting transfers between devices, exchange(): return lax.all_to_all(x, axis, 0, 0, tiled=True)  30.2 us
    all_to_all x3, waiting for transfers between devices, exchange(): return lax.all_to_all(x, axis, 0, 0, tiled=True)  12.2 us
    all_to_all x1, blocking collectives, exchange(): return lax.all_to_all(x, axis, 0, 0, tiled=True)  11.3 us
    pallas_call x6, Pallas kernels, call(): pl.pallas_call(kernel, out_shape=[jax.ShapeDtypeStruct(s, jnp.float32) fo...  8.65 us
    ppermute x10, waiting for transfers between devices, shift(): return lax.ppermute(x, axis, pairs)  2.18 us
  transfers between devices with their start and end apart: 13, of which 4 were waited for; matrix products, arithmetic and copies ran while one was open for 1% of the time, Pallas kernels for 2%

profile of v3, /device:TPU:1, one launch (start us, length us, event | category | flops | bytes accessed | tf_op | source)
XLA Modules:
  0.0 103.2 jit_solution(10571689122624019602)
XLA Ops:
  0.6 0.0 copy-start
  0.6 1.0 %copy-done = f32[4,2,128,128]{3,2,1,0:T(8,128)S(1)} copy-done((f32[4,2,128,128]{3,2,1,0:T(8,128)S(1)}, f32[4,2,128,128]{3,2,1,0:T(8,128)}, u32[]{:S(2)}) %copy-start) | copy-done | bytes 524312
  1.7 0.2 pack_edges.1
  1.9 4.0 %collective-permute-start = (f32[4,2,64,128]{3,2,1,0:T(8,128)S(1)}, f32[4,2,64,128]{3,2,1,0:T(8,128)S(1)}, u32[]{:S(2)}, u32[]{:S(2)}) collective-permute-start(f32[4,2,64,128]{3,2,1,0:T(8,128)S(1)} %get-tuple-element.17), channel_id=1, source_target_pairs={{0,16},{16,32},{32,48},{48,64},{64,80},{80,96},{96,112},{112,128},... | collective-permute-start | bytes 786440 | tf_op jit(solution)/shard_map/object_halo/ppermute | solution.py:257
  5.9 1.3 %collective-permute-start.1 = (f32[4,2,64,128]{3,2,1,0:T(8,128)S(1)}, f32[4,2,64,128]{3,2,1,0:T(8,128)S(1)}, u32[]{:S(2)}, u32[]{:S(2)}) collective-permute-start(f32[4,2,64,128]{3,2,1,0:T(8,128)S(1)} %get-tuple-element.18), channel_id=1, source_target_pairs={{16,0},{32,16},{48,32},{64,48},{80,64},{96,80},{112,96},{128,112},... | collective-permute-start | bytes 786440 | tf_op jit(solution)/shard_map/object_halo/ppermute | solution.py:257
  7.2 4.0 %collective-permute-start.2 = (f32[4,2,64,128]{3,2,1,0:T(8,128)S(1)}, f32[4,2,64,128]{3,2,1,0:T(8,128)S(1)}, u32[]{:S(2)}, u32[]{:S(2)}) collective-permute-start(f32[4,2,64,128]{3,2,1,0:T(8,128)S(1)} %get-tuple-element.19), channel_id=1, source_target_pairs={{0,1},{1,2},{2,3},{3,4},{4,5},{5,6},{6,7},{7,8},{8,9},{9,10},{10,1... | collective-permute-start | bytes 786440 | tf_op jit(solution)/shard_map/object_halo/ppermute | solution.py:257
  11.2 0.0 copy-start.2
  11.2 0.0 copy-start.3
  11.2 0.0 copy-start.5
  11.2 7.2 %collective-permute-start.3 = (f32[4,2,64,128]{3,2,1,0:T(8,128)S(1)}, f32[4,2,64,128]{3,2,1,0:T(8,128)S(1)}, u32[]{:S(2)}, u32[]{:S(2)}) collective-permute-start(f32[4,2,64,128]{3,2,1,0:T(8,128)S(1)} %get-tuple-element.20), channel_id=1, source_target_pairs={{1,0},{2,1},{3,2},{4,3},{5,4},{6,5},{7,6},{8,7},{9,8},{10,9},{11,1... | collective-permute-start | bytes 786440 | tf_op jit(solution)/shard_map/object_halo/ppermute | solution.py:257
  18.4 0.0 collective-permute-done.above
  18.4 0.0 collective-permute-done.1.below
  18.4 0.2 pack_corners.1
  18.6 1.9 %collective-permute-start.4 = (f32[4,2,64,128]{3,2,1,0:T(8,128)S(1)}, f32[4,2,64,128]{3,2,1,0:T(8,128)S(1)}, u32[]{:S(2)}, u32[]{:S(2)}) collective-permute-start(f32[4,2,64,128]{3,2,1,0:T(8,128)S(1)} %get-tuple-element.21), channel_id=1, source_target_pairs={{0,1},{1,2},{2,3},{3,4},{4,5},{5,6},{6,7},{7,8},{8,9},{9,10},{10,1... | collective-permute-start | bytes 786440 | tf_op jit(solution)/shard_map/object_halo/ppermute | solution.py:257
  20.6 4.8 %collective-permute-start.5 = (f32[4,2,64,128]{3,2,1,0:T(8,128)S(1)}, f32[4,2,64,128]{3,2,1,0:T(8,128)S(1)}, u32[]{:S(2)}, u32[]{:S(2)}) collective-permute-start(f32[4,2,64,128]{3,2,1,0:T(8,128)S(1)} %get-tuple-element.22), channel_id=1, source_target_pairs={{1,0},{2,1},{3,2},{4,3},{5,4},{6,5},{7,6},{8,7},{9,8},{10,9},{11,1... | collective-permute-start | bytes 786440 | tf_op jit(solution)/shard_map/object_halo/ppermute | solution.py:257
  26.1 0.0 copy-start.4
  26.1 0.0 collective-permute-done.2.from_left
  26.1 0.0 collective-permute-done.3.from_right
  26.1 0.0 collective-permute-done.4.corner_left
  26.1 2.2 %collective-permute-done.5.corner_right = f32[4,2,64,128]{3,2,1,0:T(8,128)S(1)} collective-permute-done((f32[4,2,64,128]{3,2,1,0:T(8,128)S(1)}, f32[4,2,64,128]{3,2,1,0:T(8,128)S(1)}, u32[]{:S(2)}, u32[]{:S(2)}) %collective-permute-start.5) | collective-permute-done | bytes 262176 | tf_op jit(solution)/shard_map/object_halo/ppermute | solution.py:257
  28.3 0.0 copy-done.1
  28.3 0.0 copy-done.2
  28.3 0.0 copy-done.3
  28.3 0.0 copy-done.5
  28.3 0.0 copy-done.4
  28.3 6.5 %slot_gradients.1 = (f32[4,2,128,128]{3,2,1,0:T(8,128)S(1)}, f32[4,2,128,128]{3,2,1,0:T(8,128)S(1)}, f32[4,2,128,128]{3,2,1,0:T(8,128)S(1)}, f32[4,2,128,128]{3,2,1,0:T(8,128)S(1)}, f32[2,128,128]{2,1,0:T(8,128)S(1)}) custom-call(s32[1,1,2,2]{3,2,1,0:T(2,128)S(1)} %copy-done.4, s32[1,1]{1,0:T(1,128)S(6)} %copy.9.count, f32[4,2,128,128]{3,2,1,0:T(8,128)S(1)} %copy-done.1, ...), custom_call_target="tpu_custom_call" | custom-call | flops 1610612736 | bytes 4849684 | tf_op jit(solution)/shard_map/slot_gradients/pallas_call | solution.py:238
  34.7 11.3 %all_to_all.27 = f32[8,32,128]{2,1,0:T(8,128)S(1)} all-to-all(f32[8,32,128]{2,1,0:T(8,128)S(1)} %bitcast.3), channel_id=1, replica_groups=mesh['z'=12,'x'=4,'y'=8,'c'=2] {'x','c'}, dimensions={0} | all-to-all | bytes 262144 | tf_op jit(solution)/shard_map/probe_sum/all_to_all | solution.py:261
  46.1 0.7 broadcast_in_dim.9
  46.7 7.0 %all-to-all-start.1 = ((f32[8,32,128]{2,1,0:T(8,128)}), f32[8,32,128]{2,1,0:T(8,128)S(1)}, u32[]{:S(2)}, u32[]{:S(2)}) async-start(f32[8,32,128]{2,1,0:T(8,128)} %broadcast_in_dim.9), calls=%async_computation.1 | async-start | bytes 262144 | tf_op jit(solution)/shard_map/probe_sum/all_to_all | solution.py:261
  53.8 0.3 pack_sides.1
  54.1 4.7 %collective-permute-start.6 = (f32[4,2,128,128]{3,2,1,0:T(8,128)S(1)}, f32[4,2,128,128]{3,2,1,0:T(8,128)S(1)}, u32[]{:S(2)}, u32[]{:S(2)}) collective-permute-start(f32[4,2,128,128]{3,2,1,0:T(8,128)S(1)} %get-tuple-element.26), channel_id=1, source_target_pairs={{0,1},{1,2},{2,3},{3,4},{4,5},{5,6},{6,7},{7,8},{8,9},{9,10},{10,1... | collective-permute-start | bytes 1572872 | tf_op jit(solution)/shard_map/gradient_halo/ppermute | solution.py:257
  58.8 1.9 %collective-permute-start.7 = (f32[4,2,128,128]{3,2,1,0:T(8,128)S(1)}, f32[4,2,128,128]{3,2,1,0:T(8,128)S(1)}, u32[]{:S(2)}, u32[]{:S(2)}) collective-permute-start(f32[4,2,128,128]{3,2,1,0:T(8,128)S(1)} %get-tuple-element.27), channel_id=1, source_target_pairs={{1,0},{2,1},{3,2},{4,3},{5,4},{6,5},{7,6},{8,7},{9,8},{10,9},{11,1... | collective-permute-start | bytes 1572872 | tf_op jit(solution)/shard_map/gradient_halo/ppermute | solution.py:257
  60.7 0.9 all-to-all-done.1
  61.6 0.7 broadcast_in_dim.10
  62.3 15.2 %all-to-all-start.2 = ((f32[12,32,128]{2,1,0:T(8,128)}), f32[12,32,128]{2,1,0:T(8,128)S(1)}, u32[]{:S(2)}, u32[]{:S(2)}) async-start(f32[12,32,128]{2,1,0:T(8,128)} %broadcast_in_dim.10), calls=%async_computation.2 | async-start | bytes 393216 | tf_op jit(solution)/shard_map/probe_sum/all_to_all | solution.py:261
  77.5 0.0 collective-permute-done.6.from_left
  77.5 0.0 collective-permute-done.7.from_right
  77.5 0.3 add_vertical.1
  77.9 2.2 %collective-permute-start.8 = (f32[4,2,64,128]{3,2,1,0:T(8,128)S(1)}, f32[4,2,64,128]{3,2,1,0:T(8,128)S(1)}, u32[]{:S(2)}, u32[]{:S(2)}) collective-permute-start(f32[4,2,64,128]{3,2,1,0:T(8,128)S(1)} %get-tuple-element.29), channel_id=1, source_target_pairs={{0,16},{16,32},{32,48},{48,64},{64,80},{80,96},{96,112},{112,128},... | collective-permute-start | bytes 786440 | tf_op jit(solution)/shard_map/gradient_halo/ppermute | solution.py:257
  80.1 1.3 %collective-permute-start.9 = (f32[4,2,64,128]{3,2,1,0:T(8,128)S(1)}, f32[4,2,64,128]{3,2,1,0:T(8,128)S(1)}, u32[]{:S(2)}, u32[]{:S(2)}) collective-permute-start(f32[4,2,64,128]{3,2,1,0:T(8,128)S(1)} %get-tuple-element.30), channel_id=1, source_target_pairs={{16,0},{32,16},{48,32},{64,48},{80,64},{96,80},{112,96},{128,112},... | collective-permute-start | bytes 786440 | tf_op jit(solution)/shard_map/gradient_halo/ppermute | solution.py:257
  81.4 7.2 %all-to-all-done.2 = f32[12,32,128]{2,1,0:T(8,128)S(1)} async-done(((f32[12,32,128]{2,1,0:T(8,128)}), f32[12,32,128]{2,1,0:T(8,128)S(1)}, u32[]{:S(2)}, u32[]{:S(2)}) %all-to-all-start.2) | async-done | bytes 196640 | tf_op jit(solution)/shard_map/probe_sum/all_to_all | solution.py:261
  88.6 0.7 broadcast_in_dim.11
  89.3 8.0 %all-to-all-start.3 = ((f32[8,32,128]{2,1,0:T(8,128)}), f32[8,32,128]{2,1,0:T(8,128)S(1)}, u32[]{:S(2)}, u32[]{:S(2)}) async-start(f32[8,32,128]{2,1,0:T(8,128)} %broadcast_in_dim.11), calls=%async_computation.3 | async-start | bytes 262144 | tf_op jit(solution)/shard_map/probe_sum/all_to_all | solution.py:261
  97.2 0.0 collective-permute-done.8.from_above
  97.2 0.0 collective-permute-done.9.from_below
  97.2 1.1 %add_own.1 = f32[4,2,128,128]{3,2,1,0:T(8,128)} custom-call(f32[4,2,128,128]{3,2,1,0:T(8,128)S(1)} %get-tuple-element.23.own, f32[4,2,128,128]{3,2,1,0:T(8,128)S(1)} %collective-permute-done.6.from_left, f32[4,2,128,128]{3,2,1,0:T(8,128)S(1)} %collective-permute-done.7.from_right, f32[4,2,64,128]{3,2,1,0:T(8,128)S(1)} %collective-permute-done.8.from_above, ...), custom_call_target="tpu_custom_call" | custom-call | bytes 2621440 | tf_op jit(solution)/shard_map/gradient_halo/add_own/pallas_call | solution.py:238
  98.4 4.1 %all-to-all-done.3 = f32[8,32,128]{2,1,0:T(8,128)S(1)} async-done(((f32[8,32,128]{2,1,0:T(8,128)}), f32[8,32,128]{2,1,0:T(8,128)S(1)}, u32[]{:S(2)}, u32[]{:S(2)}) %all-to-all-start.3) | async-done | bytes 131104 | tf_op jit(solution)/shard_map/probe_sum/all_to_all | solution.py:261
  102.5 0.7 copy.10
  (4 shorter events, 0.0 us)
Async XLA Ops:
  0.6 1.0 %copy-start = (f32[4,2,128,128]{3,2,1,0:T(8,128)S(1)}, f32[4,2,128,128]{3,2,1,0:T(8,128)}, u32[]{:S(2)}) copy-start(f32[4,2,128,128]{3,2,1,0:T(8,128)} %tile.3) | copy-start | bytes 1572868
  1.7 26.6 %copy-start.1 = (f32[4,2,128,128]{3,2,1,0:T(8,128)S(1)}, f32[4,2,128,128]{3,2,1,0:T(8,128)}, u32[]{:S(2)}) copy-start(f32[4,2,128,128]{3,2,1,0:T(8,128)} %tile.3) | copy-start | bytes 1572868
  1.9 16.5 %collective-permute-start = (f32[4,2,64,128]{3,2,1,0:T(8,128)S(1)}, f32[4,2,64,128]{3,2,1,0:T(8,128)S(1)}, u32[]{:S(2)}, u32[]{:S(2)}) collective-permute-start(f32[4,2,64,128]{3,2,1,0:T(8,128)S(1)} %get-tuple-element.17), channel_id=1, source_target_pairs={{0,16},{16,32},{32,48},{48,64},{64,80},{80,96},{96,112},{112,128},... | collective-permute-start | bytes 786440 | tf_op jit(solution)/shard_map/object_halo/ppermute | solution.py:257
  5.9 12.6 %collective-permute-start.1 = (f32[4,2,64,128]{3,2,1,0:T(8,128)S(1)}, f32[4,2,64,128]{3,2,1,0:T(8,128)S(1)}, u32[]{:S(2)}, u32[]{:S(2)}) collective-permute-start(f32[4,2,64,128]{3,2,1,0:T(8,128)S(1)} %get-tuple-element.18), channel_id=1, source_target_pairs={{16,0},{32,16},{48,32},{64,48},{80,64},{96,80},{112,96},{128,112},... | collective-permute-start | bytes 786440 | tf_op jit(solution)/shard_map/object_halo/ppermute | solution.py:257
  7.2 18.9 %collective-permute-start.2 = (f32[4,2,64,128]{3,2,1,0:T(8,128)S(1)}, f32[4,2,64,128]{3,2,1,0:T(8,128)S(1)}, u32[]{:S(2)}, u32[]{:S(2)}) collective-permute-start(f32[4,2,64,128]{3,2,1,0:T(8,128)S(1)} %get-tuple-element.19), channel_id=1, source_target_pairs={{0,1},{1,2},{2,3},{3,4},{4,5},{5,6},{6,7},{7,8},{8,9},{9,10},{10,1... | collective-permute-start | bytes 786440 | tf_op jit(solution)/shard_map/object_halo/ppermute | solution.py:257
  11.2 17.1 %copy-start.2 = (f32[2,128,128]{2,1,0:T(8,128)S(1)}, f32[2,128,128]{2,1,0:T(8,128)}, u32[]{:S(2)}) copy-start(f32[2,128,128]{2,1,0:T(8,128)} %probe.1) | copy-start | bytes 393220
  11.2 17.0 %copy-start.3 = (f32[1,1,2,128,128]{4,3,2,1,0:T(8,128)S(1)}, f32[1,1,2,128,128]{4,3,2,1,0:T(8,128)}, u32[]{:S(2)}) copy-start(f32[1,1,2,128,128]{4,3,2,1,0:T(8,128)} %param.10) | copy-start | bytes 393220
  11.2 17.0 %copy-start.5 = (bf16[8,128,128]{2,1,0:T(8,128)(2,1)S(1)}, bf16[8,128,128]{2,1,0:T(8,128)(2,1)}, u32[]{:S(2)}) copy-start(bf16[8,128,128]{2,1,0:T(8,128)(2,1)} %constant.4.clone.consts) | copy-start | bytes 786436
  11.2 14.8 %collective-permute-start.3 = (f32[4,2,64,128]{3,2,1,0:T(8,128)S(1)}, f32[4,2,64,128]{3,2,1,0:T(8,128)S(1)}, u32[]{:S(2)}, u32[]{:S(2)}) collective-permute-start(f32[4,2,64,128]{3,2,1,0:T(8,128)S(1)} %get-tuple-element.20), channel_id=1, source_target_pairs={{1,0},{2,1},{3,2},{4,3},{5,4},{6,5},{7,6},{8,7},{9,8},{10,9},{11,1... | collective-permute-start | bytes 786440 | tf_op jit(solution)/shard_map/object_halo/ppermute | solution.py:257
  18.6 7.5 %collective-permute-start.4 = (f32[4,2,64,128]{3,2,1,0:T(8,128)S(1)}, f32[4,2,64,128]{3,2,1,0:T(8,128)S(1)}, u32[]{:S(2)}, u32[]{:S(2)}) collective-permute-start(f32[4,2,64,128]{3,2,1,0:T(8,128)S(1)} %get-tuple-element.21), channel_id=1, source_target_pairs={{0,1},{1,2},{2,3},{3,4},{4,5},{5,6},{6,7},{7,8},{8,9},{9,10},{10,1... | collective-permute-start | bytes 786440 | tf_op jit(solution)/shard_map/object_halo/ppermute | solution.py:257
  20.6 7.7 %collective-permute-start.5 = (f32[4,2,64,128]{3,2,1,0:T(8,128)S(1)}, f32[4,2,64,128]{3,2,1,0:T(8,128)S(1)}, u32[]{:S(2)}, u32[]{:S(2)}) collective-permute-start(f32[4,2,64,128]{3,2,1,0:T(8,128)S(1)} %get-tuple-element.22), channel_id=1, source_target_pairs={{1,0},{2,1},{3,2},{4,3},{5,4},{6,5},{7,6},{8,7},{9,8},{10,9},{11,1... | collective-permute-start | bytes 786440 | tf_op jit(solution)/shard_map/object_halo/ppermute | solution.py:257
  26.1 2.2 %copy-start.4 = (s32[1,1,2,2]{3,2,1,0:T(2,128)S(1)}, s32[1,1,2,2]{3,2,1,0:T(2,128)}, u32[]{:S(2)}) copy-start(s32[1,1,2,2]{3,2,1,0:T(2,128)} %pos.1) | copy-start | bytes 52
  46.7 14.9 %all-to-all-start.1 = ((f32[8,32,128]{2,1,0:T(8,128)}), f32[8,32,128]{2,1,0:T(8,128)S(1)}, u32[]{:S(2)}, u32[]{:S(2)}) async-start(f32[8,32,128]{2,1,0:T(8,128)} %broadcast_in_dim.9), calls=%async_computation.1 | async-start | bytes 262144 | tf_op jit(solution)/shard_map/probe_sum/all_to_all | solution.py:261
  54.1 23.4 %collective-permute-start.6 = (f32[4,2,128,128]{3,2,1,0:T(8,128)S(1)}, f32[4,2,128,128]{3,2,1,0:T(8,128)S(1)}, u32[]{:S(2)}, u32[]{:S(2)}) collective-permute-start(f32[4,2,128,128]{3,2,1,0:T(8,128)S(1)} %get-tuple-element.26), channel_id=1, source_target_pairs={{0,1},{1,2},{2,3},{3,4},{4,5},{5,6},{6,7},{7,8},{8,9},{9,10},{10,1... | collective-permute-start | bytes 1572872 | tf_op jit(solution)/shard_map/gradient_halo/ppermute | solution.py:257
  58.8 18.7 %collective-permute-start.7 = (f32[4,2,128,128]{3,2,1,0:T(8,128)S(1)}, f32[4,2,128,128]{3,2,1,0:T(8,128)S(1)}, u32[]{:S(2)}, u32[]{:S(2)}) collective-permute-start(f32[4,2,128,128]{3,2,1,0:T(8,128)S(1)} %get-tuple-element.27), channel_id=1, source_target_pairs={{1,0},{2,1},{3,2},{4,3},{5,4},{6,5},{7,6},{8,7},{9,8},{10,9},{11,1... | collective-permute-start | bytes 1572872 | tf_op jit(solution)/shard_map/gradient_halo/ppermute | solution.py:257
  62.3 26.3 %all-to-all-start.2 = ((f32[12,32,128]{2,1,0:T(8,128)}), f32[12,32,128]{2,1,0:T(8,128)S(1)}, u32[]{:S(2)}, u32[]{:S(2)}) async-start(f32[12,32,128]{2,1,0:T(8,128)} %broadcast_in_dim.10), calls=%async_computation.2 | async-start | bytes 393216 | tf_op jit(solution)/shard_map/probe_sum/all_to_all | solution.py:261
  77.9 19.3 %collective-permute-start.8 = (f32[4,2,64,128]{3,2,1,0:T(8,128)S(1)}, f32[4,2,64,128]{3,2,1,0:T(8,128)S(1)}, u32[]{:S(2)}, u32[]{:S(2)}) collective-permute-start(f32[4,2,64,128]{3,2,1,0:T(8,128)S(1)} %get-tuple-element.29), channel_id=1, source_target_pairs={{0,16},{16,32},{32,48},{48,64},{64,80},{80,96},{96,112},{112,128},... | collective-permute-start | bytes 786440 | tf_op jit(solution)/shard_map/gradient_halo/ppermute | solution.py:257
  80.1 17.1 %collective-permute-start.9 = (f32[4,2,64,128]{3,2,1,0:T(8,128)S(1)}, f32[4,2,64,128]{3,2,1,0:T(8,128)S(1)}, u32[]{:S(2)}, u32[]{:S(2)}) collective-permute-start(f32[4,2,64,128]{3,2,1,0:T(8,128)S(1)} %get-tuple-element.30), channel_id=1, source_target_pairs={{16,0},{32,16},{48,32},{64,48},{80,64},{96,80},{112,96},{128,112},... | collective-permute-start | bytes 786440 | tf_op jit(solution)/shard_map/gradient_halo/ppermute | solution.py:257
  89.3 13.2 %all-to-all-start.3 = ((f32[8,32,128]{2,1,0:T(8,128)}), f32[8,32,128]{2,1,0:T(8,128)S(1)}, u32[]{:S(2)}, u32[]{:S(2)}) async-start(f32[8,32,128]{2,1,0:T(8,128)} %broadcast_in_dim.11), calls=%async_computation.3 | async-start | bytes 262144 | tf_op jit(solution)/shard_map/probe_sum/all_to_all | solution.py:261

commit v4 on v3

--- a/solution.py
+++ b/solution.py
@@ -60,11 +60,11 @@
     return lax.broadcasted_iota(jnp.int32, (N, N), 1) < H
 
 
-def pack_columns(x, to_left, to_right, k, c):
+def pack_columns(x):
     low = lax.broadcasted_iota(jnp.int32, (H, N), 1) < H
     upper, lower = x[:H], x[H:]
-    to_right[k, c] = jnp.where(low, pltpu.roll(upper, H, 1), lower)
-    to_left[k, c] = jnp.where(low, upper, pltpu.roll(lower, H, 1))
+    to_right = jnp.where(low, pltpu.roll(upper, H, 1), lower)
+    return jnp.where(low, upper, pltpu.roll(lower, H, 1)), to_right
 
 
 def unpack_columns(from_left, from_right):
@@ -74,20 +74,29 @@
     return jnp.concatenate([upper, lower], axis=0)
 
 
-def edges_kernel(tile, to_up, to_down, to_left, to_right):
+def even(axis):
+    return jnp.full((H, N), jnp.bitwise_and(lax.axis_index(axis), 1), jnp.int32) == 0
+
+
+def sort(is_even, before, after):
+    return jnp.where(is_even, before, after), jnp.where(is_even, after, before)
+
+
+def edges_kernel(tile, row_across, row_mate, col_across, col_mate):
+    row_even, col_even = even("x"), even("c")
     for k in range(tile.shape[0]):
         for c in range(2):
             t = tile[k, c]
-            to_up[k, c] = t[:H]
-            to_down[k, c] = t[H:]
-            pack_columns(t, to_left, to_right, k, c)
-
-
-def corners_kernel(above, below, to_left, to_right):
-    for k in range(above.shape[0]):
-        for c in range(2):
-            v = jnp.concatenate([above[k, c], below[k, c]], axis=0)
-            pack_columns(v, to_left, to_right, k, c)
+            row_across[k, c], row_mate[k, c] = sort(row_even, t[:H], t[H:])
+            col_across[k, c], col_mate[k, c] = sort(col_even, *pack_columns(t))
+
+
+def corners_kernel(row_across, row_mate, col_across, col_mate):
+    row_even, col_even = even("x"), even("c")
+    for k in range(row_across.shape[0]):
+        for c in range(2):
+            v = jnp.concatenate(sort(row_even, row_across[k, c], row_mate[k, c]), axis=0)
+            col_across[k, c], col_mate[k, c] = sort(col_even, *pack_columns(v))
 
 
 def turned_rows(x):
@@ -95,12 +104,12 @@
 
 
 def grad_kernel(
-    pos, count, tile, above, below, from_left, from_right, corner_left, corner_right,
+    pos, count, tile, row_across, row_mate, col_across, col_mate, corner_across, corner_mate,
     probe, measured, consts,
     own_out, vert_out, horiz_out, corner_out, probe_out, patches, waves,
 ):
     slices = tile.shape[0]
-    low = lane_mask()
+    row_even, col_even = even("x"), even("c")
     rows = lax.broadcasted_iota(jnp.int32, (N, N), 0)
     cols = lax.broadcasted_iota(jnp.int32, (N, N), 1)
     def operator(i):
@@ -125,9 +134,12 @@
 
     def candidates(k, c):
         own = pltpu.roll(turned_rows(tile[k, c]), H, 1)
-        vert = pltpu.roll(jnp.concatenate([above[k, c], below[k, c]], axis=0), H, 1)
-        horiz = turned_rows(unpack_columns(from_left[k, c], from_right[k, c]))
-        corner = unpack_columns(corner_left[k, c], corner_right[k, c])
+        vert = sort(row_even, row_across[k, c], row_mate[k, c])
+        vert = pltpu.roll(jnp.concatenate(vert, axis=0), H, 1)
+        horiz = sort(col_even, col_across[k, c], col_mate[k, c])
+        horiz = turned_rows(unpack_columns(*horiz))
+        corner = sort(col_even, corner_across[k, c], corner_mate[k, c])
+        corner = unpack_columns(*corner)
         return own, vert, horiz, corner
 
     wave = []
@@ -204,31 +216,38 @@
         probe_out[c] = total
 
 
-def sides_kernel(horiz_in, corner_in, left_out, right_out):
+def sides_kernel(horiz_in, corner_in, col_across, col_mate):
     low = lane_mask()
+    col_even = jnp.concatenate([even("c")] * 2, axis=0)
     for k in range(horiz_in.shape[0]):
         for c in range(2):
             horiz, corner = turned_rows(horiz_in[k, c]), corner_in[k, c]
-            left_out[k, c] = jnp.where(low, horiz, pltpu.roll(corner, H, 1))
-            right_out[k, c] = jnp.where(low, pltpu.roll(horiz, H, 1), corner)
-
-
-def vertical_kernel(vert, from_left, from_right, up_out, down_out):
+            to_left = jnp.where(low, horiz, pltpu.roll(corner, H, 1))
+            to_right = jnp.where(low, pltpu.roll(horiz, H, 1), corner)
+            col_across[k, c], col_mate[k, c] = sort(col_even, to_left, to_right)
+
+
+def vertical_kernel(vert, col_across, col_mate, row_across, row_mate):
     low = lane_mask()
+    row_even = even("x")
+    col_even = jnp.concatenate([even("c")] * 2, axis=0)
     for k in range(vert.shape[0]):
         for c in range(2):
-            add = jnp.where(low, pltpu.roll(from_left[k, c], H, 1), from_right[k, c])
+            from_left, from_right = sort(col_even, col_across[k, c], col_mate[k, c])
+            add = jnp.where(low, pltpu.roll(from_left, H, 1), from_right)
             v = pltpu.roll(vert[k, c], H, 1) + add
-            up_out[k, c] = v[:H]
-            down_out[k, c] = v[H:]
-
-
-def final_kernel(own, from_left, from_right, from_above, from_below, out):
+            row_across[k, c], row_mate[k, c] = sort(row_even, v[:H], v[H:])
+
+
+def final_kernel(own, col_across, col_mate, row_across, row_mate, out):
     low = lane_mask()
+    row_even = even("x")
+    col_even = jnp.concatenate([even("c")] * 2, axis=0)
     for k in range(own.shape[0]):
         for c in range(2):
-            add = jnp.where(low, from_left[k, c], pltpu.roll(from_right[k, c], H, 1))
-            v = jnp.concatenate([from_above[k, c], from_below[k, c]], axis=0)
+            from_left, from_right = sort(col_even, col_across[k, c], col_mate[k, c])
+            add = jnp.where(low, from_left, pltpu.roll(from_right, H, 1))
+            v = jnp.concatenate(sort(row_even, row_across[k, c], row_mate[k, c]), axis=0)
             out[k, c] = turned_rows(pltpu.roll(own[k, c], H, 1)) + add + v
 
 
@@ -251,10 +270,10 @@
     )(*args)
 
 
-def shift(x, axis, forward):
+def swap(across, mate, axis):
     size = lax.axis_size(axis)
-    pairs = [(i, i + 1) if forward else (i + 1, i) for i in range(size - 1)]
-    return lax.ppermute(x, axis, pairs)
+    over = [(i, i + 1 if i % 2 else i - 1) for i in range(1, size - 1)]
+    return lax.ppermute(across, axis, over), lax.ppermute(mate, axis, [(i, i ^ 1) for i in range(size)])
 
 
 def exchange(x, axis):
@@ -274,22 +293,16 @@
     half = (slices, 2, H, N)
     consts = jnp.asarray(constant_operands())
     with jax.named_scope("object_halo"):
-        to_up, to_down, to_left, to_right = call(
-            edges_kernel, [half] * 4, (object_field,), "pack_edges"
-        )
-        above = shift(to_down, ROW, True)
-        below = shift(to_up, ROW, False)
-        from_left = shift(to_right, COL, True)
-        from_right = shift(to_left, COL, False)
-        to_left, to_right = call(corners_kernel, [half] * 2, (above, below), "pack_corners")
-        corner_left = shift(to_right, COL, True)
-        corner_right = shift(to_left, COL, False)
+        edges = call(edges_kernel, [half] * 4, (object_field,), "pack_edges")
+        rows = swap(*edges[:2], ROW)
+        cols = swap(*edges[2:], COL)
+        corners = swap(*call(corners_kernel, [half] * 2, rows, "pack_corners"), COL)
     own, vert, horiz, corner, probe_sum = call(
         grad_kernel,
         [full, full, full, full, (2, N, N)],
         (
-            positions, counts, object_field, above, below, from_left, from_right,
-            corner_left, corner_right, probe_wave, measured[0, 0], consts,
+            positions, counts, object_field, *rows, *cols, *corners,
+            probe_wave, measured[0, 0], consts,
         ),
         "slot_gradients",
         scalars=2,
@@ -298,17 +311,9 @@
         scratch=[pltpu.VMEM((slices, 2, 2, N, N), jnp.float32) for _ in range(2)],
     )
     with jax.named_scope("gradient_halo"):
-        left, right = call(sides_kernel, [full] * 2, (horiz, corner), "pack_sides")
-        got_right = shift(left, COL, False)
-        got_left = shift(right, COL, True)
-        up, down = call(
-            vertical_kernel, [half, half], (vert, got_left, got_right), "add_vertical"
-        )
-        got_below = shift(up, ROW, False)
-        got_above = shift(down, ROW, True)
-        (result,) = call(
-            final_kernel, [full], (own, got_left, got_right, got_above, got_below), "add_own"
-        )
+        cols = swap(*call(sides_kernel, [full] * 2, (horiz, corner), "pack_sides"), COL)
+        rows = swap(*call(vertical_kernel, [half] * 2, (vert, *cols), "add_vertical"), ROW)
+        (result,) = call(final_kernel, [full], (own, *cols, *rows), "add_own")
     with jax.named_scope("probe_sum"):
         near = ("x", "c")
         groups = lax.axis_size(near)

time: 104 us -> 98.7 us (0.949)
  blocking collectives: 11.3 us -> 8.47 us
  waiting for transfers between devices: 14.4 us -> 12.4 us
    all_to_all x1, blocking collectives: 11.3 us -> 8.47 us  [exchange(): return lax.all_to_all(x, axis, 0, 0, tiled=True)]
    ppermute x10, waiting for transfers between devices: 2.18 us -> 0.89 us  [the longest x5 0.88 us: swap(): lax.ppermute(across, axis, over)]
where the time goes in v4:
time: 98.7 us; the launch traced here: 98 us
  starting transfers between devices  63.1 us (64%)
  waiting for transfers between devices  12.4 us (13%)
  Pallas kernels  8.68 us (9%)
  blocking collectives  8.47 us (9%)
  local copies, waits for them, and re-layouts  3.75 us (4%)
  between operations  1.53 us (2%)
    all_to_all x3, starting transfers between devices, exchange(): return lax.all_to_all(x, axis, 0, 0, tiled=True)  30.3 us
    ppermute x5, starting transfers between devices, swap(): lax.ppermute(mate, axis, [(i, i ^ 1) for i in range(size)])  20.5 us
    ppermute x5, starting transfers between devices, swap(): lax.ppermute(across, axis, over)  12.3 us
    all_to_all x3, waiting for transfers between devices, exchange(): return lax.all_to_all(x, axis, 0, 0, tiled=True)  11.5 us
    pallas_call x6, Pallas kernels, call(): pl.pallas_call(kernel, out_shape=[jax.ShapeDtypeStruct(s, jnp.float32) fo...  8.68 us
    all_to_all x1, blocking collectives, exchange(): return lax.all_to_all(x, axis, 0, 0, tiled=True)  8.47 us
  transfers between devices with their start and end apart: 13, of which 4 were waited for; matrix products, arithmetic and copies ran while one was open for 1% of the time, Pallas kernels for 2%

profile of v4, /device:TPU:1, one launch (start us, length us, event | category | flops | bytes accessed | tf_op | source)
XLA Modules:
  0.0 98.0 jit_solution(150053999538682066)
XLA Ops:
  0.6 0.0 copy-start
  0.6 1.0 %copy-done = f32[4,2,128,128]{3,2,1,0:T(8,128)S(1)} copy-done((f32[4,2,128,128]{3,2,1,0:T(8,128)S(1)}, f32[4,2,128,128]{3,2,1,0:T(8,128)}, u32[]{:S(2)}) %copy-start) | copy-done | bytes 524312
  1.7 0.2 pack_edges.1
  1.9 0.7 collective-permute-start
  2.6 6.4 %collective-permute-start.1 = (f32[4,2,64,128]{3,2,1,0:T(8,128)S(1)}, f32[4,2,64,128]{3,2,1,0:T(8,128)S(1)}, u32[]{:S(2)}, u32[]{:S(2)}) collective-permute-start(f32[4,2,64,128]{3,2,1,0:T(8,128)S(1)} %get-tuple-element.18), channel_id=1, source_target_pairs={{0,16},{16,0},{32,48},{48,32},{64,80},{80,64},{96,112},{112,96},{1... | collective-permute-start | bytes 786440 | tf_op jit(solution)/shard_map/object_halo/ppermute | solution.py:276
  9.0 4.3 %collective-permute-start.2 = (f32[4,2,64,128]{3,2,1,0:T(8,128)S(1)}, f32[4,2,64,128]{3,2,1,0:T(8,128)S(1)}, u32[]{:S(2)}, u32[]{:S(2)}) collective-permute-start(f32[4,2,64,128]{3,2,1,0:T(8,128)S(1)} %get-tuple-element.19), channel_id=1, source_target_pairs={{1,2},{2,1},{3,4},{4,3},{5,6},{6,5},{7,8},{8,7},{9,10},{10,9},{11,... | collective-permute-start | bytes 786440 | tf_op jit(solution)/shard_map/object_halo/ppermute | solution.py:276
  13.3 0.0 copy-start.2
  13.3 0.0 copy-start.3
  13.3 0.0 copy-start.5
  13.3 4.4 %collective-permute-start.3 = (f32[4,2,64,128]{3,2,1,0:T(8,128)S(1)}, f32[4,2,64,128]{3,2,1,0:T(8,128)S(1)}, u32[]{:S(2)}, u32[]{:S(2)}) collective-permute-start(f32[4,2,64,128]{3,2,1,0:T(8,128)S(1)} %get-tuple-element.20), channel_id=1, source_target_pairs={{0,1},{1,0},{2,3},{3,2},{4,5},{5,4},{6,7},{7,6},{8,9},{9,8},{10,11... | collective-permute-start | bytes 786440 | tf_op jit(solution)/shard_map/object_halo/ppermute | solution.py:276
  17.8 0.0 collective-permute-done.row_across
  17.8 0.0 collective-permute-done.1.row_mate
  17.8 0.2 pack_corners.1
  18.0 1.9 %collective-permute-start.4 = (f32[4,2,64,128]{3,2,1,0:T(8,128)S(1)}, f32[4,2,64,128]{3,2,1,0:T(8,128)S(1)}, u32[]{:S(2)}, u32[]{:S(2)}) collective-permute-start(f32[4,2,64,128]{3,2,1,0:T(8,128)S(1)} %get-tuple-element.21), channel_id=1, source_target_pairs={{1,2},{2,1},{3,4},{4,3},{5,6},{6,5},{7,8},{8,7},{9,10},{10,9},{11,... | collective-permute-start | bytes 786440 | tf_op jit(solution)/shard_map/object_halo/ppermute | solution.py:276
  20.0 4.2 %collective-permute-start.5 = (f32[4,2,64,128]{3,2,1,0:T(8,128)S(1)}, f32[4,2,64,128]{3,2,1,0:T(8,128)S(1)}, u32[]{:S(2)}, u32[]{:S(2)}) collective-permute-start(f32[4,2,64,128]{3,2,1,0:T(8,128)S(1)} %get-tuple-element.22), channel_id=1, source_target_pairs={{0,1},{1,0},{2,3},{3,2},{4,5},{5,4},{6,7},{7,6},{8,9},{9,8},{10,11... | collective-permute-start | bytes 786440 | tf_op jit(solution)/shard_map/object_halo/ppermute | solution.py:276
  24.8 0.0 copy-start.4
  24.8 0.0 collective-permute-done.2.col_across
  24.8 0.0 collective-permute-done.3.col_mate
  24.9 0.9 collective-permute-done.4.corner_across
  25.7 0.0 collective-permute-done.5.corner_mate
  25.7 0.0 copy-done.1
  25.7 0.0 copy-done.2
  25.7 0.0 copy-done.3
  25.7 0.0 copy-done.5
  25.8 0.0 copy-done.4
  25.8 6.4 %slot_gradients.1 = (f32[4,2,128,128]{3,2,1,0:T(8,128)S(1)}, f32[4,2,128,128]{3,2,1,0:T(8,128)S(1)}, f32[4,2,128,128]{3,2,1,0:T(8,128)S(1)}, f32[4,2,128,128]{3,2,1,0:T(8,128)S(1)}, f32[2,128,128]{2,1,0:T(8,128)S(1)}) custom-call(s32[1,1,2,2]{3,2,1,0:T(2,128)S(1)} %copy-done.4, s32[1,1]{1,0:T(1,128)S(6)} %copy.9.count, f32[4,2,128,128]{3,2,1,0:T(8,128)S(1)} %copy-done.1, ...), custom_call_target="tpu_custom_call" | custom-call | flops 1610612736 | bytes 4849684 | tf_op jit(solution)/shard_map/slot_gradients/pallas_call | solution.py:257
  32.2 8.5 %all_to_all.27 = f32[8,32,128]{2,1,0:T(8,128)S(1)} all-to-all(f32[8,32,128]{2,1,0:T(8,128)S(1)} %bitcast.3), channel_id=1, replica_groups=mesh['z'=12,'x'=4,'y'=8,'c'=2] {'x','c'}, dimensions={0} | all-to-all | bytes 262144 | tf_op jit(solution)/shard_map/probe_sum/all_to_all | solution.py:280
  40.7 0.7 broadcast_in_dim.9
  41.4 8.1 %all-to-all-start.1 = ((f32[8,32,128]{2,1,0:T(8,128)}), f32[8,32,128]{2,1,0:T(8,128)S(1)}, u32[]{:S(2)}, u32[]{:S(2)}) async-start(f32[8,32,128]{2,1,0:T(8,128)} %broadcast_in_dim.9), calls=%async_computation.1 | async-start | bytes 262144 | tf_op jit(solution)/shard_map/probe_sum/all_to_all | solution.py:280
  49.5 0.3 pack_sides.1
  49.8 4.7 %collective-permute-start.6 = (f32[4,2,128,128]{3,2,1,0:T(8,128)S(1)}, f32[4,2,128,128]{3,2,1,0:T(8,128)S(1)}, u32[]{:S(2)}, u32[]{:S(2)}) collective-permute-start(f32[4,2,128,128]{3,2,1,0:T(8,128)S(1)} %get-tuple-element.26), channel_id=1, source_target_pairs={{1,2},{2,1},{3,4},{4,3},{5,6},{6,5},{7,8},{8,7},{9,10},{10,9},{11,... | collective-permute-start | bytes 1572872 | tf_op jit(solution)/shard_map/gradient_halo/ppermute | solution.py:276
  54.5 1.9 %collective-permute-start.7 = (f32[4,2,128,128]{3,2,1,0:T(8,128)S(1)}, f32[4,2,128,128]{3,2,1,0:T(8,128)S(1)}, u32[]{:S(2)}, u32[]{:S(2)}) collective-permute-start(f32[4,2,128,128]{3,2,1,0:T(8,128)S(1)} %get-tuple-element.27), channel_id=1, source_target_pairs={{0,1},{1,0},{2,3},{3,2},{4,5},{5,4},{6,7},{7,6},{8,9},{9,8},{10,11... | collective-permute-start | bytes 1572872 | tf_op jit(solution)/shard_map/gradient_halo/ppermute | solution.py:276
  56.4 0.9 all-to-all-done.1
  57.3 0.7 broadcast_in_dim.10
  58.0 14.3 %all-to-all-start.2 = ((f32[12,32,128]{2,1,0:T(8,128)}), f32[12,32,128]{2,1,0:T(8,128)S(1)}, u32[]{:S(2)}, u32[]{:S(2)}) async-start(f32[12,32,128]{2,1,0:T(8,128)} %broadcast_in_dim.10), calls=%async_computation.2 | async-start | bytes 393216 | tf_op jit(solution)/shard_map/probe_sum/all_to_all | solution.py:280
  72.3 0.0 collective-permute-done.6.col_across
  72.3 0.0 collective-permute-done.7.col_mate
  72.3 0.3 add_vertical.1
  72.7 0.7 collective-permute-start.8
  73.4 3.5 %collective-permute-start.9 = (f32[4,2,64,128]{3,2,1,0:T(8,128)S(1)}, f32[4,2,64,128]{3,2,1,0:T(8,128)S(1)}, u32[]{:S(2)}, u32[]{:S(2)}) collective-permute-start(f32[4,2,64,128]{3,2,1,0:T(8,128)S(1)} %get-tuple-element.30), channel_id=1, source_target_pairs={{0,16},{16,0},{32,48},{48,32},{64,80},{80,64},{96,112},{112,96},{1... | collective-permute-start | bytes 786440 | tf_op jit(solution)/shard_map/gradient_halo/ppermute | solution.py:276
  76.9 6.5 %all-to-all-done.2 = f32[12,32,128]{2,1,0:T(8,128)S(1)} async-done(((f32[12,32,128]{2,1,0:T(8,128)}), f32[12,32,128]{2,1,0:T(8,128)S(1)}, u32[]{:S(2)}, u32[]{:S(2)}) %all-to-all-start.2) | async-done | bytes 196640 | tf_op jit(solution)/shard_map/probe_sum/all_to_all | solution.py:280
  83.4 0.7 broadcast_in_dim.11
  84.1 8.0 %all-to-all-start.3 = ((f32[8,32,128]{2,1,0:T(8,128)}), f32[8,32,128]{2,1,0:T(8,128)S(1)}, u32[]{:S(2)}, u32[]{:S(2)}) async-start(f32[8,32,128]{2,1,0:T(8,128)} %broadcast_in_dim.11), calls=%async_computation.3 | async-start | bytes 262144 | tf_op jit(solution)/shard_map/probe_sum/all_to_all | solution.py:280
  92.0 0.0 collective-permute-done.8.row_across
  92.0 0.0 collective-permute-done.9.row_mate
  92.0 1.1 %add_own.1 = f32[4,2,128,128]{3,2,1,0:T(8,128)} custom-call(f32[4,2,128,128]{3,2,1,0:T(8,128)S(1)} %get-tuple-element.23.own, f32[4,2,128,128]{3,2,1,0:T(8,128)S(1)} %collective-permute-done.6.col_across, f32[4,2,128,128]{3,2,1,0:T(8,128)S(1)} %collective-permute-done.7.col_mate, f32[4,2,64,128]{3,2,1,0:T(8,128)S(1)} %collective-permute-done.8.row_across, ...), custom_call_target="tpu_custom_call" | custom-call | bytes 2621440 | tf_op jit(solution)/shard_map/gradient_halo/add_own/pallas_call | solution.py:257
  93.2 4.1 %all-to-all-done.3 = f32[8,32,128]{2,1,0:T(8,128)S(1)} async-done(((f32[8,32,128]{2,1,0:T(8,128)}), f32[8,32,128]{2,1,0:T(8,128)S(1)}, u32[]{:S(2)}, u32[]{:S(2)}) %all-to-all-start.3) | async-done | bytes 131104 | tf_op jit(solution)/shard_map/probe_sum/all_to_all | solution.py:280
  97.3 0.7 copy.10
  (4 shorter events, 0.0 us)
Async XLA Ops:
  0.6 1.0 %copy-start = (f32[4,2,128,128]{3,2,1,0:T(8,128)S(1)}, f32[4,2,128,128]{3,2,1,0:T(8,128)}, u32[]{:S(2)}) copy-start(f32[4,2,128,128]{3,2,1,0:T(8,128)} %tile.3) | copy-start | bytes 1572868
  1.7 24.1 %copy-start.1 = (f32[4,2,128,128]{3,2,1,0:T(8,128)S(1)}, f32[4,2,128,128]{3,2,1,0:T(8,128)}, u32[]{:S(2)}) copy-start(f32[4,2,128,128]{3,2,1,0:T(8,128)} %tile.3) | copy-start | bytes 1572868
  1.9 15.9 %collective-permute-start = (f32[4,2,64,128]{3,2,1,0:T(8,128)S(1)}, f32[4,2,64,128]{3,2,1,0:T(8,128)S(1)}, u32[]{:S(2)}, u32[]{:S(2)}) collective-permute-start(f32[4,2,64,128]{3,2,1,0:T(8,128)S(1)} %get-tuple-element.17), channel_id=1, source_target_pairs={{16,32},{32,16},{48,64},{64,48},{80,96},{96,80},{112,128},{128,112... | collective-permute-start | bytes 786440 | tf_op jit(solution)/shard_map/object_halo/ppermute | solution.py:276
  2.6 15.2 %collective-permute-start.1 = (f32[4,2,64,128]{3,2,1,0:T(8,128)S(1)}, f32[4,2,64,128]{3,2,1,0:T(8,128)S(1)}, u32[]{:S(2)}, u32[]{:S(2)}) collective-permute-start(f32[4,2,64,128]{3,2,1,0:T(8,128)S(1)} %get-tuple-element.18), channel_id=1, source_target_pairs={{0,16},{16,0},{32,48},{48,32},{64,80},{80,64},{96,112},{112,96},{1... | collective-permute-start | bytes 786440 | tf_op jit(solution)/shard_map/object_halo/ppermute | solution.py:276
  9.0 15.9 %collective-permute-start.2 = (f32[4,2,64,128]{3,2,1,0:T(8,128)S(1)}, f32[4,2,64,128]{3,2,1,0:T(8,128)S(1)}, u32[]{:S(2)}, u32[]{:S(2)}) collective-permute-start(f32[4,2,64,128]{3,2,1,0:T(8,128)S(1)} %get-tuple-element.19), channel_id=1, source_target_pairs={{1,2},{2,1},{3,4},{4,3},{5,6},{6,5},{7,8},{8,7},{9,10},{10,9},{11,... | collective-permute-start | bytes 786440 | tf_op jit(solution)/shard_map/object_halo/ppermute | solution.py:276
  13.3 12.4 %copy-start.2 = (f32[2,128,128]{2,1,0:T(8,128)S(1)}, f32[2,128,128]{2,1,0:T(8,128)}, u32[]{:S(2)}) copy-start(f32[2,128,128]{2,1,0:T(8,128)} %probe.1) | copy-start | bytes 393220
  13.3 12.4 %copy-start.3 = (f32[1,1,2,128,128]{4,3,2,1,0:T(8,128)S(1)}, f32[1,1,2,128,128]{4,3,2,1,0:T(8,128)}, u32[]{:S(2)}) copy-start(f32[1,1,2,128,128]{4,3,2,1,0:T(8,128)} %param.10) | copy-start | bytes 393220
  13.3 12.4 %copy-start.5 = (bf16[8,128,128]{2,1,0:T(8,128)(2,1)S(1)}, bf16[8,128,128]{2,1,0:T(8,128)(2,1)}, u32[]{:S(2)}) copy-start(bf16[8,128,128]{2,1,0:T(8,128)(2,1)} %constant.4.clone.consts) | copy-start | bytes 786436
  13.3 11.5 %collective-permute-start.3 = (f32[4,2,64,128]{3,2,1,0:T(8,128)S(1)}, f32[4,2,64,128]{3,2,1,0:T(8,128)S(1)}, u32[]{:S(2)}, u32[]{:S(2)}) collective-permute-start(f32[4,2,64,128]{3,2,1,0:T(8,128)S(1)} %get-tuple-element.20), channel_id=1, source_target_pairs={{0,1},{1,0},{2,3},{3,2},{4,5},{5,4},{6,7},{7,6},{8,9},{9,8},{10,11... | collective-permute-start | bytes 786440 | tf_op jit(solution)/shard_map/object_halo/ppermute | solution.py:276
  18.0 7.7 %collective-permute-start.4 = (f32[4,2,64,128]{3,2,1,0:T(8,128)S(1)}, f32[4,2,64,128]{3,2,1,0:T(8,128)S(1)}, u32[]{:S(2)}, u32[]{:S(2)}) collective-permute-start(f32[4,2,64,128]{3,2,1,0:T(8,128)S(1)} %get-tuple-element.21), channel_id=1, source_target_pairs={{1,2},{2,1},{3,4},{4,3},{5,6},{6,5},{7,8},{8,7},{9,10},{10,9},{11,... | collective-permute-start | bytes 786440 | tf_op jit(solution)/shard_map/object_halo/ppermute | solution.py:276
  20.0 5.8 %collective-permute-start.5 = (f32[4,2,64,128]{3,2,1,0:T(8,128)S(1)}, f32[4,2,64,128]{3,2,1,0:T(8,128)S(1)}, u32[]{:S(2)}, u32[]{:S(2)}) collective-permute-start(f32[4,2,64,128]{3,2,1,0:T(8,128)S(1)} %get-tuple-element.22), channel_id=1, source_target_pairs={{0,1},{1,0},{2,3},{3,2},{4,5},{5,4},{6,7},{7,6},{8,9},{9,8},{10,11... | collective-permute-start | bytes 786440 | tf_op jit(solution)/shard_map/object_halo/ppermute | solution.py:276
  24.8 0.9 copy-start.4
  41.4 16.0 %all-to-all-start.1 = ((f32[8,32,128]{2,1,0:T(8,128)}), f32[8,32,128]{2,1,0:T(8,128)S(1)}, u32[]{:S(2)}, u32[]{:S(2)}) async-start(f32[8,32,128]{2,1,0:T(8,128)} %broadcast_in_dim.9), calls=%async_computation.1 | async-start | bytes 262144 | tf_op jit(solution)/shard_map/probe_sum/all_to_all | solution.py:280
  49.8 22.5 %collective-permute-start.6 = (f32[4,2,128,128]{3,2,1,0:T(8,128)S(1)}, f32[4,2,128,128]{3,2,1,0:T(8,128)S(1)}, u32[]{:S(2)}, u32[]{:S(2)}) collective-permute-start(f32[4,2,128,128]{3,2,1,0:T(8,128)S(1)} %get-tuple-element.26), channel_id=1, source_target_pairs={{1,2},{2,1},{3,4},{4,3},{5,6},{6,5},{7,8},{8,7},{9,10},{10,9},{11,... | collective-permute-start | bytes 1572872 | tf_op jit(solution)/shard_map/gradient_halo/ppermute | solution.py:276
  54.5 17.8 %collective-permute-start.7 = (f32[4,2,128,128]{3,2,1,0:T(8,128)S(1)}, f32[4,2,128,128]{3,2,1,0:T(8,128)S(1)}, u32[]{:S(2)}, u32[]{:S(2)}) collective-permute-start(f32[4,2,128,128]{3,2,1,0:T(8,128)S(1)} %get-tuple-element.27), channel_id=1, source_target_pairs={{0,1},{1,0},{2,3},{3,2},{4,5},{5,4},{6,7},{7,6},{8,9},{9,8},{10,11... | collective-permute-start | bytes 1572872 | tf_op jit(solution)/shard_map/gradient_halo/ppermute | solution.py:276
  58.0 25.3 %all-to-all-start.2 = ((f32[12,32,128]{2,1,0:T(8,128)}), f32[12,32,128]{2,1,0:T(8,128)S(1)}, u32[]{:S(2)}, u32[]{:S(2)}) async-start(f32[12,32,128]{2,1,0:T(8,128)} %broadcast_in_dim.10), calls=%async_computation.2 | async-start | bytes 393216 | tf_op jit(solution)/shard_map/probe_sum/all_to_all | solution.py:280
  72.7 19.3 %collective-permute-start.8 = (f32[4,2,64,128]{3,2,1,0:T(8,128)S(1)}, f32[4,2,64,128]{3,2,1,0:T(8,128)S(1)}, u32[]{:S(2)}, u32[]{:S(2)}) collective-permute-start(f32[4,2,64,128]{3,2,1,0:T(8,128)S(1)} %get-tuple-element.29), channel_id=1, source_target_pairs={{16,32},{32,16},{48,64},{64,48},{80,96},{96,80},{112,128},{128,112... | collective-permute-start | bytes 786440 | tf_op jit(solution)/shard_map/gradient_halo/ppermute | solution.py:276
  73.4 18.7 %collective-permute-start.9 = (f32[4,2,64,128]{3,2,1,0:T(8,128)S(1)}, f32[4,2,64,128]{3,2,1,0:T(8,128)S(1)}, u32[]{:S(2)}, u32[]{:S(2)}) collective-permute-start(f32[4,2,64,128]{3,2,1,0:T(8,128)S(1)} %get-tuple-element.30), channel_id=1, source_target_pairs={{0,16},{16,0},{32,48},{48,32},{64,80},{80,64},{96,112},{112,96},{1... | collective-permute-start | bytes 786440 | tf_op jit(solution)/shard_map/gradient_halo/ppermute | solution.py:276
  84.1 13.2 %all-to-all-start.3 = ((f32[8,32,128]{2,1,0:T(8,128)}), f32[8,32,128]{2,1,0:T(8,128)S(1)}, u32[]{:S(2)}, u32[]{:S(2)}) async-start(f32[8,32,128]{2,1,0:T(8,128)} %broadcast_in_dim.11), calls=%async_computation.3 | async-start | bytes 262144 | tf_op jit(solution)/shard_map/probe_sum/all_to_all | solution.py:280

commit v5 on v4

--- a/solution.py
+++ b/solution.py
@@ -280,11 +280,19 @@
     return lax.all_to_all(x, axis, 0, 0, tiled=True)
 
 
-def gathered_sum(x, axis):
-    n = lax.axis_size(axis)
-    rows = x.shape[0]
-    parts = exchange(jnp.broadcast_to(x, (n, *x.shape)).reshape(n * rows, N), axis)
-    return parts.reshape(n, rows, N).sum(axis=0)
+def sum_kernel(parts, out):
+    total = parts[0]
+    for i in range(1, parts.shape[0]):
+        total += parts[i]
+    for i in range(out.shape[0]):
+        out[i] = total
+
+
+def summed(parts, groups, copies):
+    rows = parts.shape[0] // groups
+    args = (parts.reshape(groups, rows, N),)
+    (out,) = call(sum_kernel, [(copies, rows, N)], args, "sum_parts", flops=20 * 10**9)
+    return out.reshape(copies * rows, N)
 
 
 def per_device(object_field, probe_wave, positions, counts, measured):
@@ -310,19 +318,19 @@
         flops=16 * 6 * (2 * N) ** 3,
         scratch=[pltpu.VMEM((slices, 2, 2, N, N), jnp.float32) for _ in range(2)],
     )
-    with jax.named_scope("gradient_halo"):
+    plane, across_planes = ("x", "y"), ("z", "c")
+    groups, copies = lax.axis_size(plane), lax.axis_size(across_planes)
+    with jax.named_scope("probe_sum_plane"):
+        parts = exchange(probe_sum.reshape(2 * N, N), plane)
+    with jax.named_scope("gradient_columns"):
         cols = swap(*call(sides_kernel, [full] * 2, (horiz, corner), "pack_sides"), COL)
+    with jax.named_scope("probe_sum_z"):
+        parts = exchange(summed(parts, groups, copies), across_planes)
+    with jax.named_scope("gradient_rows"):
         rows = swap(*call(vertical_kernel, [half] * 2, (vert, *cols), "add_vertical"), ROW)
         (result,) = call(final_kernel, [full], (own, *cols, *rows), "add_own")
-    with jax.named_scope("probe_sum"):
-        near = ("x", "c")
-        groups = lax.axis_size(near)
-        part = exchange(probe_sum.reshape(2 * N, N), near)
-        part = part.reshape(groups, 2 * N // groups, N).sum(axis=0)
-        part = gathered_sum(part, "y")
-        part = gathered_sum(part, "z")
-        spread = jnp.broadcast_to(part, (groups, *part.shape)).reshape(2 * N, N)
-        probe_grad = exchange(spread, near).reshape(2, N, N)
+    with jax.named_scope("probe_sum_gather"):
+        probe_grad = exchange(summed(parts, copies, groups), plane).reshape(2, N, N)
     return (result, probe_grad)
 
 

time: 98.7 us -> 95.4 us (0.967)
  blocking collectives: 8.47 us -> 0 us
  waiting for transfers between devices: 12.4 us -> 16.2 us
  local copies, waits for them, and re-layouts: 3.75 us -> 1.72 us
  Pallas kernels: 8.68 us -> 10.7 us
  starting transfers between devices: 63.1 us -> 64.2 us
    all_to_all x1 -> x0, blocking collectives: 8.47 us -> none  [exchange(): return lax.all_to_all(x, axis, 0, 0, tiled=True)]
    all_to_all x3, waiting for transfers between devices: 11.5 us -> 15.3 us  [exchange(): return lax.all_to_all(x, axis, 0, 0, tiled=True)]
    pallas_call x6 -> x8, Pallas kernels: 8.68 us -> 10.7 us  [call(): pl.pallas_call(kernel, out_shape=[jax.ShapeDtypeStruct(s, jnp.float32) fo...]
    broadcast_in_dim x3 -> x0, local copies, waits for them, and re-layouts: 2.03 us -> none  [the longest x2 1.36 us: gathered_sum(): jnp.broadcast_to(x, (n, *x.shape)).reshape(n * rows, N)]
  transfers between devices with their start and end apart: 13 -> 13, of which waited for: 4 -> 4; matrix products, arithmetic and copies ran while one was open for 1% -> 0% of each run, Pallas kernels for 2% -> 4%
where the time goes in v5:
time: 95.4 us; the launch traced here: 94.4 us
  starting transfers between devices  64.2 us (67%)
  waiting for transfers between devices  16.2 us (17%)
  Pallas kernels  10.7 us (11%)
  local copies, waits for them, and re-layouts  1.72 us (2%)
  between operations  1.54 us (2%)
    all_to_all x3, starting transfers between devices, exchange(): return lax.all_to_all(x, axis, 0, 0, tiled=True)  30.1 us
    ppermute x5, starting transfers between devices, swap(): lax.ppermute(mate, axis, [(i, i ^ 1) for i in range(size)])  20.8 us
    all_to_all x3, waiting for transfers between devices, exchange(): return lax.all_to_all(x, axis, 0, 0, tiled=True)  15.3 us
    ppermute x5, starting transfers between devices, swap(): lax.ppermute(across, axis, over)  13.3 us
    pallas_call x8, Pallas kernels, call(): pl.pallas_call(kernel, out_shape=[jax.ShapeDtypeStruct(s, jnp.float32) fo...  10.7 us
  transfers between devices with their start and end apart: 13, of which 4 were waited for; matrix products, arithmetic and copies ran while one was open for 0% of the time, Pallas kernels for 4%

profile of v5, /device:TPU:1, one launch (start us, length us, event | category | flops | bytes accessed | tf_op | source)
XLA Modules:
  0.0 94.4 jit_solution(14142712730321387999)
XLA Ops:
  0.6 0.0 copy-start
  0.6 1.0 %copy-done = f32[4,2,128,128]{3,2,1,0:T(8,128)S(1)} copy-done((f32[4,2,128,128]{3,2,1,0:T(8,128)S(1)}, f32[4,2,128,128]{3,2,1,0:T(8,128)}, u32[]{:S(2)}) %copy-start) | copy-done | bytes 524312
  1.7 0.0 copy-start.1
  1.7 0.2 pack_edges.1
  1.9 0.7 collective-permute-start
  2.6 6.4 %collective-permute-start.1 = (f32[4,2,64,128]{3,2,1,0:T(8,128)S(1)}, f32[4,2,64,128]{3,2,1,0:T(8,128)S(1)}, u32[]{:S(2)}, u32[]{:S(2)}) collective-permute-start(f32[4,2,64,128]{3,2,1,0:T(8,128)S(1)} %get-tuple-element.18), channel_id=1, source_target_pairs={{0,16},{16,0},{32,48},{48,32},{64,80},{80,64},{96,112},{112,96},{1... | collective-permute-start | bytes 786440 | tf_op jit(solution)/shard_map/object_halo/ppermute | solution.py:276
  9.0 4.3 %collective-permute-start.2 = (f32[4,2,64,128]{3,2,1,0:T(8,128)S(1)}, f32[4,2,64,128]{3,2,1,0:T(8,128)S(1)}, u32[]{:S(2)}, u32[]{:S(2)}) collective-permute-start(f32[4,2,64,128]{3,2,1,0:T(8,128)S(1)} %get-tuple-element.19), channel_id=1, source_target_pairs={{1,2},{2,1},{3,4},{4,3},{5,6},{6,5},{7,8},{8,7},{9,10},{10,9},{11,... | collective-permute-start | bytes 786440 | tf_op jit(solution)/shard_map/object_halo/ppermute | solution.py:276
  13.3 0.0 copy-start.2
  13.3 0.0 copy-start.3
  13.3 0.0 copy-start.5
  13.3 4.4 %collective-permute-start.3 = (f32[4,2,64,128]{3,2,1,0:T(8,128)S(1)}, f32[4,2,64,128]{3,2,1,0:T(8,128)S(1)}, u32[]{:S(2)}, u32[]{:S(2)}) collective-permute-start(f32[4,2,64,128]{3,2,1,0:T(8,128)S(1)} %get-tuple-element.20), channel_id=1, source_target_pairs={{0,1},{1,0},{2,3},{3,2},{4,5},{5,4},{6,7},{7,6},{8,9},{9,8},{10,11... | collective-permute-start | bytes 786440 | tf_op jit(solution)/shard_map/object_halo/ppermute | solution.py:276
  17.8 0.0 collective-permute-done.row_across
  17.8 0.0 collective-permute-done.1.row_mate
  17.8 0.2 pack_corners.1
  18.0 1.9 %collective-permute-start.4 = (f32[4,2,64,128]{3,2,1,0:T(8,128)S(1)}, f32[4,2,64,128]{3,2,1,0:T(8,128)S(1)}, u32[]{:S(2)}, u32[]{:S(2)}) collective-permute-start(f32[4,2,64,128]{3,2,1,0:T(8,128)S(1)} %get-tuple-element.21), channel_id=1, source_target_pairs={{1,2},{2,1},{3,4},{4,3},{5,6},{6,5},{7,8},{8,7},{9,10},{10,9},{11,... | collective-permute-start | bytes 786440 | tf_op jit(solution)/shard_map/object_halo/ppermute | solution.py:276
  20.0 4.2 %collective-permute-start.5 = (f32[4,2,64,128]{3,2,1,0:T(8,128)S(1)}, f32[4,2,64,128]{3,2,1,0:T(8,128)S(1)}, u32[]{:S(2)}, u32[]{:S(2)}) collective-permute-start(f32[4,2,64,128]{3,2,1,0:T(8,128)S(1)} %get-tuple-element.22), channel_id=1, source_target_pairs={{0,1},{1,0},{2,3},{3,2},{4,5},{5,4},{6,7},{7,6},{8,9},{9,8},{10,11... | collective-permute-start | bytes 786440 | tf_op jit(solution)/shard_map/object_halo/ppermute | solution.py:276
  24.8 0.0 copy-start.4
  24.8 0.0 collective-permute-done.2.col_across
  24.8 0.0 collective-permute-done.3.col_mate
  24.9 0.9 collective-permute-done.4.corner_across
  25.7 0.0 collective-permute-done.5.corner_mate
  25.7 0.0 copy-done.1
  25.7 0.0 copy-done.2
  25.7 0.0 copy-done.3
  25.7 0.0 copy-done.5
  25.8 0.0 copy-done.4
  25.8 7.1 %slot_gradients.1 = (f32[4,2,128,128]{3,2,1,0:T(8,128)S(1)}, f32[4,2,128,128]{3,2,1,0:T(8,128)S(1)}, f32[4,2,128,128]{3,2,1,0:T(8,128)S(1)}, f32[4,2,128,128]{3,2,1,0:T(8,128)S(1)}, f32[2,128,128]{2,1,0:T(8,128)}) custom-call(s32[1,1,2,2]{3,2,1,0:T(2,128)S(1)} %copy-done.4, s32[1,1]{1,0:T(1,128)S(6)} %copy.9.count, f32[4,2,128,128]{3,2,1,0:T(8,128)S(1)} %copy-done.1, ...), custom_call_target="tpu_custom_call" | custom-call | flops 1610612736 | bytes 4849684 | tf_op jit(solution)/shard_map/slot_gradients/pallas_call | solution.py:257
  32.9 8.0 %all-to-all-start = ((f32[32,8,128]{2,1,0:T(8,128)}), f32[32,8,128]{2,1,0:T(8,128)S(1)}, u32[]{:S(2)}, u32[]{:S(2)}) async-start(f32[32,8,128]{2,1,0:T(8,128)} %bitcast.1), calls=%async_computation | async-start | bytes 262144 | tf_op jit(solution)/shard_map/probe_sum_plane/all_to_all | solution.py:280
  40.9 0.3 pack_sides.1
  41.2 5.7 %collective-permute-start.6 = (f32[4,2,128,128]{3,2,1,0:T(8,128)S(1)}, f32[4,2,128,128]{3,2,1,0:T(8,128)S(1)}, u32[]{:S(2)}, u32[]{:S(2)}) collective-permute-start(f32[4,2,128,128]{3,2,1,0:T(8,128)S(1)} %get-tuple-element.26), channel_id=1, source_target_pairs={{1,2},{2,1},{3,4},{4,3},{5,6},{6,5},{7,8},{8,7},{9,10},{10,9},{11,... | collective-permute-start | bytes 1572872 | tf_op jit(solution)/shard_map/gradient_columns/ppermute | solution.py:276
  46.9 1.9 %collective-permute-start.7 = (f32[4,2,128,128]{3,2,1,0:T(8,128)S(1)}, f32[4,2,128,128]{3,2,1,0:T(8,128)S(1)}, u32[]{:S(2)}, u32[]{:S(2)}) collective-permute-start(f32[4,2,128,128]{3,2,1,0:T(8,128)S(1)} %get-tuple-element.27), channel_id=1, source_target_pairs={{0,1},{1,0},{2,3},{3,2},{4,5},{5,4},{6,7},{7,6},{8,9},{9,8},{10,11... | collective-permute-start | bytes 1572872 | tf_op jit(solution)/shard_map/gradient_columns/ppermute | solution.py:276
  48.8 1.2 %all-to-all-done.parts = f32[32,8,128]{2,1,0:T(8,128)S(1)} async-done(((f32[32,8,128]{2,1,0:T(8,128)}), f32[32,8,128]{2,1,0:T(8,128)S(1)}, u32[]{:S(2)}, u32[]{:S(2)}) %all-to-all-start) | async-done | bytes 131104 | tf_op jit(solution)/shard_map/probe_sum_plane/all_to_all | solution.py:280
  50.0 0.7 sum_parts.2
  50.7 18.2 %all-to-all-start.1 = ((f32[24,8,128]{2,1,0:T(8,128)}), f32[24,8,128]{2,1,0:T(8,128)S(1)}, u32[]{:S(2)}, u32[]{:S(2)}) async-start(f32[24,8,128]{2,1,0:T(8,128)} %sum_parts.2), calls=%async_computation.1 | async-start | bytes 196608 | tf_op jit(solution)/shard_map/probe_sum_z/all_to_all | solution.py:280
  68.9 0.0 collective-permute-done.6.col_across
  68.9 0.0 collective-permute-done.7.col_mate
  68.9 0.3 add_vertical.1
  69.3 0.7 collective-permute-start.8
  70.0 3.9 %collective-permute-start.9 = (f32[4,2,64,128]{3,2,1,0:T(8,128)S(1)}, f32[4,2,64,128]{3,2,1,0:T(8,128)S(1)}, u32[]{:S(2)}, u32[]{:S(2)}) collective-permute-start(f32[4,2,64,128]{3,2,1,0:T(8,128)S(1)} %get-tuple-element.30), channel_id=1, source_target_pairs={{0,16},{16,0},{32,48},{48,32},{64,80},{80,64},{96,112},{112,96},{1... | collective-permute-start | bytes 786440 | tf_op jit(solution)/shard_map/gradient_rows/ppermute | solution.py:276
  73.9 6.1 %all-to-all-done.1.parts = f32[24,8,128]{2,1,0:T(8,128)S(1)} async-done(((f32[24,8,128]{2,1,0:T(8,128)}), f32[24,8,128]{2,1,0:T(8,128)S(1)}, u32[]{:S(2)}, u32[]{:S(2)}) %all-to-all-start.1) | async-done | bytes 98336 | tf_op jit(solution)/shard_map/probe_sum_z/all_to_all | solution.py:280
  80.0 0.7 sum_parts.3
  80.7 3.9 %all-to-all-start.2 = ((f32[32,8,128]{2,1,0:T(8,128)}), f32[32,8,128]{2,1,0:T(8,128)S(1)}, u32[]{:S(2)}, u32[]{:S(2)}) async-start(f32[32,8,128]{2,1,0:T(8,128)} %sum_parts.3), calls=%async_computation.2 | async-start | bytes 262144 | tf_op jit(solution)/shard_map/probe_sum_gather/all_to_all | solution.py:280
  84.6 0.0 collective-permute-done.8.row_across
  84.6 0.0 collective-permute-done.9.row_mate
  84.6 1.1 %add_own.1 = f32[4,2,128,128]{3,2,1,0:T(8,128)} custom-call(f32[4,2,128,128]{3,2,1,0:T(8,128)S(1)} %get-tuple-element.23.own, f32[4,2,128,128]{3,2,1,0:T(8,128)S(1)} %collective-permute-done.6.col_across, f32[4,2,128,128]{3,2,1,0:T(8,128)S(1)} %collective-permute-done.7.col_mate, f32[4,2,64,128]{3,2,1,0:T(8,128)S(1)} %collective-permute-done.8.row_across, ...), custom_call_target="tpu_custom_call" | custom-call | bytes 2621440 | tf_op jit(solution)/shard_map/gradient_rows/add_own/pallas_call | solution.py:257
  85.8 8.0 %all-to-all-done.2 = f32[32,8,128]{2,1,0:T(8,128)S(1)} async-done(((f32[32,8,128]{2,1,0:T(8,128)}), f32[32,8,128]{2,1,0:T(8,128)S(1)}, u32[]{:S(2)}, u32[]{:S(2)}) %all-to-all-start.2) | async-done | bytes 131104 | tf_op jit(solution)/shard_map/probe_sum_gather/all_to_all | solution.py:280
  93.8 0.7 copy.10
Async XLA Ops:
  0.6 1.0 %copy-start = (f32[4,2,128,128]{3,2,1,0:T(8,128)S(1)}, f32[4,2,128,128]{3,2,1,0:T(8,128)}, u32[]{:S(2)}) copy-start(f32[4,2,128,128]{3,2,1,0:T(8,128)} %tile.3) | copy-start | bytes 1572868
  1.7 24.1 %copy-start.1 = (f32[4,2,128,128]{3,2,1,0:T(8,128)S(1)}, f32[4,2,128,128]{3,2,1,0:T(8,128)}, u32[]{:S(2)}) copy-start(f32[4,2,128,128]{3,2,1,0:T(8,128)} %tile.3) | copy-start | bytes 1572868
  1.9 15.9 %collective-permute-start = (f32[4,2,64,128]{3,2,1,0:T(8,128)S(1)}, f32[4,2,64,128]{3,2,1,0:T(8,128)S(1)}, u32[]{:S(2)}, u32[]{:S(2)}) collective-permute-start(f32[4,2,64,128]{3,2,1,0:T(8,128)S(1)} %get-tuple-element.17), channel_id=1, source_target_pairs={{16,32},{32,16},{48,64},{64,48},{80,96},{96,80},{112,128},{128,112... | collective-permute-start | bytes 786440 | tf_op jit(solution)/shard_map/object_halo/ppermute | solution.py:276
  2.6 15.2 %collective-permute-start.1 = (f32[4,2,64,128]{3,2,1,0:T(8,128)S(1)}, f32[4,2,64,128]{3,2,1,0:T(8,128)S(1)}, u32[]{:S(2)}, u32[]{:S(2)}) collective-permute-start(f32[4,2,64,128]{3,2,1,0:T(8,128)S(1)} %get-tuple-element.18), channel_id=1, source_target_pairs={{0,16},{16,0},{32,48},{48,32},{64,80},{80,64},{96,112},{112,96},{1... | collective-permute-start | bytes 786440 | tf_op jit(solution)/shard_map/object_halo/ppermute | solution.py:276
  9.0 15.9 %collective-permute-start.2 = (f32[4,2,64,128]{3,2,1,0:T(8,128)S(1)}, f32[4,2,64,128]{3,2,1,0:T(8,128)S(1)}, u32[]{:S(2)}, u32[]{:S(2)}) collective-permute-start(f32[4,2,64,128]{3,2,1,0:T(8,128)S(1)} %get-tuple-element.19), channel_id=1, source_target_pairs={{1,2},{2,1},{3,4},{4,3},{5,6},{6,5},{7,8},{8,7},{9,10},{10,9},{11,... | collective-permute-start | bytes 786440 | tf_op jit(solution)/shard_map/object_halo/ppermute | solution.py:276
  13.3 12.4 %copy-start.2 = (f32[2,128,128]{2,1,0:T(8,128)S(1)}, f32[2,128,128]{2,1,0:T(8,128)}, u32[]{:S(2)}) copy-start(f32[2,128,128]{2,1,0:T(8,128)} %probe.1) | copy-start | bytes 393220
  13.3 12.4 %copy-start.3 = (f32[1,1,2,128,128]{4,3,2,1,0:T(8,128)S(1)}, f32[1,1,2,128,128]{4,3,2,1,0:T(8,128)}, u32[]{:S(2)}) copy-start(f32[1,1,2,128,128]{4,3,2,1,0:T(8,128)} %param.10) | copy-start | bytes 393220
  13.3 12.4 %copy-start.5 = (bf16[8,128,128]{2,1,0:T(8,128)(2,1)S(1)}, bf16[8,128,128]{2,1,0:T(8,128)(2,1)}, u32[]{:S(2)}) copy-start(bf16[8,128,128]{2,1,0:T(8,128)(2,1)} %constant.2.clone.consts) | copy-start | bytes 786436
  13.3 11.5 %collective-permute-start.3 = (f32[4,2,64,128]{3,2,1,0:T(8,128)S(1)}, f32[4,2,64,128]{3,2,1,0:T(8,128)S(1)}, u32[]{:S(2)}, u32[]{:S(2)}) collective-permute-start(f32[4,2,64,128]{3,2,1,0:T(8,128)S(1)} %get-tuple-element.20), channel_id=1, source_target_pairs={{0,1},{1,0},{2,3},{3,2},{4,5},{5,4},{6,7},{7,6},{8,9},{9,8},{10,11... | collective-permute-start | bytes 786440 | tf_op jit(solution)/shard_map/object_halo/ppermute | solution.py:276
  18.0 7.7 %collective-permute-start.4 = (f32[4,2,64,128]{3,2,1,0:T(8,128)S(1)}, f32[4,2,64,128]{3,2,1,0:T(8,128)S(1)}, u32[]{:S(2)}, u32[]{:S(2)}) collective-permute-start(f32[4,2,64,128]{3,2,1,0:T(8,128)S(1)} %get-tuple-element.21), channel_id=1, source_target_pairs={{1,2},{2,1},{3,4},{4,3},{5,6},{6,5},{7,8},{8,7},{9,10},{10,9},{11,... | collective-permute-start | bytes 786440 | tf_op jit(solution)/shard_map/object_halo/ppermute | solution.py:276
  20.0 5.8 %collective-permute-start.5 = (f32[4,2,64,128]{3,2,1,0:T(8,128)S(1)}, f32[4,2,64,128]{3,2,1,0:T(8,128)S(1)}, u32[]{:S(2)}, u32[]{:S(2)}) collective-permute-start(f32[4,2,64,128]{3,2,1,0:T(8,128)S(1)} %get-tuple-element.22), channel_id=1, source_target_pairs={{0,1},{1,0},{2,3},{3,2},{4,5},{5,4},{6,7},{7,6},{8,9},{9,8},{10,11... | collective-permute-start | bytes 786440 | tf_op jit(solution)/shard_map/object_halo/ppermute | solution.py:276
  24.8 0.9 copy-start.4
  32.9 17.2 %all-to-all-start = ((f32[32,8,128]{2,1,0:T(8,128)}), f32[32,8,128]{2,1,0:T(8,128)S(1)}, u32[]{:S(2)}, u32[]{:S(2)}) async-start(f32[32,8,128]{2,1,0:T(8,128)} %bitcast.1), calls=%async_computation | async-start | bytes 262144 | tf_op jit(solution)/shard_map/probe_sum_plane/all_to_all | solution.py:280
  41.2 27.7 %collective-permute-start.6 = (f32[4,2,128,128]{3,2,1,0:T(8,128)S(1)}, f32[4,2,128,128]{3,2,1,0:T(8,128)S(1)}, u32[]{:S(2)}, u32[]{:S(2)}) collective-permute-start(f32[4,2,128,128]{3,2,1,0:T(8,128)S(1)} %get-tuple-element.26), channel_id=1, source_target_pairs={{1,2},{2,1},{3,4},{4,3},{5,6},{6,5},{7,8},{8,7},{9,10},{10,9},{11,... | collective-permute-start | bytes 1572872 | tf_op jit(solution)/shard_map/gradient_columns/ppermute | solution.py:276
  46.9 22.1 %collective-permute-start.7 = (f32[4,2,128,128]{3,2,1,0:T(8,128)S(1)}, f32[4,2,128,128]{3,2,1,0:T(8,128)S(1)}, u32[]{:S(2)}, u32[]{:S(2)}) collective-permute-start(f32[4,2,128,128]{3,2,1,0:T(8,128)S(1)} %get-tuple-element.27), channel_id=1, source_target_pairs={{0,1},{1,0},{2,3},{3,2},{4,5},{5,4},{6,7},{7,6},{8,9},{9,8},{10,11... | collective-permute-start | bytes 1572872 | tf_op jit(solution)/shard_map/gradient_columns/ppermute | solution.py:276
  50.7 29.3 %all-to-all-start.1 = ((f32[24,8,128]{2,1,0:T(8,128)}), f32[24,8,128]{2,1,0:T(8,128)S(1)}, u32[]{:S(2)}, u32[]{:S(2)}) async-start(f32[24,8,128]{2,1,0:T(8,128)} %sum_parts.2), calls=%async_computation.1 | async-start | bytes 196608 | tf_op jit(solution)/shard_map/probe_sum_z/all_to_all | solution.py:280
  69.3 15.3 %collective-permute-start.8 = (f32[4,2,64,128]{3,2,1,0:T(8,128)S(1)}, f32[4,2,64,128]{3,2,1,0:T(8,128)S(1)}, u32[]{:S(2)}, u32[]{:S(2)}) collective-permute-start(f32[4,2,64,128]{3,2,1,0:T(8,128)S(1)} %get-tuple-element.29), channel_id=1, source_target_pairs={{16,32},{32,16},{48,64},{64,48},{80,96},{96,80},{112,128},{128,112... | collective-permute-start | bytes 786440 | tf_op jit(solution)/shard_map/gradient_rows/ppermute | solution.py:276
  70.0 14.7 %collective-permute-start.9 = (f32[4,2,64,128]{3,2,1,0:T(8,128)S(1)}, f32[4,2,64,128]{3,2,1,0:T(8,128)S(1)}, u32[]{:S(2)}, u32[]{:S(2)}) collective-permute-start(f32[4,2,64,128]{3,2,1,0:T(8,128)S(1)} %get-tuple-element.30), channel_id=1, source_target_pairs={{0,16},{16,0},{32,48},{48,32},{64,80},{80,64},{96,112},{112,96},{1... | collective-permute-start | bytes 786440 | tf_op jit(solution)/shard_map/gradient_rows/ppermute | solution.py:276
  80.7 13.1 %all-to-all-start.2 = ((f32[32,8,128]{2,1,0:T(8,128)}), f32[32,8,128]{2,1,0:T(8,128)S(1)}, u32[]{:S(2)}, u32[]{:S(2)}) async-start(f32[32,8,128]{2,1,0:T(8,128)} %sum_parts.3), calls=%async_computation.2 | async-start | bytes 262144 | tf_op jit(solution)/shard_map/probe_sum_gather/all_to_all | solution.py:280

commit v6 on v5

--- a/solution.py
+++ b/solution.py
@@ -82,13 +82,22 @@
     return jnp.where(is_even, before, after), jnp.where(is_even, after, before)
 
 
-def edges_kernel(tile, row_across, row_mate, col_across, col_mate):
-    row_even, col_even = even("x"), even("c")
+def rows_kernel(tile, row_across, row_mate, arrived):
+    odd = jnp.bitwise_and(lax.axis_index("x"), 1)
+    copies = []
+    for i, (half, out) in enumerate(((odd, row_across), (1 - odd, row_mate))):
+        rows = pl.ds(pl.multiple_of(half * H, H), H)
+        copies.append(pltpu.make_async_copy(tile.at[:, :, rows, :], out, arrived.at[i]))
+        copies[-1].start()
+    for copy in copies:
+        copy.wait()
+
+
+def columns_kernel(tile, col_across, col_mate):
+    col_even = even("c")
     for k in range(tile.shape[0]):
         for c in range(2):
-            t = tile[k, c]
-            row_across[k, c], row_mate[k, c] = sort(row_even, t[:H], t[H:])
-            col_across[k, c], col_mate[k, c] = sort(col_even, *pack_columns(t))
+            col_across[k, c], col_mate[k, c] = sort(col_even, *pack_columns(tile[k, c]))
 
 
 def corners_kernel(row_across, row_mate, col_across, col_mate):
@@ -251,13 +260,13 @@
             out[k, c] = turned_rows(pltpu.roll(own[k, c], H, 1)) + add + v
 
 
-def call(kernel, outs, args, name, scalars=0, scratch=(), vmem=4, flops=0):
+def call(kernel, outs, args, name, scalars=0, where=None, scratch=(), vmem=4, flops=0):
     spec = pl.BlockSpec(memory_space=pltpu.VMEM)
     smem = pl.BlockSpec(memory_space=pltpu.SMEM)
     return pl.pallas_call(
         kernel,
         out_shape=[jax.ShapeDtypeStruct(s, jnp.float32) for s in outs],
-        in_specs=[smem] * scalars + [spec] * (len(args) - scalars),
+        in_specs=[smem] * scalars + [where or spec] * (len(args) - scalars),
         out_specs=[spec] * len(outs),
         scratch_shapes=list(scratch),
         compiler_params=pltpu.CompilerParams(vmem_limit_bytes=vmem * 1024 * 1024),
@@ -301,9 +310,12 @@
     half = (slices, 2, H, N)
     consts = jnp.asarray(constant_operands())
     with jax.named_scope("object_halo"):
-        edges = call(edges_kernel, [half] * 4, (object_field,), "pack_edges")
-        rows = swap(*edges[:2], ROW)
-        cols = swap(*edges[2:], COL)
+        rows = call(
+            rows_kernel, [half] * 2, (pltpu.with_memory_space_constraint(object_field, pltpu.HBM),), "pick_rows",
+            where=pl.BlockSpec(memory_space=pltpu.HBM), scratch=[pltpu.SemaphoreType.DMA((2,))],
+        )
+        rows = swap(*rows, ROW)
+        cols = swap(*call(columns_kernel, [half] * 2, (object_field,), "pack_columns"), COL)
         corners = swap(*call(corners_kernel, [half] * 2, rows, "pack_corners"), COL)
     own, vert, horiz, corner, probe_sum = call(
         grad_kernel,

time: 95.4 us -> 95.2 us (level)
  Pallas kernels: 10.7 us -> 11.8 us
  local copies, waits for them, and re-layouts: 1.72 us -> 0.69 us
    pallas_call x8 -> x9, Pallas kernels: 10.7 us -> 11.8 us  [call(): pl.pallas_call(kernel, out_shape=[jax.ShapeDtypeStruct(s, jnp.float32) fo...]
    unnamed x13 -> x11, local copies, waits for them, and re-layouts: 1.72 us -> 0.69 us
where the time goes in v6:
time: 95.2 us; the launch traced here: 94.3 us
  starting transfers between devices  63.6 us (67%)
  waiting for transfers between devices  16.6 us (17%)
  Pallas kernels  11.8 us (12%)
  between operations  1.55 us (2%)
    all_to_all x3, starting transfers between devices, exchange(): return lax.all_to_all(x, axis, 0, 0, tiled=True)  29.9 us
    ppermute x5, starting transfers between devices, swap(): lax.ppermute(mate, axis, [(i, i ^ 1) for i in range(size)])  20.6 us
    all_to_all x3, waiting for transfers between devices, exchange(): return lax.all_to_all(x, axis, 0, 0, tiled=True)  15.5 us
    ppermute x5, starting transfers between devices, swap(): lax.ppermute(across, axis, over)  13 us
    pallas_call x9, Pallas kernels, call(): pl.pallas_call(kernel, out_shape=[jax.ShapeDtypeStruct(s, jnp.float32) fo...  11.8 us
  transfers between devices with their start and end apart: 13, of which 4 were waited for; matrix products, arithmetic and copies ran while one was open for 0% of the time, Pallas kernels for 4%

profile of v6, /device:TPU:1, one launch (start us, length us, event | category | flops | bytes accessed | tf_op | source)
XLA Modules:
  0.0 94.3 jit_solution(17246955081462689680)
XLA Ops:
  0.6 0.0 copy-start
  0.6 1.1 %pick_rows.1 = (f32[4,2,64,128]{3,2,1,0:T(8,128)S(1)}, f32[4,2,64,128]{3,2,1,0:T(8,128)S(1)}) custom-call(f32[4,2,128,128]{3,2,1,0:T(8,128)} %tile.5), custom_call_target="tpu_custom_call" | custom-call | bytes 1048576 | tf_op jit(solution)/shard_map/object_halo/pick_rows/pallas_call | solution.py:266
  1.8 0.7 collective-permute-start
  2.4 6.4 %collective-permute-start.1 = (f32[4,2,64,128]{3,2,1,0:T(8,128)S(1)}, f32[4,2,64,128]{3,2,1,0:T(8,128)S(1)}, u32[]{:S(2)}, u32[]{:S(2)}) collective-permute-start(f32[4,2,64,128]{3,2,1,0:T(8,128)S(1)} %get-tuple-element.18), channel_id=1, source_target_pairs={{0,16},{16,0},{32,48},{48,32},{64,80},{80,64},{96,112},{112,96},{1... | collective-permute-start | bytes 786440 | tf_op jit(solution)/shard_map/object_halo/ppermute | solution.py:285
  8.8 0.0 copy-done
  8.9 0.2 pack_columns.1
  9.1 4.3 %collective-permute-start.2 = (f32[4,2,64,128]{3,2,1,0:T(8,128)S(1)}, f32[4,2,64,128]{3,2,1,0:T(8,128)S(1)}, u32[]{:S(2)}, u32[]{:S(2)}) collective-permute-start(f32[4,2,64,128]{3,2,1,0:T(8,128)S(1)} %get-tuple-element.19), channel_id=1, source_target_pairs={{1,2},{2,1},{3,4},{4,3},{5,6},{6,5},{7,8},{8,7},{9,10},{10,9},{11,... | collective-permute-start | bytes 786440 | tf_op jit(solution)/shard_map/object_halo/ppermute | solution.py:285
  13.4 0.0 copy-start.1
  13.4 0.0 copy-start.2
  13.4 0.0 copy-start.4
  13.4 4.4 %collective-permute-start.3 = (f32[4,2,64,128]{3,2,1,0:T(8,128)S(1)}, f32[4,2,64,128]{3,2,1,0:T(8,128)S(1)}, u32[]{:S(2)}, u32[]{:S(2)}) collective-permute-start(f32[4,2,64,128]{3,2,1,0:T(8,128)S(1)} %get-tuple-element.20), channel_id=1, source_target_pairs={{0,1},{1,0},{2,3},{3,2},{4,5},{5,4},{6,7},{7,6},{8,9},{9,8},{10,11... | collective-permute-start | bytes 786440 | tf_op jit(solution)/shard_map/object_halo/ppermute | solution.py:285
  17.9 0.0 collective-permute-done.row_across
  17.9 0.0 collective-permute-done.1.row_mate
  17.9 0.2 pack_corners.1
  18.1 1.9 %collective-permute-start.4 = (f32[4,2,64,128]{3,2,1,0:T(8,128)S(1)}, f32[4,2,64,128]{3,2,1,0:T(8,128)S(1)}, u32[]{:S(2)}, u32[]{:S(2)}) collective-permute-start(f32[4,2,64,128]{3,2,1,0:T(8,128)S(1)} %get-tuple-element.21), channel_id=1, source_target_pairs={{1,2},{2,1},{3,4},{4,3},{5,6},{6,5},{7,8},{8,7},{9,10},{10,9},{11,... | collective-permute-start | bytes 786440 | tf_op jit(solution)/shard_map/object_halo/ppermute | solution.py:285
  20.0 4.0 %collective-permute-start.5 = (f32[4,2,64,128]{3,2,1,0:T(8,128)S(1)}, f32[4,2,64,128]{3,2,1,0:T(8,128)S(1)}, u32[]{:S(2)}, u32[]{:S(2)}) collective-permute-start(f32[4,2,64,128]{3,2,1,0:T(8,128)S(1)} %get-tuple-element.22), channel_id=1, source_target_pairs={{0,1},{1,0},{2,3},{3,2},{4,5},{5,4},{6,7},{7,6},{8,9},{9,8},{10,11... | collective-permute-start | bytes 786440 | tf_op jit(solution)/shard_map/object_halo/ppermute | solution.py:285
  24.7 0.0 copy-start.3
  24.7 0.0 collective-permute-done.2.col_across
  24.7 0.0 collective-permute-done.3.col_mate
  24.7 1.1 %collective-permute-done.4.corner_across = f32[4,2,64,128]{3,2,1,0:T(8,128)S(1)} collective-permute-done((f32[4,2,64,128]{3,2,1,0:T(8,128)S(1)}, f32[4,2,64,128]{3,2,1,0:T(8,128)S(1)}, u32[]{:S(2)}, u32[]{:S(2)}) %collective-permute-start.4) | collective-permute-done | bytes 262176 | tf_op jit(solution)/shard_map/object_halo/ppermute | solution.py:285
  25.8 0.0 collective-permute-done.5.corner_mate
  25.8 0.0 copy-done.1
  25.8 0.0 copy-done.2
  25.8 0.0 copy-done.4
  25.8 0.0 copy-done.3
  25.8 7.1 %slot_gradients.1 = (f32[4,2,128,128]{3,2,1,0:T(8,128)S(1)}, f32[4,2,128,128]{3,2,1,0:T(8,128)S(1)}, f32[4,2,128,128]{3,2,1,0:T(8,128)S(1)}, f32[4,2,128,128]{3,2,1,0:T(8,128)S(1)}, f32[2,128,128]{2,1,0:T(8,128)}) custom-call(s32[1,1,2,2]{3,2,1,0:T(2,128)S(1)} %copy-done.3, s32[1,1]{1,0:T(1,128)S(6)} %copy.9.count, f32[4,2,128,128]{3,2,1,0:T(8,128)S(1)} %copy-done, ...), custom_call_target="tpu_custom_call" | custom-call | flops 1610612736 | bytes 4849684 | tf_op jit(solution)/shard_map/slot_gradients/pallas_call | solution.py:266
  33.0 8.0 %all-to-all-start = ((f32[32,8,128]{2,1,0:T(8,128)}), f32[32,8,128]{2,1,0:T(8,128)S(1)}, u32[]{:S(2)}, u32[]{:S(2)}) async-start(f32[32,8,128]{2,1,0:T(8,128)} %bitcast.1), calls=%async_computation | async-start | bytes 262144 | tf_op jit(solution)/shard_map/probe_sum_plane/all_to_all | solution.py:289
  40.9 0.3 pack_sides.1
  41.3 5.4 %collective-permute-start.6 = (f32[4,2,128,128]{3,2,1,0:T(8,128)S(1)}, f32[4,2,128,128]{3,2,1,0:T(8,128)S(1)}, u32[]{:S(2)}, u32[]{:S(2)}) collective-permute-start(f32[4,2,128,128]{3,2,1,0:T(8,128)S(1)} %get-tuple-element.26), channel_id=1, source_target_pairs={{1,2},{2,1},{3,4},{4,3},{5,6},{6,5},{7,8},{8,7},{9,10},{10,9},{11,... | collective-permute-start | bytes 1572872 | tf_op jit(solution)/shard_map/gradient_columns/ppermute | solution.py:285
  46.7 1.9 %collective-permute-start.7 = (f32[4,2,128,128]{3,2,1,0:T(8,128)S(1)}, f32[4,2,128,128]{3,2,1,0:T(8,128)S(1)}, u32[]{:S(2)}, u32[]{:S(2)}) collective-permute-start(f32[4,2,128,128]{3,2,1,0:T(8,128)S(1)} %get-tuple-element.27), channel_id=1, source_target_pairs={{0,1},{1,0},{2,3},{3,2},{4,5},{5,4},{6,7},{7,6},{8,9},{9,8},{10,11... | collective-permute-start | bytes 1572872 | tf_op jit(solution)/shard_map/gradient_columns/ppermute | solution.py:285
  48.7 1.4 %all-to-all-done.parts = f32[32,8,128]{2,1,0:T(8,128)S(1)} async-done(((f32[32,8,128]{2,1,0:T(8,128)}), f32[32,8,128]{2,1,0:T(8,128)S(1)}, u32[]{:S(2)}, u32[]{:S(2)}) %all-to-all-start) | async-done | bytes 131104 | tf_op jit(solution)/shard_map/probe_sum_plane/all_to_all | solution.py:289
  50.1 0.7 sum_parts.2
  50.8 18.0 %all-to-all-start.1 = ((f32[24,8,128]{2,1,0:T(8,128)}), f32[24,8,128]{2,1,0:T(8,128)S(1)}, u32[]{:S(2)}, u32[]{:S(2)}) async-start(f32[24,8,128]{2,1,0:T(8,128)} %sum_parts.2), calls=%async_computation.1 | async-start | bytes 196608 | tf_op jit(solution)/shard_map/probe_sum_z/all_to_all | solution.py:289
  68.8 0.0 collective-permute-done.6.col_across
  68.8 0.0 collective-permute-done.7.col_mate
  68.8 0.3 add_vertical.1
  69.2 0.7 collective-permute-start.8
  69.8 3.9 %collective-permute-start.9 = (f32[4,2,64,128]{3,2,1,0:T(8,128)S(1)}, f32[4,2,64,128]{3,2,1,0:T(8,128)S(1)}, u32[]{:S(2)}, u32[]{:S(2)}) collective-permute-start(f32[4,2,64,128]{3,2,1,0:T(8,128)S(1)} %get-tuple-element.30), channel_id=1, source_target_pairs={{0,16},{16,0},{32,48},{48,32},{64,80},{80,64},{96,112},{112,96},{1... | collective-permute-start | bytes 786440 | tf_op jit(solution)/shard_map/gradient_rows/ppermute | solution.py:285
  73.7 6.1 %all-to-all-done.1.parts = f32[24,8,128]{2,1,0:T(8,128)S(1)} async-done(((f32[24,8,128]{2,1,0:T(8,128)}), f32[24,8,128]{2,1,0:T(8,128)S(1)}, u32[]{:S(2)}, u32[]{:S(2)}) %all-to-all-start.1) | async-done | bytes 98336 | tf_op jit(solution)/shard_map/probe_sum_z/all_to_all | solution.py:289
  79.8 0.7 sum_parts.3
  80.5 4.0 %all-to-all-start.2 = ((f32[32,8,128]{2,1,0:T(8,128)}), f32[32,8,128]{2,1,0:T(8,128)S(1)}, u32[]{:S(2)}, u32[]{:S(2)}) async-start(f32[32,8,128]{2,1,0:T(8,128)} %sum_parts.3), calls=%async_computation.2 | async-start | bytes 262144 | tf_op jit(solution)/shard_map/probe_sum_gather/all_to_all | solution.py:289
  84.5 0.0 collective-permute-done.8.row_across
  84.5 0.0 collective-permute-done.9.row_mate
  84.5 1.1 %add_own.1 = f32[4,2,128,128]{3,2,1,0:T(8,128)} custom-call(f32[4,2,128,128]{3,2,1,0:T(8,128)S(1)} %get-tuple-element.23.own, f32[4,2,128,128]{3,2,1,0:T(8,128)S(1)} %collective-permute-done.6.col_across, f32[4,2,128,128]{3,2,1,0:T(8,128)S(1)} %collective-permute-done.7.col_mate, f32[4,2,64,128]{3,2,1,0:T(8,128)S(1)} %collective-permute-done.8.row_across, ...), custom_call_target="tpu_custom_call" | custom-call | bytes 2621440 | tf_op jit(solution)/shard_map/gradient_rows/add_own/pallas_call | solution.py:266
  85.6 8.0 %all-to-all-done.2 = f32[32,8,128]{2,1,0:T(8,128)S(1)} async-done(((f32[32,8,128]{2,1,0:T(8,128)}), f32[32,8,128]{2,1,0:T(8,128)S(1)}, u32[]{:S(2)}, u32[]{:S(2)}) %all-to-all-start.2) | async-done | bytes 131104 | tf_op jit(solution)/shard_map/probe_sum_gather/all_to_all | solution.py:289
  93.6 0.7 copy.10
Async XLA Ops:
  0.6 8.2 %copy-start = (f32[4,2,128,128]{3,2,1,0:T(8,128)S(1)}, f32[4,2,128,128]{3,2,1,0:T(8,128)}, u32[]{:S(2)}) copy-start(f32[4,2,128,128]{3,2,1,0:T(8,128)} %tile.5) | copy-start | bytes 1572868
  1.8 16.1 %collective-permute-start = (f32[4,2,64,128]{3,2,1,0:T(8,128)S(1)}, f32[4,2,64,128]{3,2,1,0:T(8,128)S(1)}, u32[]{:S(2)}, u32[]{:S(2)}) collective-permute-start(f32[4,2,64,128]{3,2,1,0:T(8,128)S(1)} %get-tuple-element.17), channel_id=1, source_target_pairs={{16,32},{32,16},{48,64},{64,48},{80,96},{96,80},{112,128},{128,112... | collective-permute-start | bytes 786440 | tf_op jit(solution)/shard_map/object_halo/ppermute | solution.py:285
  2.4 15.4 %collective-permute-start.1 = (f32[4,2,64,128]{3,2,1,0:T(8,128)S(1)}, f32[4,2,64,128]{3,2,1,0:T(8,128)S(1)}, u32[]{:S(2)}, u32[]{:S(2)}) collective-permute-start(f32[4,2,64,128]{3,2,1,0:T(8,128)S(1)} %get-tuple-element.18), channel_id=1, source_target_pairs={{0,16},{16,0},{32,48},{48,32},{64,80},{80,64},{96,112},{112,96},{1... | collective-permute-start | bytes 786440 | tf_op jit(solution)/shard_map/object_halo/ppermute | solution.py:285
  9.1 15.6 %collective-permute-start.2 = (f32[4,2,64,128]{3,2,1,0:T(8,128)S(1)}, f32[4,2,64,128]{3,2,1,0:T(8,128)S(1)}, u32[]{:S(2)}, u32[]{:S(2)}) collective-permute-start(f32[4,2,64,128]{3,2,1,0:T(8,128)S(1)} %get-tuple-element.19), channel_id=1, source_target_pairs={{1,2},{2,1},{3,4},{4,3},{5,6},{6,5},{7,8},{8,7},{9,10},{10,9},{11,... | collective-permute-start | bytes 786440 | tf_op jit(solution)/shard_map/object_halo/ppermute | solution.py:285
  13.4 12.4 %copy-start.1 = (f32[2,128,128]{2,1,0:T(8,128)S(1)}, f32[2,128,128]{2,1,0:T(8,128)}, u32[]{:S(2)}) copy-start(f32[2,128,128]{2,1,0:T(8,128)} %probe.1) | copy-start | bytes 393220
  13.4 12.4 %copy-start.2 = (f32[1,1,2,128,128]{4,3,2,1,0:T(8,128)S(1)}, f32[1,1,2,128,128]{4,3,2,1,0:T(8,128)}, u32[]{:S(2)}) copy-start(f32[1,1,2,128,128]{4,3,2,1,0:T(8,128)} %param.10) | copy-start | bytes 393220
  13.4 12.4 %copy-start.4 = (bf16[8,128,128]{2,1,0:T(8,128)(2,1)S(1)}, bf16[8,128,128]{2,1,0:T(8,128)(2,1)}, u32[]{:S(2)}) copy-start(bf16[8,128,128]{2,1,0:T(8,128)(2,1)} %constant.2.clone.consts) | copy-start | bytes 786436
  13.4 11.3 %collective-permute-start.3 = (f32[4,2,64,128]{3,2,1,0:T(8,128)S(1)}, f32[4,2,64,128]{3,2,1,0:T(8,128)S(1)}, u32[]{:S(2)}, u32[]{:S(2)}) collective-permute-start(f32[4,2,64,128]{3,2,1,0:T(8,128)S(1)} %get-tuple-element.20), channel_id=1, source_target_pairs={{0,1},{1,0},{2,3},{3,2},{4,5},{5,4},{6,7},{7,6},{8,9},{9,8},{10,11... | collective-permute-start | bytes 786440 | tf_op jit(solution)/shard_map/object_halo/ppermute | solution.py:285
  18.1 7.7 %collective-permute-start.4 = (f32[4,2,64,128]{3,2,1,0:T(8,128)S(1)}, f32[4,2,64,128]{3,2,1,0:T(8,128)S(1)}, u32[]{:S(2)}, u32[]{:S(2)}) collective-permute-start(f32[4,2,64,128]{3,2,1,0:T(8,128)S(1)} %get-tuple-element.21), channel_id=1, source_target_pairs={{1,2},{2,1},{3,4},{4,3},{5,6},{6,5},{7,8},{8,7},{9,10},{10,9},{11,... | collective-permute-start | bytes 786440 | tf_op jit(solution)/shard_map/object_halo/ppermute | solution.py:285
  20.0 5.8 %collective-permute-start.5 = (f32[4,2,64,128]{3,2,1,0:T(8,128)S(1)}, f32[4,2,64,128]{3,2,1,0:T(8,128)S(1)}, u32[]{:S(2)}, u32[]{:S(2)}) collective-permute-start(f32[4,2,64,128]{3,2,1,0:T(8,128)S(1)} %get-tuple-element.22), channel_id=1, source_target_pairs={{0,1},{1,0},{2,3},{3,2},{4,5},{5,4},{6,7},{7,6},{8,9},{9,8},{10,11... | collective-permute-start | bytes 786440 | tf_op jit(solution)/shard_map/object_halo/ppermute | solution.py:285
  24.7 1.1 %copy-start.3 = (s32[1,1,2,2]{3,2,1,0:T(2,128)S(1)}, s32[1,1,2,2]{3,2,1,0:T(2,128)}, u32[]{:S(2)}) copy-start(s32[1,1,2,2]{3,2,1,0:T(2,128)} %pos.1) | copy-start | bytes 52
  33.0 17.1 %all-to-all-start = ((f32[32,8,128]{2,1,0:T(8,128)}), f32[32,8,128]{2,1,0:T(8,128)S(1)}, u32[]{:S(2)}, u32[]{:S(2)}) async-start(f32[32,8,128]{2,1,0:T(8,128)} %bitcast.1), calls=%async_computation | async-start | bytes 262144 | tf_op jit(solution)/shard_map/probe_sum_plane/all_to_all | solution.py:289
  41.3 27.5 %collective-permute-start.6 = (f32[4,2,128,128]{3,2,1,0:T(8,128)S(1)}, f32[4,2,128,128]{3,2,1,0:T(8,128)S(1)}, u32[]{:S(2)}, u32[]{:S(2)}) collective-permute-start(f32[4,2,128,128]{3,2,1,0:T(8,128)S(1)} %get-tuple-element.26), channel_id=1, source_target_pairs={{1,2},{2,1},{3,4},{4,3},{5,6},{6,5},{7,8},{8,7},{9,10},{10,9},{11,... | collective-permute-start | bytes 1572872 | tf_op jit(solution)/shard_map/gradient_columns/ppermute | solution.py:285
  46.7 22.1 %collective-permute-start.7 = (f32[4,2,128,128]{3,2,1,0:T(8,128)S(1)}, f32[4,2,128,128]{3,2,1,0:T(8,128)S(1)}, u32[]{:S(2)}, u32[]{:S(2)}) collective-permute-start(f32[4,2,128,128]{3,2,1,0:T(8,128)S(1)} %get-tuple-element.27), channel_id=1, source_target_pairs={{0,1},{1,0},{2,3},{3,2},{4,5},{5,4},{6,7},{7,6},{8,9},{9,8},{10,11... | collective-permute-start | bytes 1572872 | tf_op jit(solution)/shard_map/gradient_columns/ppermute | solution.py:285
  50.8 29.1 %all-to-all-start.1 = ((f32[24,8,128]{2,1,0:T(8,128)}), f32[24,8,128]{2,1,0:T(8,128)S(1)}, u32[]{:S(2)}, u32[]{:S(2)}) async-start(f32[24,8,128]{2,1,0:T(8,128)} %sum_parts.2), calls=%async_computation.1 | async-start | bytes 196608 | tf_op jit(solution)/shard_map/probe_sum_z/all_to_all | solution.py:289
  69.2 15.3 %collective-permute-start.8 = (f32[4,2,64,128]{3,2,1,0:T(8,128)S(1)}, f32[4,2,64,128]{3,2,1,0:T(8,128)S(1)}, u32[]{:S(2)}, u32[]{:S(2)}) collective-permute-start(f32[4,2,64,128]{3,2,1,0:T(8,128)S(1)} %get-tuple-element.29), channel_id=1, source_target_pairs={{16,32},{32,16},{48,64},{64,48},{80,96},{96,80},{112,128},{128,112... | collective-permute-start | bytes 786440 | tf_op jit(solution)/shard_map/gradient_rows/ppermute | solution.py:285
  69.8 14.7 %collective-permute-start.9 = (f32[4,2,64,128]{3,2,1,0:T(8,128)S(1)}, f32[4,2,64,128]{3,2,1,0:T(8,128)S(1)}, u32[]{:S(2)}, u32[]{:S(2)}) collective-permute-start(f32[4,2,64,128]{3,2,1,0:T(8,128)S(1)} %get-tuple-element.30), channel_id=1, source_target_pairs={{0,16},{16,0},{32,48},{48,32},{64,80},{80,64},{96,112},{112,96},{1... | collective-permute-start | bytes 786440 | tf_op jit(solution)/shard_map/gradient_rows/ppermute | solution.py:285
  80.5 13.1 %all-to-all-start.2 = ((f32[32,8,128]{2,1,0:T(8,128)}), f32[32,8,128]{2,1,0:T(8,128)S(1)}, u32[]{:S(2)}, u32[]{:S(2)}) async-start(f32[32,8,128]{2,1,0:T(8,128)} %sum_parts.3), calls=%async_computation.2 | async-start | bytes 262144 | tf_op jit(solution)/shard_map/probe_sum_gather/all_to_all | solution.py:289
